TPU v7x, 32 devices: a whole 2x2x4 slice. The times are simulated.
32 devices in a mesh: grp: 2 (over x), row: 16 (over z, y, core).
Axes of the slice: x: 2, y: 2, z: 4, core: 2. Of those that a mesh axis runs over, the one named last changes fastest.
Arguments:
- fields: bfloat16 [128, 128, 1024], P(('grp', 'row')), parts along dimension 0, may hold values from -6 to 6
- kernel: bfloat16 [7, 7, 2048], P(None, None, 'grp'), parts along dimension 2, may hold values from -0.875 to 0.875
- norm_gain: float32 [2048], P('grp'), parts along dimension 0, may hold values from 0.4 to 1.6
- proj_in: bfloat16 [2048, 4096], P(('grp', 'row')), parts along dimension 0, may hold values from -0.1875 to 0.1875
- proj_out: bfloat16 [8192, 1024], P('grp', 'row'), parts along dimension 0, may hold values from -0.09375 to 0.09375
- cotangent: bfloat16 [128, 128, 1024], P(('grp', 'row')), parts along dimension 0, may hold values from -6 to 6
Outputs:
- result: bfloat16 [128, 128, 1024], P(('grp', 'row')), parts along dimension 0
- fields_grad: bfloat16 [128, 128, 1024], P(('grp', 'row')), parts along dimension 0
- proj_in_grad: bfloat16 [2048, 4096], P(('grp', 'row')), parts along dimension 0
- proj_out_grad: bfloat16 [8192, 1024], P('grp', 'row'), parts along dimension 0
- kernel_grad: float32 [7, 7, 2048], P(None, None, 'grp'), parts along dimension 2
- gain_grad: float32 [2048], P('grp'), parts along dimension 0
There are 2 independent parts, one for each index of `grp`. A program takes and returns all parts, laid end to end along the dimension named above; each array names one. Nothing has to cross between parts.
All inputs are finite; a program needn't handle non-finite values.
Results may differ from a plain program's by a relative error of at most 0.017.
Values may be sent and summed in bfloat16 or wider, within the bound.
No kernel may reach another device: no remote copies, remote signals or barrier semaphores. Data moves between devices by JAX's collectives and lax.ppermute only.
A program may use at most 128 MiB of HBM per device.

v0:
```python
import math

import jax
import jax.numpy as jnp
from jax import lax
from jax.sharding import PartitionSpec as P


def extended(value, sides, width):
    for axis, dim in sides:
        size, length = (lax.axis_size(axis), value.shape[dim])
        up = [(i, (i + 1) % size) for i in range(size - 1)]
        down = [(j, i) for i, j in up]
        last = lax.slice_in_dim(value, length - width, length, axis=dim)
        first = lax.slice_in_dim(value, 0, width, axis=dim)
        before = lax.ppermute(last, axis, up)
        after = lax.ppermute(first, axis, down)
        value = jnp.concatenate([before, value, after], axis=dim)
    return value


def wrap_lon(values):
    return jnp.concatenate([values[:, -3:], values, values[:, :3]], axis=1)


def depthwise(padded, kernel):
    outcome = lax.conv_general_dilated(
        padded[None],
        kernel[:, :, None, :],
        (1, 1),
        "VALID",
        dimension_numbers=("NHWC", "HWIO", "NHWC"),
        feature_group_count=kernel.shape[2],
        preferred_element_type=jnp.float32,
    )
    return outcome[0]


def kernel_sums(conv_grad, padded):
    lat_rows = conv_grad.shape[0]
    lon_cells = conv_grad.shape[1]
    grad_wide = conv_grad.astype(jnp.float32)
    stacked = []
    for lat_off in range(7):
        line = []
        for lon_off in range(7):
            window = padded[lat_off : lat_off + lat_rows, lon_off : lon_off + lon_cells].astype(
                jnp.float32
            )
            line.append(jnp.sum(grad_wide * window, axis=(0, 1)))
        stacked.append(jnp.stack(line))
    return jnp.stack(stacked)


def on_device(fields, kernel, norm_gain, proj_in, proj_out, cotangent):
    lat_rows, lon_cells, channels = fields.shape
    row_devs = lax.axis_size("row")
    grad_scale = 1.0 / math.sqrt(lat_rows * row_devs * lon_cells)
    full_in, full_out = (
        lax.all_gather(proj_in, "row", axis=0, tiled=True),
        lax.all_gather(proj_out, "row", axis=1, tiled=True),
    )
    rimmed = extended(fields, (("row", 0),), 3)
    padded = wrap_lon(rimmed)
    conv_out = depthwise(padded, kernel)
    row_mean = jnp.mean(conv_out, axis=-1, keepdims=True)
    centred = conv_out - row_mean
    inv_std = lax.rsqrt(jnp.mean(centred * centred, axis=-1, keepdims=True) + 1e-06)
    whitened = centred * inv_std
    normed = (whitened * norm_gain).astype(jnp.bfloat16)
    flat_norm = normed.reshape(-1, channels)
    out_grad = cotangent.reshape(-1, channels)
    pre_act = jnp.dot(flat_norm, full_in, preferred_element_type=jnp.float32)
    gauss_area = 0.5 * (1.0 + jax.scipy.special.erf(pre_act / math.sqrt(2.0)))
    gauss_dens = jnp.exp(-0.5 * pre_act * pre_act) / math.sqrt(2.0 * math.pi)
    hidden = (pre_act * gauss_area).astype(jnp.bfloat16)
    branch = jnp.dot(hidden, full_out, preferred_element_type=jnp.float32)
    result = (fields.astype(jnp.float32) + branch.reshape(fields.shape)).astype(jnp.bfloat16)
    picked = out_grad
    down_share = lax.psum_scatter(
        (jnp.dot(picked.T, hidden, preferred_element_type=jnp.float32) * grad_scale).astype(
            jnp.bfloat16
        ),
        "row",
        scatter_dimension=0,
        tiled=True,
    ).astype(jnp.float32)
    proj_out_grad = down_share.T.astype(jnp.bfloat16)
    hidden_grad = jnp.dot(out_grad, full_out.T, preferred_element_type=jnp.float32)
    pre_grad = (hidden_grad * (gauss_area + pre_act * gauss_dens)).astype(jnp.bfloat16)
    picked = flat_norm
    proj_in_grad = lax.psum_scatter(
        (jnp.dot(picked.T, pre_grad, preferred_element_type=jnp.float32) * grad_scale).astype(
            jnp.bfloat16
        ),
        "row",
        scatter_dimension=0,
        tiled=True,
    )
    norm_flat = jnp.dot(pre_grad, full_in.T, preferred_element_type=jnp.float32)
    norm_grad = norm_flat.reshape(fields.shape)
    gain_local = jnp.sum(norm_grad * whitened, axis=(0, 1)) * grad_scale
    white_grad = norm_grad * norm_gain
    conv_grad = inv_std * (
        white_grad
        - jnp.mean(white_grad, axis=-1, keepdims=True)
        - whitened * jnp.mean(white_grad * whitened, axis=-1, keepdims=True)
    )
    conv_grad = conv_grad.astype(jnp.bfloat16)
    grad_rimmed = extended(conv_grad, (("row", 0),), 3)
    back_conv = depthwise(wrap_lon(grad_rimmed), kernel[::-1, ::-1])
    kernel_local = kernel_sums(conv_grad, padded) * grad_scale
    kernel_grad, gain_grad = (
        lax.psum(kernel_local.astype(jnp.bfloat16), "row").astype(jnp.float32),
        lax.psum(gain_local.astype(jnp.bfloat16), "row").astype(jnp.float32),
    )
    fields_grad = (cotangent.astype(jnp.float32) + back_conv).astype(jnp.bfloat16)
    return (result, fields_grad, proj_in_grad, proj_out_grad, kernel_grad, gain_grad)


def solution(mesh):
    in_specs = (
        P(("grp", "row"), None, None),
        P(None, None, "grp"),
        P("grp"),
        P(("grp", "row"), None),
        P("grp", "row"),
        P(("grp", "row"), None, None),
    )
    out_specs = (
        P(("grp", "row"), None, None),
        P(("grp", "row"), None, None),
        P(("grp", "row"), None),
        P("grp", "row"),
        P(None, None, "grp"),
        P("grp"),
    )
    return jax.shard_map(
        on_device, mesh=mesh, in_specs=in_specs, out_specs=out_specs, check_vma=False
    )
```

profile of v0, /device:TPU:0, one launch (start us, length us, event | category | flops | bytes accessed | tf_op | source)
XLA Modules:
  0.0 570.5 jit_solution(11965039655250825067)
XLA Ops:
  8.7 1.5 fusion.105
  11.5 3.1 collective-permute-start
  18.1 3.0 maximum_bitcast_fusion
  22.3 1.5 copy.104
  24.1 9.7 %fusion.88 = f32[4,8,17,1024]{3,1,2,0:T(8,128)S(1)} fusion(bf16[10,1,7,6,1024]{4,2,3,0,1:T(8,128)(2,1)S(1)} %slice.276, bf16[10,1,8,17,1024]{4,2,3,0,1:T(8,128)(2,1)S(1)} %copy.104, pred[8,17]{0,1:T(8,128)(4,1)S(1)} %copy-done.37, bf16[7,7,1,1024]{3,1,0,2:T(8,128)(2,1)S(1)} %bitcast.144), kind=kOutput, calls=%fused_computation.164 | convolution fusion | flops 66453504 | bytes 5974152 | tf_op jit(solution)/shard_map/conv_general_dilated | solution.py:27
  35.3 1.8 slice_reduce_fusion
  39.5 2.8 copy.107
  44.9 10.1 %pad_maximum_fusion.4 = (bf16[10,131,1024]{2,0,1:T(8,128)(2,1)}, bf16[10,131,1024]{2,0,1:T(8,128)(2,1)}) fusion(bf16[10,3,1024]{2,0,1:T(8,128)(2,1)S(1)} %get-tuple-element.101, bf16[3,128,1024]{2,0,1:T(4,128)(2,1)S(1)} %copy-done.4, bf16[4,128,1024]{2,0,1:T(4,128)(2,1)S(1)} %copy.98, bf16[3,128,1024]{2,0,1:T(4,128)(2,1)S(1)} %copy-done.7, ...), kind=kLoop, calls=%fused_computation.73 | loop fusion | flops 21463040 | bytes 8110080 | tf_op jit(solution)/shard_map/concatenate | solution.py:23
  55.1 37.8 %all-gather.3.cloned.1.call-done = bf16[1024,4096]{1,0:T(8,128)(2,1)} async-done(((bf16[64,4096]{1,0:T(8,128)(2,1)}), bf16[1024,4096]{1,0:T(8,128)(2,1)}) %all-gather.3.cloned.1.call-update) | async-done | bytes 8388624 | tf_op jit(solution)/shard_map/all_gather | solution.py:60
  92.9 10.5 %multiply_convert_fusion.2 = (bf16[512,4096]{1,0:T(8,128)(2,1)}, f32[512,4096]{1,0:T(8,128)}) fusion(bf16[512,1024]{1,0:T(8,128)(2,1)} %multiply_convert_fusion.3, bf16[1024,4096]{1,0:T(8,128)(2,1)} %all-gather.3.cloned.1.call-done), kind=kOutput, calls=%fused_computation.59 | convolution fusion | flops 4305453056 | bytes 22020096 | tf_op jit(solution)/shard_map/dot_general | solution.py:73
  103.4 64.8 %all-gather.5.cloned.1.call-done = bf16[4096,1024]{0,1:T(8,128)(2,1)} async-done(((bf16[4096,64]{0,1:T(8,128)(2,1)}), bf16[4096,1024]{0,1:T(8,128)(2,1)}) %all-gather.5.cloned.1.call-update) | async-done | bytes 8388624 | tf_op jit(solution)/shard_map/all_gather | solution.py:61
  168.2 10.3 %fusion.5 = bf16[512,4096]{1,0:T(8,128)(2,1)S(1)} fusion(f32[512,4096]{1,0:T(8,128)} %get-tuple-element.111, bf16[512,1024]{1,0:T(8,128)(2,1)S(1)} %bitcast.142, bf16[4096,1024]{0,1:T(8,128)(2,1)} %all-gather.5.cloned.1.call-done), kind=kOutput, calls=%fused_computation.57 | convolution fusion | flops 4315938816 | bytes 22020096 | tf_op jit(solution)/shard_map/dot_general | solution.py:89
  178.6 6.8 %multiply_reduce_fusion = (f32[1024]{0:T(1024)}, f32[512]{0:T(512)S(1)}, f32[512]{0:T(512)S(1)}, f32[512,1024]{1,0:T(8,128)}) fusion(f32[4,1,128,1024]{3,2,0,1:T(8,128)S(1)} %copy-done.12, f32[512]{0:T(512)S(1)} %bitcast.198, f32[512]{0:T(512)S(1)} %bitcast.196, f32[1024]{0:T(1024)S(1)} %copy-done.19, bf16[512,4096]{1,0:T(8,128)(2,1)S(1)} %fusion.5, ...), kind=kOutput, calls=%fused_computation.156 | convolution fusion | flops 4299159552 | bytes 16793600 | tf_op jit(solution)/shard_map/dot_general | solution.py:100
  185.7 36.4 %fusion.71 = (f32[1024]{0:T(1024)S(1)}, f32[1024]{0:T(1024)}, f32[1024]{0:T(1024)}, f32[1024]{0:T(1024)}, f32[1024]{0:T(1024)}, /*index=5*/f32[1024]{0:T(1024)},...) fusion(bf16[10,131,1024]{2,0,1:T(8,128)(2,1)} %get-tuple-elemen, ...), kind=kLoop, calls=%fused_computation.140 | loop fusion | flops 33011712 | bytes 24203264 | tf_op jit(solution)/shard_map/reduce_sum | solution.py:50
  222.1 2.3 fusion.29
  224.4 13.1 %fusion.75 = (f32[1024]{0:T(1024)S(1)}, f32[1024]{0:T(1024)S(1)}, f32[1024]{0:T(1024)S(1)}, f32[1024]{0:T(1024)S(1)}, f32[1024]{0:T(1024)}, /*index=5*/f32[1024]...) fusion(bf16[4,128,1024]{2,0,1:T(4,128)(2,1)S(1)} %get-tuple-ele, ...), kind=kLoop, calls=%fused_computation.144 | loop fusion | flops 28817408 | bytes 19996672 | tf_op jit(solution)/shard_map/reduce_sum | solution.py:50
  237.6 7.0 %fusion.106 = f32[512,1024]{1,0:T(8,128)S(1)} fusion(bf16[512,4096]{1,0:T(8,128)(2,1)} %get-tuple-element.110, bf16[4096,1024]{0,1:T(8,128)(2,1)S(1)} %bitcast.200), kind=kOutput, calls=%fused_computation.198 | convolution fusion | flops 4294967296 | bytes 14680064 | tf_op jit(solution)/shard_map/dot_general | solution.py:77
  244.8 11.9 %fusion.74 = (f32[1024]{0:T(1024)S(1)}, f32[1024]{0:T(1024)S(1)}, f32[1024]{0:T(1024)S(1)}, f32[1024]{0:T(1024)S(1)}, f32[1024]{0:T(1024)S(1)}, /*index=5*/f32[1...) fusion(bf16[4,128,1024]{2,0,1:T(4,128)(2,1)S(1)} %get-tuple-ele, ...), kind=kLoop, calls=%fused_computation.143 | loop fusion | flops 26728448 | bytes 11051008 | tf_op jit(solution)/shard_map/reduce_sum | solution.py:50
  259.4 9.0 %multiply_convert_fusion.1 = bf16[1024,4096]{1,0:T(8,128)(2,1)} fusion(bf16[512,1024]{1,0:T(8,128)(2,1)S(1)} %copy-done.13, bf16[512,4096]{1,0:T(8,128)(2,1)} %copy-done.39), kind=kOutput, calls=%fused_computation.50 | convolution fusion | flops 4303355904 | bytes 13631488 | tf_op jit(solution)/shard_map/dot_general | solution.py:93
  269.6 9.1 %fusion.6 = bf16[1024,4096]{0,1:T(8,128)(2,1)} fusion(bf16[512,4096]{1,0:T(8,128)(2,1)} %get-tuple-element.110, bf16[512,1024]{1,0:T(8,128)(2,1)S(1)} %bitcast.143), kind=kOutput, calls=%fused_computation.58 | convolution fusion | flops 4303355904 | bytes 13631488 | tf_op jit(solution)/shard_map/dot_general | solution.py:81
  278.7 11.5 %copy.139 = bf16[1024,4096]{1,0:T(8,128)(2,1)} copy(bf16[1024,4096]{0,1:T(8,128)(2,1)} %fusion.6) | data formatting | bytes 16777216
  292.2 3.2 collective-permute-start.2
  299.5 36.1 %psum.15 = bf16[1024]{0:T(1024)(128)(2,1)S(1)} all-reduce(bf16[1024]{0:T(1024)(128)(2,1)S(1)} %multiply_convert_fusion.5), channel_id=1, replica_groups=mesh['grp'=2,'row'=16] {'row'}, use_global_device_ids=true, to_apply=%region_57.0 | all-reduce | flops 1024 | bytes 4096 | tf_op jit(solution)/shard_map/psum | solution.py:115
  336.2 7.3 %all-reduce.2.cloned.1.call-done = bf16[7,7,1024]{2,1,0:T(8,128)(2,1)} async-done(((bf16[7,7,1024]{2,1,0:T(8,128)(2,1)}), bf16[7,7,1024]{2,1,0:T(8,128)(2,1)}) %all-reduce.2.cloned.1.call-update) | async-done | bytes 100368 | tf_op jit(solution)/shard_map/psum | solution.py:114
  343.5 1.6 convert_element_type.261
  345.1 1.8 copy.119
  347.0 1.8 copy.120
  348.8 3.5 fusion.10
  353.5 1.5 copy.123
  355.3 9.4 %fusion.85 = f32[4,8,17,1024]{3,1,2,0:T(8,128)S(1)} fusion(bf16[10,1,7,6,1024]{4,2,3,0,1:T(8,128)(2,1)S(1)} %slice.280, bf16[10,1,8,17,1024]{4,2,3,0,1:T(8,128)(2,1)S(1)} %copy.123, pred[8,17]{0,1:T(8,128)(4,1)S(1)} %copy-done.38, bf16[7,7,1,1024]{3,1,0,2:T(8,128)(2,1)S(1)} %bitcast.145), kind=kOutput, calls=%fused_computation.163 | convolution fusion | flops 66453504 | bytes 5974152 | tf_op jit(solution)/shard_map/conv_general_dilated | solution.py:27
  368.6 86.3 %reduce-scatter.5.cloned.1.call-done = bf16[64,4096]{1,0:T(8,128)(2,1)} async-done(((bf16[1024,4096]{1,0:T(8,128)(2,1)}), bf16[64,4096]{1,0:T(8,128)(2,1)}) %reduce-scatter.5.cloned.1.call-update) | async-done | bytes 524304 | tf_op jit(solution)/shard_map/reduce_scatter | solution.py:92
  454.9 108.9 %reduce-scatter.7.cloned.1.call-done = bf16[64,4096]{1,0:T(8,128)(2,1)} async-done(((bf16[1024,4096]{1,0:T(8,128)(2,1)}), bf16[64,4096]{1,0:T(8,128)(2,1)}) %reduce-scatter.7.cloned.1.call-update) | async-done | bytes 524304
  (149 shorter events, 30.0 us)
Async XLA Ops:
  7.2 85.7 %all-gather.3.cloned.1.call-start = ((), (), s32[]{:S(2)}) async-start(), calls=%async_computation.2 | async-start | bytes 8912896 | tf_op jit(solution)/shard_map/all_gather | solution.py:60
  7.9 160.3 %all-gather.5.cloned.1.call-start = ((), (), s32[]{:S(2)}) async-start(), calls=%async_computation.3 | async-start | bytes 8912896 | tf_op jit(solution)/shard_map/all_gather | solution.py:61
  8.7 334.9 %all-reduce.2.cloned.1.call-start = ((), (), s32[]{:S(2)}) async-start(), calls=%async_computation.5 | async-start | bytes 229376 | tf_op jit(solution)/shard_map/psum | solution.py:114
  10.2 5.2 collective-permute-start.1
  11.5 4.9 collective-permute-start
  15.5 29.5 %copy-start.1 = (bf16[4,128,1024]{2,0,1:T(4,128)(2,1)}, bf16[4,128,1024]{2,0,1:T(4,128)(2,1)S(1)}, u32[]{:S(2)}) copy-start(bf16[4,128,1024]{2,0,1:T(4,128)(2,1)S(1)} %copy.98) | copy-start | bytes 3145732
  55.1 113.1 %copy-start.14 = (bf16[4,128,1024]{2,1,0:T(8,128)(2,1)S(1)}, bf16[4,128,1024]{2,1,0:T(8,128)(2,1)}, u32[]{:S(2)}) copy-start(bf16[4,128,1024]{2,1,0:T(8,128)(2,1)} %param.11) | copy-start | bytes 3145732
  185.6 38.7 %slice-start = ((s8[4292608]{0:T(1024)(128)(4,1)}), s8[4194304]{0:T(1024)(128)(4,1)S(1)}, s32[]{:S(2)}) async-start(s8[4292608]{0:T(1024)(128)(4,1)} %bitcast.132), calls=%async_computation.7 | async-start | bytes 8388608
  185.6 36.4 %copy-start = (bf16[10,131,1024]{2,0,1:T(8,128)(2,1)S(1)}, bf16[10,131,1024]{2,0,1:T(8,128)(2,1)}, u32[]{:S(2)}) copy-start(bf16[10,131,1024]{2,0,1:T(8,128)(2,1)} %get-tuple-element.99) | copy-start | bytes 8048644
  185.6 38.7 %slice-start.1 = ((s8[4292608]{0:T(1024)(128)(4,1)}), s8[98304]{0:T(1024)(128)(4,1)S(1)}, s32[]{:S(2)}) async-start(s8[4292608]{0:T(1024)(128)(4,1)} %bitcast.132), calls=%async_computation.8 | async-start | bytes 196608
  222.1 15.5 %slice-start.2 = ((s8[8388608]{0:T(1024)(128)(4,1)}), s8[4194304]{0:T(1024)(128)(4,1)S(1)}, s32[]{:S(2)}) async-start(s8[8388608]{0:T(1024)(128)(4,1)} %bitcast.199), calls=%async_computation.9 | async-start | bytes 8388608
  224.4 13.2 %slice-start.3 = ((s8[8388608]{0:T(1024)(128)(4,1)}), s8[4194304]{0:T(1024)(128)(4,1)S(1)}, s32[]{:S(2)}) async-start(s8[8388608]{0:T(1024)(128)(4,1)} %bitcast.199), calls=%async_computation.10 | async-start | bytes 8388608
  244.6 12.1 %copy-start.32 = (f32[1024]{0:T(1024)S(1)}, f32[1024]{0:T(1024)}, u32[]{:S(2)}) copy-start(f32[1024]{0:T(1024)} %get-tuple-element.58) | copy-start | bytes 12292
  244.6 12.1 %copy-start.33 = (f32[1024]{0:T(1024)S(1)}, f32[1024]{0:T(1024)}, u32[]{:S(2)}) copy-start(f32[1024]{0:T(1024)} %get-tuple-element.59) | copy-start | bytes 12292
  244.6 12.1 %copy-start.34 = (f32[1024]{0:T(1024)S(1)}, f32[1024]{0:T(1024)}, u32[]{:S(2)}) copy-start(f32[1024]{0:T(1024)} %get-tuple-element.60) | copy-start | bytes 12292
  244.6 12.8 %copy-start.29 = (f32[1024]{0:T(1024)S(1)}, f32[1024]{0:T(1024)}, u32[]{:S(2)}) copy-start(f32[1024]{0:T(1024)} %get-tuple-element.61) | copy-start | bytes 12292
  244.7 12.8 %copy-start.30 = (f32[1024]{0:T(1024)S(1)}, f32[1024]{0:T(1024)}, u32[]{:S(2)}) copy-start(f32[1024]{0:T(1024)} %get-tuple-element.62) | copy-start | bytes 12292
  244.7 12.8 %copy-start.31 = (f32[1024]{0:T(1024)S(1)}, f32[1024]{0:T(1024)}, u32[]{:S(2)}) copy-start(f32[1024]{0:T(1024)} %get-tuple-element.63) | copy-start | bytes 12292
  244.7 13.6 %copy-start.26 = (f32[1024]{0:T(1024)S(1)}, f32[1024]{0:T(1024)}, u32[]{:S(2)}) copy-start(f32[1024]{0:T(1024)} %get-tuple-element.64) | copy-start | bytes 12292
  244.7 13.6 %copy-start.27 = (f32[1024]{0:T(1024)S(1)}, f32[1024]{0:T(1024)}, u32[]{:S(2)}) copy-start(f32[1024]{0:T(1024)} %get-tuple-element.65) | copy-start | bytes 12292
  244.7 13.6 %copy-start.28 = (f32[1024]{0:T(1024)S(1)}, f32[1024]{0:T(1024)}, u32[]{:S(2)}) copy-start(f32[1024]{0:T(1024)} %get-tuple-element.66) | copy-start | bytes 12292
  244.7 13.7 %copy-start.23 = (f32[1024]{0:T(1024)S(1)}, f32[1024]{0:T(1024)}, u32[]{:S(2)}) copy-start(f32[1024]{0:T(1024)} %get-tuple-element.67) | copy-start | bytes 12292
  244.7 13.7 %copy-start.24 = (f32[1024]{0:T(1024)S(1)}, f32[1024]{0:T(1024)}, u32[]{:S(2)}) copy-start(f32[1024]{0:T(1024)} %get-tuple-element.68) | copy-start | bytes 12292
  244.7 13.7 %copy-start.25 = (f32[1024]{0:T(1024)S(1)}, f32[1024]{0:T(1024)}, u32[]{:S(2)}) copy-start(f32[1024]{0:T(1024)} %get-tuple-element.69) | copy-start | bytes 12292
  244.7 13.7 %copy-start.20 = (f32[1024]{0:T(1024)S(1)}, f32[1024]{0:T(1024)}, u32[]{:S(2)}) copy-start(f32[1024]{0:T(1024)} %get-tuple-element.70) | copy-start | bytes 12292
  244.7 13.7 %copy-start.21 = (f32[1024]{0:T(1024)S(1)}, f32[1024]{0:T(1024)}, u32[]{:S(2)}) copy-start(f32[1024]{0:T(1024)} %get-tuple-element.71) | copy-start | bytes 12292
  244.8 13.7 %copy-start.22 = (f32[1024]{0:T(1024)S(1)}, f32[1024]{0:T(1024)}, u32[]{:S(2)}) copy-start(f32[1024]{0:T(1024)} %get-tuple-element.72) | copy-start | bytes 12292
  244.8 14.6 %copy-start.13 = (bf16[512,1024]{1,0:T(8,128)(2,1)S(1)}, bf16[512,1024]{1,0:T(8,128)(2,1)}, u32[]{:S(2)}) copy-start(bf16[512,1024]{1,0:T(8,128)(2,1)} %multiply_convert_fusion.3) | copy-start | bytes 3145732
  259.4 195.5 %reduce-scatter.5.cloned.1.call-start = ((), (), s32[]{:S(2)}) async-start(), calls=%async_computation.4 | async-start | bytes 8912896 | tf_op jit(solution)/shard_map/reduce_scatter | solution.py:92
  268.4 295.3 %reduce-scatter.7.cloned.1.call-start = ((), (), s32[]{:S(2)}) async-start(), calls=%async_computation.6 | async-start | bytes 8912896
  292.2 53.0 %collective-permute-start.2 = (bf16[3,128,1024]{2,1,0:T(8,128)(2,1)}, bf16[3,128,1024]{2,1,0:T(8,128)(2,1)}, u32[]{:S(2)}, u32[]{:S(2)}) collective-permute-start(bf16[3,128,1024]{2,1,0:T(8,128)(2,1)} %copy.117), channel_id=1, source_target_pairs={{0,1},{1,2},{2,3},{3,4},{4,5},{5,6},{6,7},{7,8},{8,9},{9,10},{10,1... | collective-permute-start | bytes 2359304 | tf_op jit(solution)/shard_map/ppermute | solution.py:16
  296.5 50.4 %collective-permute-start.3 = (bf16[3,128,1024]{2,1,0:T(8,128)(2,1)}, bf16[3,128,1024]{2,1,0:T(8,128)(2,1)}, u32[]{:S(2)}, u32[]{:S(2)}) collective-permute-start(bf16[3,128,1024]{2,1,0:T(8,128)(2,1)} %copy.118), channel_id=1, source_target_pairs={{1,0},{2,1},{3,2},{4,3},{5,4},{6,5},{7,6},{8,7},{9,8},{10,9},{11,1... | collective-permute-start | bytes 2359304 | tf_op jit(solution)/shard_map/ppermute | solution.py:17
  (21 other events, 105.4 us)
Sparse Core Ops, SparseCore 0:
  10.2 82.6 all-gather.2
  95.0 73.1 all-gather.4
  259.5 84.0 all-reduce.1
  348.0 106.8 reduce-scatter.4
  459.4 104.3 reduce-scatter.6
where the time goes:
time: 575 us; the launch traced here: 571 us
  waiting for transfers between devices  307 us (53%)
  other arithmetic  89 us (15%)
  matrix products  71.8 us (12%)
  local copies, waits for them, and re-layouts  42.8 us (7%)
  blocking collectives  36.1 us (6%)
  between operations  14.8 us (3%)
  starting transfers between devices  9.01 us (2%)
    unnamed x6, waiting for transfers between devices  110 us
    reduce_scatter x1, waiting for transfers between devices, on_device(): lax.psum_scatter((jnp.dot(picked.T, pre_grad, preferred_element_type=jnp....  86.3 us
    all_gather x1, waiting for transfers between devices, on_device(): lax.all_gather(proj_out, 'row', axis=1, tiled=True)  64.8 us
    reduce_sum x4, other arithmetic, kernel_sums(): line.append(jnp.sum(grad_wide * window, axis=(0, 1)))  63.7 us
    all_gather x1, waiting for transfers between devices, on_device(): lax.all_gather(proj_in, 'row', axis=0, tiled=True)  37.8 us
    psum x1, blocking collectives, on_device(): lax.psum(gain_local.astype(jnp.bfloat16), 'row').astype(jnp.float32)  36.1 us
    unnamed x100, local copies, waits for them, and re-layouts  19.3 us
    conv_general_dilated x2, matrix products, depthwise(): lax.conv_general_dilated(padded[None], kernel[:, :, None, :], (1, 1), 'VA...  19.2 us
  transfers between devices with their start and end apart: 9, of which 6 were waited for; matrix products, arithmetic and copies ran while one was open for 19% of the time, Pallas kernels for 0%

commit v1 on v0

v1 whole, which is shorter than its diff:
```python
import functools
import math

import jax
import jax.numpy as jnp
from jax import lax
from jax.experimental import pallas as pl
from jax.experimental.pallas import tpu as pltpu
from jax.sharding import PartitionSpec as P

F32 = jnp.float32
BF16 = jnp.bfloat16
KS = 7
RIM = KS // 2
LANES = 128
SUB = 8
MIB = 1024 * 1024


def cost(micros, nbytes=0):
    return pl.CostEstimate(flops=int(micros * 1.15e9), bytes_accessed=int(nbytes), transcendentals=0)


def params(mib):
    return pltpu.CompilerParams(vmem_limit_bytes=mib * MIB)


def whole(shape):
    return pl.BlockSpec(shape, lambda *_: (0,) * len(shape))


def fill_padded(before_ref, mid_ref, after_ref, pad_ref):
    lat, lon = mid_ref.shape[0], mid_ref.shape[1]
    for row in range(lat + 2 * RIM):
        if row < RIM:
            line = before_ref[row]
        elif row < RIM + lat:
            line = mid_ref[row - RIM]
        else:
            line = after_ref[row - RIM - lat]
        line = line.astype(F32)
        pad_ref[row, pl.ds(SUB, lon), :] = line
        pad_ref[row, pl.ds(0, SUB), :] = line[lon - SUB :]
        pad_ref[row, pl.ds(SUB + lon, SUB), :] = line[:SUB]


def conv_tile(pad_ref, weight_ref, start, lat, flip):
    totals = [None] * lat
    for b in range(KS):
        lines = [
            pad_ref[row, pl.ds(start + (SUB - RIM) + b, SUB), :] for row in range(lat + 2 * RIM)
        ]
        for a in range(KS):
            index = a * KS + b
            weight = weight_ref[KS * KS - 1 - index if flip else index]
            for row in range(lat):
                term = lines[row + a] * weight
                totals[row] = term if totals[row] is None else totals[row] + term
    return totals


def spread_weights(kern_ref, weight_ref):
    taps = kern_ref[...].astype(F32)
    for a in range(KS):
        for b in range(KS):
            weight_ref[a * KS + b] = jnp.broadcast_to(taps[a, b : b + 1], (SUB, LANES))


def forward_body(
    before_ref, mid_ref, after_ref, kern_ref, gain_ref, normed_ref, white_ref, inv_ref, pad_ref, weight_ref, conv_ref
):
    step = pl.program_id(0)
    lat, lon = mid_ref.shape[0], mid_ref.shape[1]
    blocks = conv_ref.shape[0]
    fill_padded(before_ref, mid_ref, after_ref, pad_ref)
    spread_weights(kern_ref, weight_ref)

    def tile(t, carry):
        start = pl.multiple_of(t * SUB, SUB)
        for row, total in enumerate(conv_tile(pad_ref, weight_ref, start, lat, False)):
            conv_ref[step, pl.ds(pl.multiple_of(row * lon + start, SUB), SUB), :] = total
        return carry

    lax.fori_loop(0, lon // SUB, tile, 0)

    @pl.when(step == blocks - 1)
    def _():
        channels = blocks * LANES
        high = 32

        def norm(t, carry):
            at = pl.ds(pl.multiple_of(t * high, high), high)
            parts = [conv_ref[j, at, :] for j in range(blocks)]
            mean = jnp.sum(functools.reduce(jnp.add, parts), axis=-1, keepdims=True) * (1.0 / channels)
            parts = [p - mean for p in parts]
            squares = functools.reduce(jnp.add, [p * p for p in parts])
            var = jnp.sum(squares, axis=-1, keepdims=True) * (1.0 / channels)
            inv = lax.rsqrt(var + 1e-06)
            inv_ref[at, :] = jnp.broadcast_to(inv, (high, LANES))
            for j in range(blocks):
                cols = slice(j * LANES, (j + 1) * LANES)
                white = parts[j] * inv
                white_ref[at, cols] = white
                normed_ref[at, cols] = (white * gain_ref[:, cols]).astype(BF16)
            return carry

        lax.fori_loop(0, conv_ref.shape[1] // high, norm, 0)


def forward_norm(before, mid, after, kernel, gain):
    lat, lon, channels = mid.shape
    tokens = lat * lon
    blocks = channels // LANES
    rows = lambda n: pl.BlockSpec((n, lon, LANES), lambda i: (0, 0, i))
    return pl.pallas_call(
        forward_body,
        grid=(blocks,),
        in_specs=[
            rows(RIM),
            rows(lat),
            rows(RIM),
            pl.BlockSpec((KS, KS, LANES), lambda i: (0, 0, i)),
            whole((1, channels)),
        ],
        out_specs=[whole((tokens, channels)), whole((tokens, channels)), whole((tokens, LANES))],
        out_shape=[
            jax.ShapeDtypeStruct((tokens, channels), BF16),
            jax.ShapeDtypeStruct((tokens, channels), F32),
            jax.ShapeDtypeStruct((tokens, LANES), F32),
        ],
        scratch_shapes=[
            pltpu.VMEM((lat + 2 * RIM, lon + 2 * SUB, LANES), F32),
            pltpu.VMEM((KS * KS, SUB, LANES), F32),
            pltpu.VMEM((blocks, tokens, LANES), F32),
        ],
        compiler_params=params(20),
        cost_estimate=cost(16),
        name="forward_norm",
    )(before, mid, after, kernel, gain.reshape(1, channels))


def backward_body(before_ref, mid_ref, after_ref, kern_ref, cot_ref, out_ref, pad_ref, weight_ref, sum_ref):
    lat, lon = mid_ref.shape[0], mid_ref.shape[1]
    fill_padded(before_ref, mid_ref, after_ref, pad_ref)
    spread_weights(kern_ref, weight_ref)

    def tile(t, carry):
        start = pl.multiple_of(t * SUB, SUB)
        for row, total in enumerate(conv_tile(pad_ref, weight_ref, start, lat, True)):
            sum_ref[row, pl.ds(start, SUB), :] = total
        return carry

    lax.fori_loop(0, lon // SUB, tile, 0)
    for row in range(lat):
        out_ref[row] = (cot_ref[row].astype(F32) + sum_ref[row]).astype(BF16)


def backward_conv(before, mid, after, kernel, cot):
    lat, lon, channels = mid.shape
    tokens = lat * lon
    rows = lambda n: pl.BlockSpec((n, lon, LANES), lambda i: (0, 0, i))
    return pl.pallas_call(
        backward_body,
        grid=(channels // LANES,),
        in_specs=[
            rows(RIM),
            rows(lat),
            rows(RIM),
            pl.BlockSpec((KS, KS, LANES), lambda i: (0, 0, i)),
            rows(lat),
        ],
        out_specs=rows(lat),
        out_shape=jax.ShapeDtypeStruct((lat, lon, channels), BF16),
        scratch_shapes=[
            pltpu.VMEM((lat + 2 * RIM, lon + 2 * SUB, LANES), F32),
            pltpu.VMEM((KS * KS, SUB, LANES), F32),
            pltpu.VMEM((lat, lon, LANES), F32),
        ],
        compiler_params=params(20),
        cost_estimate=cost(14),
        name="backward_conv",
    )(before, mid, after, kernel, cot)


def tap_sums_body(scale, before_ref, mid_ref, after_ref, grad_ref, out_ref, pad_ref, wide_ref):
    lat, lon = mid_ref.shape[0], mid_ref.shape[1]
    fill_padded(before_ref, mid_ref, after_ref, pad_ref)
    for row in range(lat):
        wide_ref[row] = grad_ref[row].astype(F32)
    for b in range(KS):

        def tile(t, totals, b=b):
            start = pl.multiple_of(t * SUB, SUB)
            grads = [wide_ref[row, pl.ds(start, SUB), :] for row in range(lat)]
            lines = [
                pad_ref[row, pl.ds(start + (SUB - RIM) + b, SUB), :] for row in range(lat + 2 * RIM)
            ]
            return tuple(
                totals[a] + functools.reduce(jnp.add, [grads[row] * lines[row + a] for row in range(lat)])
                for a in range(KS)
            )

        zero = jnp.zeros((SUB, LANES), F32)
        totals = lax.fori_loop(0, lon // SUB, tile, (zero,) * KS)
        for a in range(KS):
            out_ref[a, b : b + 1, :] = jnp.sum(totals[a], axis=0, keepdims=True) * scale


def tap_sums(before, mid, after, grad, scale):
    lat, lon, channels = mid.shape
    tokens = lat * lon
    rows = lambda n: pl.BlockSpec((n, lon, LANES), lambda i: (0, 0, i))
    return pl.pallas_call(
        functools.partial(tap_sums_body, scale),
        grid=(channels // LANES,),
        in_specs=[rows(RIM), rows(lat), rows(RIM), rows(lat)],
        out_specs=pl.BlockSpec((KS, KS, LANES), lambda i: (0, 0, i)),
        out_shape=jax.ShapeDtypeStruct((KS, KS, channels), F32),
        scratch_shapes=[
            pltpu.VMEM((lat + 2 * RIM, lon + 2 * SUB, LANES), F32),
            pltpu.VMEM((lat, lon, LANES), F32),
        ],
        compiler_params=params(20),
        cost_estimate=cost(14),
        name="tap_sums",
    )(before, mid, after, grad)


def hidden_body(n_blocks, chips_ref, n_own, n_sib, c_own, c_sib, *refs):
    shards = refs[:n_blocks]
    last_in, last_out = refs[n_blocks], refs[n_blocks + 1]
    hid_ref, grad_ref, win_ref, wout_ref, sems = refs[n_blocks + 2 :]
    size = last_in.shape[0]

    @pl.when(pl.program_id(0) == 0)
    def _():
        copies = []
        for j in range(n_blocks + 1):
            at = pl.ds(pl.multiple_of(chips_ref[j] * size, size), size)
            pair = (shards[j].at[0], shards[j].at[1]) if j < n_blocks else (last_in, last_out)
            for k, (src, dst) in enumerate(zip(pair, (win_ref, wout_ref))):
                copies.append(pltpu.make_async_copy(src, dst.at[at, :], sems.at[2 * j + k]))
        for copy in copies:
            copy.start()
        for copy in copies:
            copy.wait()

    wide = 256
    for half, (n_ref, c_ref) in enumerate(((n_own, c_own), (n_sib, c_sib))):
        for col in range(win_ref.shape[1] // wide):
            cols = slice(col * wide, (col + 1) * wide)
            pre = jnp.dot(n_ref[...], win_ref[:, cols], preferred_element_type=F32)
            back = jnp.dot(c_ref[...], wout_ref[:, cols], preferred_element_type=F32)
            area = 0.5 * (1.0 + lax.erf(pre * (1.0 / math.sqrt(2.0))))
            dens = jnp.exp(-0.5 * pre * pre) * (1.0 / math.sqrt(2.0 * math.pi))
            hid_ref[half, :, cols] = (pre * area).astype(BF16)
            grad_ref[half, :, cols] = (back * (area + pre * dens)).astype(BF16)


def hidden_step(chips, n_own, n_sib, c_own, c_sib, shards, last_in, last_out):
    tokens, channels = n_own.shape
    width = last_in.shape[1]
    high = 256
    toks = pl.BlockSpec((high, channels), lambda i, s: (i, 0))
    both = pl.BlockSpec((2, high, width), lambda i, s: (0, i, 0))
    return pl.pallas_call(
        functools.partial(hidden_body, len(shards)),
        grid_spec=pltpu.PrefetchScalarGridSpec(
            num_scalar_prefetch=1,
            grid=(tokens // high,),
            in_specs=[toks] * 4 + [pl.BlockSpec(memory_space=pl.ANY)] * (len(shards) + 2),
            out_specs=[both, both, whole((channels, width)), whole((channels, width))],
            scratch_shapes=[pltpu.SemaphoreType.DMA((2 * len(shards) + 2,))],
        ),
        out_shape=[
            jax.ShapeDtypeStruct((2, tokens, width), BF16),
            jax.ShapeDtypeStruct((2, tokens, width), BF16),
            jax.ShapeDtypeStruct((channels, width), BF16),
            jax.ShapeDtypeStruct((channels, width), BF16),
        ],
        compiler_params=params(24),
        cost_estimate=cost(11),
        name="hidden_step",
    )(chips, n_own, n_sib, c_own, c_sib, *shards, last_in, last_out)


def weight_grad_body(scale, n_own, n_sib, c_own, c_sib, hid_ref, grad_ref, out_ref):
    contract = (((0,), (0,)), ((), ()))
    for which, (own, sib, rhs) in enumerate(((n_own, n_sib, grad_ref), (c_own, c_sib, hid_ref))):
        total = lax.dot_general(own[...], rhs[0], contract, preferred_element_type=F32)
        total = total + lax.dot_general(sib[...], rhs[1], contract, preferred_element_type=F32)
        out_ref[which] = (total * scale).astype(BF16)


def weight_grads(n_own, n_sib, c_own, c_sib, hid, grad, scale):
    tokens, channels = n_own.shape
    width = hid.shape[2]
    tall = 256
    cols = pl.BlockSpec((tokens, tall), lambda i: (0, i))
    return pl.pallas_call(
        functools.partial(weight_grad_body, scale),
        grid=(channels // tall,),
        in_specs=[cols] * 4 + [whole((2, tokens, width))] * 2,
        out_specs=pl.BlockSpec((2, tall, width), lambda i: (0, i, 0)),
        out_shape=jax.ShapeDtypeStruct((2, channels, width), BF16),
        compiler_params=params(24),
        cost_estimate=cost(8),
        name="weight_grads",
    )(n_own, n_sib, c_own, c_sib, hid, grad)


def spread_first_body(lhs_ref, w_ref, out_ref):
    contract = (((1,), (1,)), ((), ()))
    for half in range(2):
        out_ref[half] = lax.dot_general(lhs_ref[half], w_ref[...], contract, preferred_element_type=F32)


def spread_last_body(lhs_ref, w_ref, prev_ref, own_ref, sib_ref):
    contract = (((1,), (1,)), ((), ()))
    own_ref[...] = prev_ref[0] + lax.dot_general(lhs_ref[0], w_ref[...], contract, preferred_element_type=F32)
    sib = prev_ref[1] + lax.dot_general(lhs_ref[1], w_ref[...], contract, preferred_element_type=F32)
    sib_ref[...] = sib.astype(BF16)


def spread(lhs, weight, prev=None):
    _, tokens, width = lhs.shape
    channels = weight.shape[0]
    high = 256
    left = pl.BlockSpec((2, high, width), lambda i: (0, i, 0))
    pair = pl.BlockSpec((2, high, channels), lambda i: (0, i, 0))
    one = pl.BlockSpec((high, channels), lambda i: (i, 0))
    common = dict(
        grid=(tokens // high,),
        compiler_params=params(24),
        cost_estimate=cost(3.5),
    )
    if prev is None:
        return pl.pallas_call(
            spread_first_body,
            in_specs=[left, whole((channels, width))],
            out_specs=pair,
            out_shape=jax.ShapeDtypeStruct((2, tokens, channels), F32),
            name="spread_first",
            **common,
        )(lhs, weight)
    return pl.pallas_call(
        spread_last_body,
        in_specs=[left, whole((channels, width)), pair],
        out_specs=[one, one],
        out_shape=[
            jax.ShapeDtypeStruct((tokens, channels), F32),
            jax.ShapeDtypeStruct((tokens, channels), BF16),
        ],
        name="spread_last",
        **common,
    )(lhs, weight, prev)


def norm_back_body(scale, own_ref, sib_ref, white_ref, inv_ref, gain_ref, out_ref, gsum_ref):
    channels = own_ref.shape[1]
    blocks = channels // LANES
    high = 16

    def tile(t, sums):
        at = pl.ds(pl.multiple_of(t * high, high), high)
        inv = inv_ref[at, :]
        terms, whites, new = [], [], []
        for j in range(blocks):
            cols = slice(j * LANES, (j + 1) * LANES)
            grad = own_ref[at, cols] + sib_ref[at, cols].astype(F32)
            white = white_ref[at, cols]
            new.append(sums[j] + jnp.sum((grad * white).reshape(high // SUB, SUB, LANES), axis=0))
            terms.append(grad * gain_ref[:, cols])
            whites.append(white)
        mean = jnp.sum(functools.reduce(jnp.add, terms), axis=-1, keepdims=True) * (1.0 / channels)
        cross = functools.reduce(jnp.add, [g * w for g, w in zip(terms, whites)])
        cross = jnp.sum(cross, axis=-1, keepdims=True) * (1.0 / channels)
        for j in range(blocks):
            cols = slice(j * LANES, (j + 1) * LANES)
            out_ref[at, cols] = (inv * (terms[j] - mean - whites[j] * cross)).astype(BF16)
        return tuple(new)

    zero = jnp.zeros((SUB, LANES), F32)
    sums = lax.fori_loop(0, own_ref.shape[0] // high, tile, (zero,) * blocks)
    for j in range(blocks):
        gsum_ref[:, j * LANES : (j + 1) * LANES] = jnp.sum(sums[j], axis=0, keepdims=True) * scale


def norm_back(own, sib, white, inv, gain, scale):
    tokens, channels = own.shape
    return pl.pallas_call(
        functools.partial(norm_back_body, scale),
        in_specs=[pl.BlockSpec(memory_space=pltpu.VMEM)] * 5,
        out_specs=[pl.BlockSpec(memory_space=pltpu.VMEM)] * 2,
        out_shape=[
            jax.ShapeDtypeStruct((tokens, channels), BF16),
            jax.ShapeDtypeStruct((1, channels), F32),
        ],
        compiler_params=params(20),
        cost_estimate=cost(3.5),
        name="norm_back",
    )(own, sib, white, inv, gain.reshape(1, channels))


def ring_order(stations):
    if stations == 8:
        return [0, 2, 4, 6, 7, 5, 3, 1]
    return list(range(stations))


def added(a, b):
    return (a.astype(F32) + b.astype(F32)).astype(BF16)


def on_device(fields, kernel, norm_gain, proj_in, proj_out, cotangent):
    lat, lon, channels = fields.shape
    row_devs = lax.axis_size("row")
    stations = row_devs // 2
    half = stations // 2
    scale = 1.0 / math.sqrt(lat * row_devs * lon)
    me = lax.axis_index("row")
    core, chip = me % 2, me // 2
    order = ring_order(stations)
    place = [order.index(i) for i in range(stations)]
    slots = [0] + [d for r in range(1, half) for d in (-r, r)] + [half]
    table = [[order[(place[p] + d) % stations] for d in slots] for p in range(stations)]
    chips = lax.dynamic_index_in_dim(jnp.array(table, jnp.int32), chip, 0, keepdims=False)
    away = lambda d: chips[slots.index(half if abs(d) == half else d)]

    def ring(step):
        return [
            (order[i] * 2 + c, order[(i + step) % stations] * 2 + c)
            for i in range(stations)
            for c in range(2)
        ]

    onward, backward = ring(1), ring(-1)
    swap = [(i, i ^ 1) for i in range(row_devs)]
    up = [(i, i + 1) for i in range(row_devs - 1)]
    down = [(i + 1, i) for i in range(row_devs - 1)]
    send = lambda value, pairs: lax.ppermute(value, "row", pairs)

    hid = proj_in.shape[1]
    mine = hid // 2
    chunks = 2
    width = mine // chunks
    size = channels // stations

    weights = jnp.stack([proj_in, proj_out.T])
    kept = lax.dynamic_slice_in_dim(weights, core * mine, mine, axis=2)
    given = lax.dynamic_slice_in_dim(weights, (1 - core) * mine, mine, axis=2)
    got = send(given, swap)
    shard = jnp.where(
        core == 0, jnp.concatenate([kept, got], axis=1), jnp.concatenate([got, kept], axis=1)
    )

    before = send(fields[lat - RIM :], up)
    after = send(fields[:RIM], down)

    def gather(part):
        on, back = part, part
        found = [part]
        for r in range(1, half):
            on, back = send(on, onward), send(back, backward)
            found += [on, back]
        last_in = send(on[0], onward)
        last_out = send(back[1], backward)
        return found, last_in, last_out

    parts = [shard[:, :, c * width : (c + 1) * width] for c in range(chunks)]
    gathered = []
    for c in range(chunks):
        part = parts[c]
        if c:
            part, _ = lax.optimization_barrier((part, gathered[-1][1]))
        gathered.append(gather(part))

    c_own = cotangent.reshape(-1, channels)
    c_sib = send(c_own, swap)
    n_own, white, inv = forward_norm(before, fields, after, kernel, norm_gain)
    n_sib = send(n_own, swap)

    def block(grads, d):
        return lax.dynamic_slice_in_dim(grads, away(d) * size, size, axis=1)

    def scatter(grads):
        on, back = None, None
        for d in range(half, 0, -1):
            ahead, behind = block(grads, d), block(grads, -d)
            if d == half:
                on, back = ahead[0], behind[1]
            elif d == half - 1:
                on = jnp.stack([added(ahead[0], on), ahead[1]])
                back = jnp.stack([behind[0], added(behind[1], back)])
            else:
                on, back = added(ahead, on), added(behind, back)
            on, back = send(on, onward), send(back, backward)
        total = block(grads, 0).astype(F32) + on.astype(F32) + back.astype(F32)
        return total.astype(BF16)

    branch = ngrad = None
    shares = []
    for c in range(chunks):
        found, last_in, last_out = gathered[c]
        hidden, pre_grad, w_in, w_out = hidden_step(
            chips, n_own, n_sib, c_own, c_sib, found, last_in, last_out
        )
        grads = weight_grads(n_own, n_sib, c_own, c_sib, hidden, pre_grad, scale)
        shares.append(scatter(grads))
        ngrad = spread(pre_grad, w_in, ngrad)
        branch = spread(hidden, w_out, branch)

    ng_sib = send(ngrad[1], swap)
    br_sib = send(branch[1], swap)
    conv_grad, gain_local = norm_back(ngrad[0], ng_sib, white, inv, norm_gain, scale)
    conv_grad = conv_grad.reshape(lat, lon, channels)
    g_before = send(conv_grad[lat - RIM :], up)
    g_after = send(conv_grad[:RIM], down)
    taps_local = tap_sums(before, fields, after, conv_grad, scale)
    result = (
        fields.astype(F32)
        + (branch[0] + br_sib.astype(F32)).reshape(fields.shape)
    ).astype(BF16)
    fields_grad = backward_conv(g_before, conv_grad, g_after, kernel, cotangent)

    small = jnp.concatenate([taps_local.reshape(KS * KS, channels), gain_local], axis=0)
    bit = 1
    while bit < row_devs:
        low = small.astype(BF16)
        other = send(low, [(i, i ^ bit) for i in range(row_devs)])
        small = low.astype(F32) + other.astype(F32)
        bit *= 2
    kernel_grad = small[: KS * KS].reshape(KS, KS, channels)
    gain_grad = small[KS * KS]

    share = jnp.concatenate(shares, axis=2)
    rows = size // 2
    keep = lax.dynamic_slice_in_dim(share, core * rows, rows, axis=1)
    give = lax.dynamic_slice_in_dim(share, (1 - core) * rows, rows, axis=1)
    got = send(give, swap)
    final = jnp.where(
        core == 0, jnp.concatenate([keep, got], axis=2), jnp.concatenate([got, keep], axis=2)
    )
    return (result, fields_grad, final[0], final[1].T, kernel_grad, gain_grad)


def solution(mesh):
    in_specs = (
        P(("grp", "row"), None, None),
        P(None, None, "grp"),
        P("grp"),
        P(("grp", "row"), None),
        P("grp", "row"),
        P(("grp", "row"), None, None),
    )
    out_specs = (
        P(("grp", "row"), None, None),
        P(("grp", "row"), None, None),
        P(("grp", "row"), None),
        P("grp", "row"),
        P(None, None, "grp"),
        P("grp"),
    )
    return jax.shard_map(
        on_device, mesh=mesh, in_specs=in_specs, out_specs=out_specs, check_vma=False
    )
```

time: 575 us -> 320 us (0.56)
  waiting for transfers between devices: 307 us -> 108 us
  Pallas kernels: 0 us -> 93.5 us
  matrix products: 71.8 us -> 0 us
  other arithmetic: 89 us -> 22.8 us
  starting transfers between devices: 9.01 us -> 67.8 us
  blocking collectives: 36.1 us -> 0 us
  local copies, waits for them, and re-layouts: 42.8 us -> 20.1 us
  between operations: 14.8 us -> 6.49 us
    unnamed x6 -> x0, waiting for transfers between devices: 110 us -> none
    ppermute x4 -> x46, waiting for transfers between devices: 0.31 us -> 108 us  [on_device(): send = lambda value, pairs: lax.ppermute(value, 'row', pairs)]
    all_gather x2 -> x0, waiting for transfers between devices: 103 us -> none  [the longest x1 64.8 us: on_device(): lax.all_gather(proj_out, 'row', axis=1, tiled=True)]
    pallas_call x0 -> x12, Pallas kernels: none -> 93.5 us  [the longest x2 19.4 us: hidden_step(): pl.pallas_call(functools.partial(hidden_body, len(shards)), grid_spec=plt...]
    reduce_scatter x1 -> x0, waiting for transfers between devices: 86.3 us -> none  [on_device(): lax.psum_scatter((jnp.dot(picked.T, pre_grad, preferred_element_type=jnp....]
    reduce_sum x6 -> x0, other arithmetic: 66.2 us -> none  [the longest x4 63.7 us: kernel_sums(): line.append(jnp.sum(grad_wide * window, axis=(0, 1)))]
    ppermute x4 -> x46, starting transfers between devices: 8.82 us -> 67.8 us  [on_device(): send = lambda value, pairs: lax.ppermute(value, 'row', pairs)]
    dot_general x6 -> x0, matrix products: 52.7 us -> none  [the longest x1 10.5 us: on_device(): pre_act = jnp.dot(flat_norm, full_in, preferred_element_type=jnp.float32)]
  transfers between devices with their start and end apart: 9 -> 46, of which waited for: 6 -> 19; matrix products, arithmetic and copies ran while one was open for 19% -> 8% of each run, Pallas kernels for 0% -> 24%
where the time goes in v1:
time: 320 us; the launch traced here: 319 us
  waiting for transfers between devices  108 us (34%)
  Pallas kernels  93.5 us (29%)
  starting transfers between devices  67.8 us (21%)
  other arithmetic  22.8 us (7%)
  local copies, waits for them, and re-layouts  20.1 us (6%)
  between operations  6.49 us (2%)
    ppermute x46, waiting for transfers between devices, on_device(): send = lambda value, pairs: lax.ppermute(value, 'row', pairs)  108 us
    ppermute x46, starting transfers between devices, on_device(): send = lambda value, pairs: lax.ppermute(value, 'row', pairs)  67.8 us
    pallas_call x2, Pallas kernels, hidden_step(): pl.pallas_call(functools.partial(hidden_body, len(shards)), grid_spec=plt...  19.4 us
    pallas_call x1, Pallas kernels, forward_norm(): pl.pallas_call(forward_body, grid=(blocks,), in_specs=[rows(RIM), rows(la...  16.5 us
    pallas_call x2, Pallas kernels, weight_grads(): pl.pallas_call(functools.partial(weight_grad_body, scale), grid=(channels...  14.1 us
    pallas_call x1, Pallas kernels, tap_sums(): pl.pallas_call(functools.partial(tap_sums_body, scale), grid=(channels //...  14.1 us
    pallas_call x1, Pallas kernels, backward_conv(): pl.pallas_call(backward_body, grid=(channels // LANES,), in_specs=[rows(R...  13.9 us
    unnamed x66, local copies, waits for them, and re-layouts  13.1 us
  transfers between devices with their start and end apart: 46, of which 19 were waited for; matrix products, arithmetic and copies ran while one was open for 8% of the time, Pallas kernels for 24%

profile of v1, /device:TPU:0, one launch (start us, length us, event | category | flops | bytes accessed | tf_op | source)
XLA Modules:
  0.0 319.2 jit_solution(9282238731885142417)
XLA Ops:
  4.4 2.9 collective-permute-start.17
  8.7 3.1 collective-permute-start
  13.8 8.5 %collective-permute-done.17.refs_2_ = bf16[2,128,1024]{2,1,0:T(8,128)(2,1)S(1)} collective-permute-done((bf16[2,128,1024]{2,1,0:T(8,128)(2,1)S(1)}, bf16[2,128,1024]{2,1,0:T(8,128)(2,1)S(1)}, u32[]{:S(2)}, u32[]{:S(2)}) %collective-permute-start.17) | collective-permute-done | bytes 524320 | tf_op jit(solution)/shard_map/ppermute | solution.py:441
  22.3 3.0 collective-permute-start.18
  26.1 7.8 %collective-permute-done.5.refs_1_ = bf16[2,128,1024]{2,1,0:T(8,128)(2,1)S(1)} collective-permute-done((bf16[2,128,1024]{2,1,0:T(8,128)(2,1)S(1)}, bf16[2,128,1024]{2,1,0:T(8,128)(2,1)S(1)}, u32[]{:S(2)}, u32[]{:S(2)}) %collective-permute-start.5) | collective-permute-done | bytes 524320 | tf_op jit(solution)/shard_map/ppermute | solution.py:441
  33.9 7.2 %collective-permute-done.18.refs_4_ = bf16[2,128,1024]{2,1,0:T(8,128)(2,1)S(1)} collective-permute-done((bf16[2,128,1024]{2,1,0:T(8,128)(2,1)S(1)}, bf16[2,128,1024]{2,1,0:T(8,128)(2,1)S(1)}, u32[]{:S(2)}, u32[]{:S(2)}) %collective-permute-start.18) | collective-permute-done | bytes 524320 | tf_op jit(solution)/shard_map/ppermute | solution.py:441
  43.6 16.5 %forward_norm.1 = (bf16[512,1024]{1,0:T(8,128)(2,1)}, f32[512,1024]{1,0:T(8,128)S(1)}, f32[512,128]{1,0:T(8,128)S(1)}) custom-call(bf16[3,128,1024]{2,1,0:T(8,128)(2,1)S(1)} %collective-permute-done.before_ref, bf16[4,128,1024]{2,1,0:T(8,128)(2,1)S(1)} %copy-done, bf16[3,128,1024]{2,1,0:T(8,128)(2,1)S(1)} %collective-permute-done.1.after_ref, ...), custom_call_target="tpu_custom_call" | custom-call | flops 18400000000 | tf_op jit(solution)/shard_map/forward_norm/pallas_call | solution.py:115
  62.1 7.8 %collective-permute-start.2 = (bf16[512,1024]{1,0:T(8,128)(2,1)}, bf16[512,1024]{1,0:T(8,128)(2,1)}, u32[]{:S(2)}, u32[]{:S(2)}) collective-permute-start(bf16[512,1024]{1,0:T(8,128)(2,1)} %get-tuple-element.24.n_own), channel_id=1, source_target_pairs={{0,1},{1,0},{2,3},{3,2},{4,5},{5,4},{6,7},{7,6},{8,9},{9,8},{10,11... | collective-permute-start | bytes 3145736 | tf_op jit(solution)/shard_map/ppermute | solution.py:441
  72.7 11.1 %collective-permute-done.7.refs_5_ = bf16[2,128,1024]{2,1,0:T(8,128)(2,1)S(1)} collective-permute-done((bf16[2,128,1024]{2,1,0:T(8,128)(2,1)S(1)}, bf16[2,128,1024]{2,1,0:T(8,128)(2,1)S(1)}, u32[]{:S(2)}, u32[]{:S(2)}) %collective-permute-start.7) | collective-permute-done | bytes 524320 | tf_op jit(solution)/shard_map/ppermute | solution.py:441
  88.0 4.3 %collective-permute-done.8.refs_7_ = bf16[128,1024]{1,0:T(8,128)(2,1)} collective-permute-done((bf16[128,1024]{1,0:T(8,128)(2,1)}, bf16[128,1024]{1,0:T(8,128)(2,1)}, u32[]{:S(2)}, u32[]{:S(2)}) %collective-permute-start.8) | collective-permute-done | bytes 262176 | tf_op jit(solution)/shard_map/ppermute | solution.py:441
  96.4 9.7 %hidden_step.3 = (bf16[2,512,1024]{2,1,0:T(8,128)(2,1)S(1)}, bf16[2,512,1024]{2,1,0:T(8,128)(2,1)S(1)}, bf16[1024,1024]{1,0:T(8,128)(2,1)S(1)}, bf16[1024,1024]{1,0:T(8,128)(2,1)S(1)}) custom-call(s32[8]{0:T(128)S(1)} %get-tuple-element.71.chips_ref, bf16[512,1024]{1,0:T(8,128)(2,1)} %get-tuple-element.24.n_own, ...), custom_call_target="tpu_custom_call" | custom-call | flops 12650000384 | tf_op jit(solution)/shard_map/hidden_step/pallas_call | solution.py:266
  109.0 7.4 %weight_grads.2 = bf16[2,1024,1024]{2,1,0:T(8,128)(2,1)S(1)} custom-call(bf16[512,1024]{1,0:T(8,128)(2,1)} %get-tuple-element.24.n_own, bf16[512,1024]{1,0:T(8,128)(2,1)} %collective-permute-done.2.n_sib, bf16[512,1024]{1,0:T(8,128)(2,1)} %bitcast.2.c_own, bf16[512,1024]{1,0:T(8,128)(2,1)} %collective-permute-done.3.c_sib, ...), custom_call_target="tpu_custom_call" | custom-call | flops 9200000000 | tf_op jit(solution)/shard_map/weight_grads/pallas_call | solution.py:300
  122.4 4.7 %collective-permute-done.25 = bf16[128,1024]{1,0:T(8,128)(2,1)S(1)} collective-permute-done((bf16[128,1024]{1,0:T(8,128)(2,1)S(1)}, bf16[128,1024]{1,0:T(8,128)(2,1)S(1)}, u32[]{:S(2)}, u32[]{:S(2)}) %collective-permute-start.25) | collective-permute-done | bytes 262176 | tf_op jit(solution)/shard_map/ppermute | solution.py:441
  132.6 4.7 %collective-permute-done.10.refs_2_ = bf16[2,128,1024]{2,1,0:T(8,128)(2,1)S(1)} collective-permute-done((bf16[2,128,1024]{2,1,0:T(8,128)(2,1)S(1)}, bf16[2,128,1024]{2,1,0:T(8,128)(2,1)S(1)}, u32[]{:S(2)}, u32[]{:S(2)}) %collective-permute-start.10) | collective-permute-done | bytes 524320 | tf_op jit(solution)/shard_map/ppermute | solution.py:441
  143.7 6.0 %collective-permute-done.26 = bf16[2,128,1024]{2,1,0:T(8,128)(2,1)} collective-permute-done((bf16[2,128,1024]{2,1,0:T(8,128)(2,1)}, bf16[2,128,1024]{2,1,0:T(8,128)(2,1)}, u32[]{:S(2)}, u32[]{:S(2)}) %collective-permute-start.26) | collective-permute-done | bytes 524320 | tf_op jit(solution)/shard_map/ppermute | solution.py:441
  157.0 3.8 %collective-permute-done.11.refs_3_ = bf16[2,128,1024]{2,1,0:T(8,128)(2,1)} collective-permute-done((bf16[2,128,1024]{2,1,0:T(8,128)(2,1)S(1)}, bf16[2,128,1024]{2,1,0:T(8,128)(2,1)}, u32[]{:S(2)}, u32[]{:S(2)}) %collective-permute-start.11) | collective-permute-done | bytes 524320 | tf_op jit(solution)/shard_map/ppermute | solution.py:441
  164.8 3.0 spread_first.2.prev_ref
  167.8 4.3 %collective-permute-done.27 = bf16[2,128,1024]{2,1,0:T(8,128)(2,1)} collective-permute-done((bf16[2,128,1024]{2,1,0:T(8,128)(2,1)}, bf16[2,128,1024]{2,1,0:T(8,128)(2,1)}, u32[]{:S(2)}, u32[]{:S(2)}) %collective-permute-start.27) | collective-permute-done | bytes 524320 | tf_op jit(solution)/shard_map/ppermute | solution.py:441
  178.4 3.4 %collective-permute-done.13.refs_5_ = bf16[2,128,1024]{2,1,0:T(8,128)(2,1)S(1)} collective-permute-done((bf16[2,128,1024]{2,1,0:T(8,128)(2,1)}, bf16[2,128,1024]{2,1,0:T(8,128)(2,1)S(1)}, u32[]{:S(2)}, u32[]{:S(2)}) %collective-permute-start.13) | collective-permute-done | bytes 524320 | tf_op jit(solution)/shard_map/ppermute | solution.py:441
  182.2 3.0 spread_first.3.prev_ref
  194.2 9.7 %hidden_step.2 = (bf16[2,512,1024]{2,1,0:T(8,128)(2,1)S(1)}, bf16[2,512,1024]{2,1,0:T(8,128)(2,1)S(1)}, bf16[1024,1024]{1,0:T(8,128)(2,1)S(1)}, bf16[1024,1024]{1,0:T(8,128)(2,1)S(1)}) custom-call(s32[8]{0:T(128)S(1)} %get-tuple-element.71.chips_ref, bf16[512,1024]{1,0:T(8,128)(2,1)} %get-tuple-element.24.n_own, ...), custom_call_target="tpu_custom_call" | custom-call | flops 12650000384 | tf_op jit(solution)/shard_map/hidden_step/pallas_call | solution.py:266
  203.9 6.7 %weight_grads.3 = bf16[2,1024,1024]{2,1,0:T(8,128)(2,1)S(1)} custom-call(bf16[512,1024]{1,0:T(8,128)(2,1)} %get-tuple-element.24.n_own, bf16[512,1024]{1,0:T(8,128)(2,1)} %collective-permute-done.2.n_sib, bf16[512,1024]{1,0:T(8,128)(2,1)} %bitcast.2.c_own, bf16[512,1024]{1,0:T(8,128)(2,1)} %collective-permute-done.3.c_sib, ...), custom_call_target="tpu_custom_call" | custom-call | flops 9200000000 | tf_op jit(solution)/shard_map/weight_grads/pallas_call | solution.py:300
  213.3 3.0 spread_last.3
  216.4 3.0 spread_last.2
  225.1 3.4 %norm_back.1 = (bf16[512,1024]{1,0:T(8,128)(2,1)S(1)}, f32[1,1024]{1,0:T(1,128)S(1)}) custom-call(f32[512,1024]{1,0:T(8,128)S(1)} %get-tuple-element.36.own_ref, bf16[512,1024]{1,0:T(8,128)(2,1)S(1)} %collective-permute-done.22.sib_ref, f32[512,1024]{1,0:T(8,128)S(1)} %copy-done.29, f32[512,128]{1,0:T(8,128)S(1)} %copy-done.31, f32[1,1024]{1,0:T(1,128)S(1)} %bitcast.75), custom_call_target="tpu_custom_call" | custom-call | flops 4024999936 | tf_op jit(solution)/shard_map/norm_back/pallas_call | solution.py:391
  228.5 14.1 %tap_sums.1 = f32[7,7,1024]{2,1,0:T(8,128)S(1)} custom-call(bf16[3,128,1024]{2,1,0:T(8,128)(2,1)S(1)} %copy-done.9, bf16[4,128,1024]{2,1,0:T(8,128)(2,1)S(1)} %copy-done, bf16[3,128,1024]{2,1,0:T(8,128)(2,1)S(1)} %copy-done.7, bf16[4,128,1024]{2,1,0:T(8,128)(2,1)S(1)} %bitcast.72), custom_call_target="tpu_custom_call" | custom-call | flops 16099999744 | tf_op jit(solution)/shard_map/tap_sums/pallas_call | solution.py:213
  247.8 3.1 collective-permute-start.23
  250.9 10.4 %collective-permute-done.43 = bf16[50,1024]{1,0:T(8,128)(2,1)S(1)} collective-permute-done((bf16[50,1024]{1,0:T(8,128)(2,1)S(1)}, bf16[50,1024]{1,0:T(8,128)(2,1)S(1)}, u32[]{:S(2)}, u32[]{:S(2)}) %collective-permute-start.43) | collective-permute-done | bytes 102432 | tf_op jit(solution)/shard_map/ppermute | solution.py:441
  270.1 11.9 %collective-permute-done.44 = bf16[50,1024]{1,0:T(8,128)(2,1)S(1)} collective-permute-done((bf16[50,1024]{1,0:T(8,128)(2,1)S(1)}, bf16[50,1024]{1,0:T(8,128)(2,1)S(1)}, u32[]{:S(2)}, u32[]{:S(2)}) %collective-permute-start.44) | collective-permute-done | bytes 102432 | tf_op jit(solution)/shard_map/ppermute | solution.py:441
  283.9 7.1 %collective-permute-done.39 = bf16[2,128,1024]{2,1,0:T(8,128)(2,1)S(1)} collective-permute-done((bf16[2,128,1024]{2,1,0:T(8,128)(2,1)S(1)}, bf16[2,128,1024]{2,1,0:T(8,128)(2,1)S(1)}, u32[]{:S(2)}, u32[]{:S(2)}) %collective-permute-start.39) | collective-permute-done | bytes 524320 | tf_op jit(solution)/shard_map/ppermute | solution.py:441
  295.7 6.7 %collective-permute-done.40 = bf16[2,128,1024]{2,1,0:T(8,128)(2,1)S(1)} collective-permute-done((bf16[2,128,1024]{2,1,0:T(8,128)(2,1)}, bf16[2,128,1024]{2,1,0:T(8,128)(2,1)S(1)}, u32[]{:S(2)}, u32[]{:S(2)}) %collective-permute-start.40) | collective-permute-done | bytes 524320 | tf_op jit(solution)/shard_map/ppermute | solution.py:441
  303.9 13.9 %backward_conv.1 = bf16[4,128,1024]{2,1,0:T(8,128)(2,1)} custom-call(bf16[3,128,1024]{2,1,0:T(8,128)(2,1)} %collective-permute-done.23.before_ref, bf16[4,128,1024]{2,1,0:T(8,128)(2,1)S(1)} %bitcast.73, bf16[3,128,1024]{2,1,0:T(8,128)(2,1)} %collective-permute-done.24.after_ref, bf16[7,7,1024]{2,1,0:T(8,128)(2,1)S(1)} %copy-done.18, ...), custom_call_target="tpu_custom_call" | custom-call | flops 16099999744 | tf_op jit(solution)/shard_map/backward_conv/pallas_call | solution.py:162
  (180 shorter events, 97.6 us)
Async XLA Ops:
  4.4 17.9 %collective-permute-start.17 = (bf16[2,128,1024]{2,1,0:T(8,128)(2,1)S(1)}, bf16[2,128,1024]{2,1,0:T(8,128)(2,1)S(1)}, u32[]{:S(2)}, u32[]{:S(2)}) collective-permute-start(bf16[2,128,1024]{2,1,0:T(8,128)(2,1)S(1)} %get-tuple-element.64.refs_0_), channel_id=1, source_target_pairs={{0,2},{1,3},{4,0},{5,1},{8,4},{9,5},{12,8},{13,9},{14,12},{15,13},... | collective-permute-start | bytes 1572872 | tf_op jit(solution)/shard_map/ppermute | solution.py:441
  7.4 36.2 %collective-permute-start.1 = (bf16[3,128,1024]{2,1,0:T(8,128)(2,1)S(1)}, bf16[3,128,1024]{2,1,0:T(8,128)(2,1)S(1)}, u32[]{:S(2)}, u32[]{:S(2)}) collective-permute-start(bf16[3,128,1024]{2,1,0:T(8,128)(2,1)S(1)} %get-tuple-element.68), channel_id=1, source_target_pairs={{1,0},{2,1},{3,2},{4,3},{5,4},{6,5},{7,6},{8,7},{9,8},{10,9},{11,1... | collective-permute-start | bytes 2359304 | tf_op jit(solution)/shard_map/ppermute | solution.py:441
  8.7 34.9 %collective-permute-start = (bf16[3,128,1024]{2,1,0:T(8,128)(2,1)S(1)}, bf16[3,128,1024]{2,1,0:T(8,128)(2,1)S(1)}, u32[]{:S(2)}, u32[]{:S(2)}) collective-permute-start(bf16[3,128,1024]{2,1,0:T(8,128)(2,1)S(1)} %get-tuple-element.69), channel_id=1, source_target_pairs={{0,1},{1,2},{2,3},{3,4},{4,5},{5,6},{6,7},{7,8},{8,9},{9,10},{10,1... | collective-permute-start | bytes 2359304 | tf_op jit(solution)/shard_map/ppermute | solution.py:441
  11.8 22.1 %collective-permute-start.5 = (bf16[2,128,1024]{2,1,0:T(8,128)(2,1)S(1)}, bf16[2,128,1024]{2,1,0:T(8,128)(2,1)S(1)}, u32[]{:S(2)}, u32[]{:S(2)}) collective-permute-start(bf16[2,128,1024]{2,1,0:T(8,128)(2,1)S(1)} %get-tuple-element.64.refs_0_), channel_id=1, source_target_pairs={{0,4},{1,5},{4,8},{5,9},{8,12},{9,13},{12,14},{13,15},{14,10},{15,... | collective-permute-start | bytes 1572872 | tf_op jit(solution)/shard_map/ppermute | solution.py:441
  22.3 18.8 %collective-permute-start.18 = (bf16[2,128,1024]{2,1,0:T(8,128)(2,1)S(1)}, bf16[2,128,1024]{2,1,0:T(8,128)(2,1)S(1)}, u32[]{:S(2)}, u32[]{:S(2)}) collective-permute-start(bf16[2,128,1024]{2,1,0:T(8,128)(2,1)S(1)} %collective-permute-done.17.refs_2_), channel_id=1, source_target_pairs={{0,2},{1,3},{4,0},{5,1},{8,4},{9,5},{12,8},{13,9},{14,12},{15,13},... | collective-permute-start | bytes 1572872 | tf_op jit(solution)/shard_map/ppermute | solution.py:441
  26.1 61.9 %collective-permute-start.3 = (bf16[512,1024]{1,0:T(8,128)(2,1)}, bf16[512,1024]{1,0:T(8,128)(2,1)}, u32[]{:S(2)}, u32[]{:S(2)}) collective-permute-start(bf16[512,1024]{1,0:T(8,128)(2,1)} %bitcast.2.c_own), channel_id=1, source_target_pairs={{0,1},{1,0},{2,3},{3,2},{4,5},{5,4},{6,7},{7,6},{8,9},{9,8},{10,11... | collective-permute-start | bytes 3145736 | tf_op jit(solution)/shard_map/ppermute | solution.py:441
  33.9 36.0 %collective-permute-start.6 = (bf16[2,128,1024]{2,1,0:T(8,128)(2,1)S(1)}, bf16[2,128,1024]{2,1,0:T(8,128)(2,1)S(1)}, u32[]{:S(2)}, u32[]{:S(2)}) collective-permute-start(bf16[2,128,1024]{2,1,0:T(8,128)(2,1)S(1)} %collective-permute-done.5.refs_1_), channel_id=1, source_target_pairs={{0,4},{1,5},{4,8},{5,9},{8,12},{9,13},{12,14},{13,15},{14,10},{15,... | collective-permute-start | bytes 1572872 | tf_op jit(solution)/shard_map/ppermute | solution.py:441
  41.1 28.8 %collective-permute-start.19 = (bf16[2,128,1024]{2,1,0:T(8,128)(2,1)S(1)}, bf16[2,128,1024]{2,1,0:T(8,128)(2,1)S(1)}, u32[]{:S(2)}, u32[]{:S(2)}) collective-permute-start(bf16[2,128,1024]{2,1,0:T(8,128)(2,1)S(1)} %collective-permute-done.18.refs_4_), channel_id=1, source_target_pairs={{0,2},{1,3},{4,0},{5,1},{8,4},{9,5},{12,8},{13,9},{14,12},{15,13},... | collective-permute-start | bytes 1572872 | tf_op jit(solution)/shard_map/ppermute | solution.py:441
  62.1 25.9 %collective-permute-start.2 = (bf16[512,1024]{1,0:T(8,128)(2,1)}, bf16[512,1024]{1,0:T(8,128)(2,1)}, u32[]{:S(2)}, u32[]{:S(2)}) collective-permute-start(bf16[512,1024]{1,0:T(8,128)(2,1)} %get-tuple-element.24.n_own), channel_id=1, source_target_pairs={{0,1},{1,0},{2,3},{3,2},{4,5},{5,4},{6,7},{7,6},{8,9},{9,8},{10,11... | collective-permute-start | bytes 3145736 | tf_op jit(solution)/shard_map/ppermute | solution.py:441
  70.7 17.3 %collective-permute-start.20 = (bf16[128,1024]{1,0:T(8,128)(2,1)}, bf16[128,1024]{1,0:T(8,128)(2,1)S(1)}, u32[]{:S(2)}, u32[]{:S(2)}) collective-permute-start(bf16[128,1024]{1,0:T(8,128)(2,1)} %slice_bitcast_fusion.2), channel_id=1, source_target_pairs={{0,2},{1,3},{4,0},{5,1},{8,4},{9,5},{12,8},{13,9},{14,12},{15,13},... | collective-permute-start | bytes 786440 | tf_op jit(solution)/shard_map/ppermute | solution.py:441
  119.9 17.4 %collective-permute-start.10 = (bf16[2,128,1024]{2,1,0:T(8,128)(2,1)S(1)}, bf16[2,128,1024]{2,1,0:T(8,128)(2,1)S(1)}, u32[]{:S(2)}, u32[]{:S(2)}) collective-permute-start(bf16[2,128,1024]{2,1,0:T(8,128)(2,1)S(1)} %get-tuple-element.25.refs_0_), channel_id=1, source_target_pairs={{0,2},{1,3},{4,0},{5,1},{8,4},{9,5},{12,8},{13,9},{14,12},{15,13},... | collective-permute-start | bytes 1572872 | tf_op jit(solution)/shard_map/ppermute | solution.py:441
  122.4 16.3 %collective-permute-start.9 = (bf16[2,128,1024]{2,1,0:T(8,128)(2,1)S(1)}, bf16[2,128,1024]{2,1,0:T(8,128)(2,1)S(1)}, u32[]{:S(2)}, u32[]{:S(2)}) collective-permute-start(bf16[2,128,1024]{2,1,0:T(8,128)(2,1)S(1)} %get-tuple-element.25.refs_0_), channel_id=1, source_target_pairs={{0,4},{1,5},{4,8},{5,9},{8,12},{9,13},{12,14},{13,15},{14,10},{15,... | collective-permute-start | bytes 1572872 | tf_op jit(solution)/shard_map/ppermute | solution.py:441
  130.1 19.5 %collective-permute-start.26 = (bf16[2,128,1024]{2,1,0:T(8,128)(2,1)}, bf16[2,128,1024]{2,1,0:T(8,128)(2,1)}, u32[]{:S(2)}, u32[]{:S(2)}) collective-permute-start(bf16[2,128,1024]{2,1,0:T(8,128)(2,1)} %pad_maximum_fusion), channel_id=1, source_target_pairs={{0,4},{1,5},{4,8},{5,9},{8,12},{9,13},{12,14},{13,15},{14,10},{15,... | collective-permute-start | bytes 1572872 | tf_op jit(solution)/shard_map/ppermute | solution.py:441
  137.3 18.0 %collective-permute-start.12 = (bf16[2,128,1024]{2,1,0:T(8,128)(2,1)S(1)}, bf16[2,128,1024]{2,1,0:T(8,128)(2,1)S(1)}, u32[]{:S(2)}, u32[]{:S(2)}) collective-permute-start(bf16[2,128,1024]{2,1,0:T(8,128)(2,1)S(1)} %collective-permute-done.10.refs_2_), channel_id=1, source_target_pairs={{0,2},{1,3},{4,0},{5,1},{8,4},{9,5},{12,8},{13,9},{14,12},{15,13},... | collective-permute-start | bytes 1572872 | tf_op jit(solution)/shard_map/ppermute | solution.py:441
  138.7 22.2 %collective-permute-start.11 = (bf16[2,128,1024]{2,1,0:T(8,128)(2,1)S(1)}, bf16[2,128,1024]{2,1,0:T(8,128)(2,1)}, u32[]{:S(2)}, u32[]{:S(2)}) collective-permute-start(bf16[2,128,1024]{2,1,0:T(8,128)(2,1)S(1)} %collective-permute-done.9.refs_1_), channel_id=1, source_target_pairs={{0,4},{1,5},{4,8},{5,9},{8,12},{9,13},{12,14},{13,15},{14,10},{15,... | collective-permute-start | bytes 1572872 | tf_op jit(solution)/shard_map/ppermute | solution.py:441
  142.3 25.5 %collective-permute-start.30 = (bf16[2,128,1024]{2,1,0:T(8,128)(2,1)}, bf16[2,128,1024]{2,1,0:T(8,128)(2,1)}, u32[]{:S(2)}, u32[]{:S(2)}) collective-permute-start(bf16[2,128,1024]{2,1,0:T(8,128)(2,1)} %pad_maximum_fusion.1), channel_id=1, source_target_pairs={{0,2},{1,3},{4,0},{5,1},{8,4},{9,5},{12,8},{13,9},{14,12},{15,13},... | collective-permute-start | bytes 1572872 | tf_op jit(solution)/shard_map/ppermute | solution.py:441
  151.8 20.3 %collective-permute-start.27 = (bf16[2,128,1024]{2,1,0:T(8,128)(2,1)}, bf16[2,128,1024]{2,1,0:T(8,128)(2,1)}, u32[]{:S(2)}, u32[]{:S(2)}) collective-permute-start(bf16[2,128,1024]{2,1,0:T(8,128)(2,1)} %add_convert_fusion.10), channel_id=1, source_target_pairs={{0,4},{1,5},{4,8},{5,9},{8,12},{9,13},{12,14},{13,15},{14,10},{15,... | collective-permute-start | bytes 1572872 | tf_op jit(solution)/shard_map/ppermute | solution.py:441
  155.3 20.9 %collective-permute-start.14 = (bf16[2,128,1024]{2,1,0:T(8,128)(2,1)S(1)}, bf16[2,128,1024]{2,1,0:T(8,128)(2,1)S(1)}, u32[]{:S(2)}, u32[]{:S(2)}) collective-permute-start(bf16[2,128,1024]{2,1,0:T(8,128)(2,1)S(1)} %collective-permute-done.12.refs_4_), channel_id=1, source_target_pairs={{0,2},{1,3},{4,0},{5,1},{8,4},{9,5},{12,8},{13,9},{14,12},{15,13},... | collective-permute-start | bytes 1572872 | tf_op jit(solution)/shard_map/ppermute | solution.py:441
  160.9 20.9 %collective-permute-start.13 = (bf16[2,128,1024]{2,1,0:T(8,128)(2,1)}, bf16[2,128,1024]{2,1,0:T(8,128)(2,1)S(1)}, u32[]{:S(2)}, u32[]{:S(2)}) collective-permute-start(bf16[2,128,1024]{2,1,0:T(8,128)(2,1)} %collective-permute-done.11.refs_3_), channel_id=1, source_target_pairs={{0,4},{1,5},{4,8},{5,9},{8,12},{9,13},{12,14},{13,15},{14,10},{15,... | collective-permute-start | bytes 1572872 | tf_op jit(solution)/shard_map/ppermute | solution.py:441
  176.3 18.0 %collective-permute-start.16 = (bf16[128,1024]{1,0:T(8,128)(2,1)S(1)}, bf16[128,1024]{1,0:T(8,128)(2,1)S(1)}, u32[]{:S(2)}, u32[]{:S(2)}) collective-permute-start(bf16[128,1024]{1,0:T(8,128)(2,1)S(1)} %slice_bitcast_fusion.3), channel_id=1, source_target_pairs={{0,2},{1,3},{4,0},{5,1},{8,4},{9,5},{12,8},{13,9},{14,12},{15,13},... | collective-permute-start | bytes 786440 | tf_op jit(solution)/shard_map/ppermute | solution.py:441
  185.1 38.7 %collective-permute-start.28 = (bf16[2,128,1024]{2,1,0:T(8,128)(2,1)S(1)}, bf16[2,128,1024]{2,1,0:T(8,128)(2,1)S(1)}, u32[]{:S(2)}, u32[]{:S(2)}) collective-permute-start(bf16[2,128,1024]{2,1,0:T(8,128)(2,1)S(1)} %get-tuple-element.50), channel_id=1, source_target_pairs={{0,4},{1,5},{4,8},{5,9},{8,12},{9,13},{12,14},{13,15},{14,10},{15,... | collective-permute-start | bytes 1572872 | tf_op jit(solution)/shard_map/ppermute | solution.py:441
  188.8 35.1 %collective-permute-start.32 = (bf16[2,128,1024]{2,1,0:T(8,128)(2,1)S(1)}, bf16[2,128,1024]{2,1,0:T(8,128)(2,1)S(1)}, u32[]{:S(2)}, u32[]{:S(2)}) collective-permute-start(bf16[2,128,1024]{2,1,0:T(8,128)(2,1)S(1)} %add_convert_fusion.7), channel_id=1, source_target_pairs={{0,2},{1,3},{4,0},{5,1},{8,4},{9,5},{12,8},{13,9},{14,12},{15,13},... | collective-permute-start | bytes 1572872 | tf_op jit(solution)/shard_map/ppermute | solution.py:441
  219.5 47.9 %collective-permute-start.21 = (bf16[512,1024]{1,0:T(8,128)(2,1)S(1)}, bf16[512,1024]{1,0:T(8,128)(2,1)}, u32[]{:S(2)}, u32[]{:S(2)}) collective-permute-start(bf16[512,1024]{1,0:T(8,128)(2,1)S(1)} %get-tuple-element.31), channel_id=1, source_target_pairs={{0,1},{1,0},{2,3},{3,2},{4,5},{5,4},{6,7},{7,6},{8,9},{9,8},{10,11... | collective-permute-start | bytes 3145736 | tf_op jit(solution)/shard_map/ppermute | solution.py:441
  221.1 41.5 %collective-permute-start.38 = (bf16[2,128,1024]{2,1,0:T(8,128)(2,1)}, bf16[2,128,1024]{2,1,0:T(8,128)(2,1)}, u32[]{:S(2)}, u32[]{:S(2)}) collective-permute-start(bf16[2,128,1024]{2,1,0:T(8,128)(2,1)} %pad_maximum_fusion.3), channel_id=1, source_target_pairs={{0,2},{1,3},{4,0},{5,1},{8,4},{9,5},{12,8},{13,9},{14,12},{15,13},... | collective-permute-start | bytes 1572872 | tf_op jit(solution)/shard_map/ppermute | solution.py:441
  223.9 19.0 %collective-permute-start.34 = (bf16[2,128,1024]{2,1,0:T(8,128)(2,1)}, bf16[2,128,1024]{2,1,0:T(8,128)(2,1)}, u32[]{:S(2)}, u32[]{:S(2)}) collective-permute-start(bf16[2,128,1024]{2,1,0:T(8,128)(2,1)} %pad_maximum_fusion.2), channel_id=1, source_target_pairs={{0,4},{1,5},{4,8},{5,9},{8,12},{9,13},{12,14},{13,15},{14,10},{15,... | collective-permute-start | bytes 1572872 | tf_op jit(solution)/shard_map/ppermute | solution.py:441
  244.3 19.5 %collective-permute-start.35 = (bf16[2,128,1024]{2,1,0:T(8,128)(2,1)S(1)}, bf16[2,128,1024]{2,1,0:T(8,128)(2,1)S(1)}, u32[]{:S(2)}, u32[]{:S(2)}) collective-permute-start(bf16[2,128,1024]{2,1,0:T(8,128)(2,1)S(1)} %add_convert_fusion.5), channel_id=1, source_target_pairs={{0,4},{1,5},{4,8},{5,9},{8,12},{9,13},{12,14},{13,15},{14,10},{15,... | collective-permute-start | bytes 1572872 | tf_op jit(solution)/shard_map/ppermute | solution.py:441
  244.4 16.9 %collective-permute-start.43 = (bf16[50,1024]{1,0:T(8,128)(2,1)S(1)}, bf16[50,1024]{1,0:T(8,128)(2,1)S(1)}, u32[]{:S(2)}, u32[]{:S(2)}) collective-permute-start(bf16[50,1024]{1,0:T(8,128)(2,1)S(1)} %add_convert_fusion.13), channel_id=1, source_target_pairs={{0,2},{1,3},{2,0},{3,1},{4,6},{5,7},{6,4},{7,5},{8,10},{9,11},{10,... | collective-permute-start | bytes 307208 | tf_op jit(solution)/shard_map/ppermute | solution.py:441
  247.8 56.1 %collective-permute-start.23 = (bf16[3,128,1024]{2,1,0:T(8,128)(2,1)}, bf16[3,128,1024]{2,1,0:T(8,128)(2,1)}, u32[]{:S(2)}, u32[]{:S(2)}) collective-permute-start(bf16[3,128,1024]{2,1,0:T(8,128)(2,1)} %bitcast.11), channel_id=1, source_target_pairs={{0,1},{1,2},{2,3},{3,4},{4,5},{5,6},{6,7},{7,8},{8,9},{9,10},{10,1... | collective-permute-start | bytes 2359304 | tf_op jit(solution)/shard_map/ppermute | solution.py:441
  261.3 42.6 %collective-permute-start.24 = (bf16[3,128,1024]{2,1,0:T(8,128)(2,1)}, bf16[3,128,1024]{2,1,0:T(8,128)(2,1)}, u32[]{:S(2)}, u32[]{:S(2)}) collective-permute-start(bf16[3,128,1024]{2,1,0:T(8,128)(2,1)} %bitcast.13), channel_id=1, source_target_pairs={{1,0},{2,1},{3,2},{4,3},{5,4},{6,5},{7,6},{8,7},{9,8},{10,9},{11,1... | collective-permute-start | bytes 2359304 | tf_op jit(solution)/shard_map/ppermute | solution.py:441
  262.6 19.3 %collective-permute-start.44 = (bf16[50,1024]{1,0:T(8,128)(2,1)S(1)}, bf16[50,1024]{1,0:T(8,128)(2,1)S(1)}, u32[]{:S(2)}, u32[]{:S(2)}) collective-permute-start(bf16[50,1024]{1,0:T(8,128)(2,1)S(1)} %add_convert_fusion.12), channel_id=1, source_target_pairs={{0,4},{1,5},{2,6},{3,7},{4,0},{5,1},{6,2},{7,3},{8,12},{9,13},{10,... | collective-permute-start | bytes 307208 | tf_op jit(solution)/shard_map/ppermute | solution.py:441
  266.3 24.7 %collective-permute-start.39 = (bf16[2,128,1024]{2,1,0:T(8,128)(2,1)S(1)}, bf16[2,128,1024]{2,1,0:T(8,128)(2,1)S(1)}, u32[]{:S(2)}, u32[]{:S(2)}) collective-permute-start(bf16[2,128,1024]{2,1,0:T(8,128)(2,1)S(1)} %get-tuple-element.43), channel_id=1, source_target_pairs={{0,2},{1,3},{4,0},{5,1},{8,4},{9,5},{12,8},{13,9},{14,12},{15,13},... | collective-permute-start | bytes 1572872 | tf_op jit(solution)/shard_map/ppermute | solution.py:441
  269.0 26.7 %collective-permute-start.36 = (bf16[2,128,1024]{2,1,0:T(8,128)(2,1)}, bf16[2,128,1024]{2,1,0:T(8,128)(2,1)S(1)}, u32[]{:S(2)}, u32[]{:S(2)}) collective-permute-start(bf16[2,128,1024]{2,1,0:T(8,128)(2,1)} %get-tuple-element.42), channel_id=1, source_target_pairs={{0,4},{1,5},{4,8},{5,9},{8,12},{9,13},{12,14},{13,15},{14,10},{15,... | collective-permute-start | bytes 1572872 | tf_op jit(solution)/shard_map/ppermute | solution.py:441
  (47 other events, 447.4 us)

commit v2 on v1

v2 whole, which is shorter than its diff:
```python
import functools
import math

import jax
import jax.numpy as jnp
from jax import lax
from jax.experimental import pallas as pl
from jax.experimental.pallas import tpu as pltpu
from jax.sharding import PartitionSpec as P

F32 = jnp.float32
BF16 = jnp.bfloat16
KS = 7
RIM = KS // 2
LANES = 128
SUB = 8
MIB = 1024 * 1024
IN_VMEM = pl.BlockSpec(memory_space=pltpu.VMEM)


def cost(micros, nbytes=0):
    return pl.CostEstimate(flops=int(micros * 1.15e9), bytes_accessed=int(nbytes), transcendentals=0)


def params(mib):
    return pltpu.CompilerParams(vmem_limit_bytes=mib * MIB)


def whole(shape):
    return pl.BlockSpec(shape, lambda *_: (0,) * len(shape))


def fill_padded(before_ref, mid_ref, after_ref, pad_ref):
    lat, lon = mid_ref.shape[0], mid_ref.shape[1]
    for row in range(lat + 2 * RIM):
        if row < RIM:
            line = before_ref[row]
        elif row < RIM + lat:
            line = mid_ref[row - RIM]
        else:
            line = after_ref[row - RIM - lat]
        line = line.astype(F32)
        pad_ref[row, pl.ds(SUB, lon), :] = line
        pad_ref[row, pl.ds(0, SUB), :] = line[lon - SUB :]
        pad_ref[row, pl.ds(SUB + lon, SUB), :] = line[:SUB]


def conv_tile(pad_ref, weight_ref, start, lat, flip):
    totals = [None] * lat
    for b in range(KS):
        lines = [
            pad_ref[row, pl.ds(start + (SUB - RIM) + b, SUB), :] for row in range(lat + 2 * RIM)
        ]
        for a in range(KS):
            index = a * KS + b
            weight = weight_ref[KS * KS - 1 - index if flip else index]
            for row in range(lat):
                term = lines[row + a] * weight
                totals[row] = term if totals[row] is None else totals[row] + term
    return totals


def spread_weights(kern_ref, weight_ref):
    taps = kern_ref[...].astype(F32)
    for a in range(KS):
        for b in range(KS):
            weight_ref[a * KS + b] = jnp.broadcast_to(taps[a, b : b + 1], (SUB, LANES))


def conv_block(before_ref, mid_ref, after_ref, kern_ref, pad_ref, weight_ref, put, flip):
    lat, lon = mid_ref.shape[0], mid_ref.shape[1]
    fill_padded(before_ref, mid_ref, after_ref, pad_ref)
    spread_weights(kern_ref, weight_ref)

    def tile(t, carry):
        start = pl.multiple_of(t * SUB, SUB)
        for row, total in enumerate(conv_tile(pad_ref, weight_ref, start, lat, flip)):
            put(row, start, total)
        return carry

    lax.fori_loop(0, lon // SUB, tile, 0, unroll=8)


def forward_first_body(before_ref, mid_ref, after_ref, kern_ref, conv_ref, pad_ref, weight_ref):
    lon = mid_ref.shape[1]

    def put(row, start, total):
        conv_ref[0, pl.ds(pl.multiple_of(row * lon + start, SUB), SUB), :] = total

    conv_block(before_ref, mid_ref, after_ref, kern_ref, pad_ref, weight_ref, put, False)


def forward_last_body(
    before_ref, mid_ref, after_ref, kern_ref, gain_ref, first_ref, normed_ref, white_ref, inv_ref, pad_ref, weight_ref, conv_ref
):
    step = pl.program_id(0)
    lon = mid_ref.shape[1]
    done, blocks = first_ref.shape[0], conv_ref.shape[0]

    def put(row, start, total):
        conv_ref[step, pl.ds(pl.multiple_of(row * lon + start, SUB), SUB), :] = total

    conv_block(before_ref, mid_ref, after_ref, kern_ref, pad_ref, weight_ref, put, False)

    @pl.when(step == blocks - 1)
    def _():
        channels = (done + blocks) * LANES
        high = 32

        def norm(t, carry):
            at = pl.ds(pl.multiple_of(t * high, high), high)
            parts = [first_ref[j, at, :] for j in range(done)]
            parts += [conv_ref[j, at, :] for j in range(blocks)]
            mean = jnp.sum(functools.reduce(jnp.add, parts), axis=-1, keepdims=True) * (1.0 / channels)
            parts = [p - mean for p in parts]
            squares = functools.reduce(jnp.add, [p * p for p in parts])
            var = jnp.sum(squares, axis=-1, keepdims=True) * (1.0 / channels)
            inv = lax.rsqrt(var + 1e-06)
            inv_ref[at, :] = jnp.broadcast_to(inv, (high, LANES))
            for j, part in enumerate(parts):
                cols = slice(j * LANES, (j + 1) * LANES)
                white = part * inv
                white_ref[at, cols] = white
                normed_ref[at, cols] = (white * gain_ref[:, cols]).astype(BF16)
            return carry

        lax.fori_loop(0, conv_ref.shape[1] // high, norm, 0)


def conv_specs(lat, lon, offset):
    rows = lambda n: pl.BlockSpec((n, lon, LANES), lambda i: (0, 0, i + offset))
    return [rows(RIM), rows(lat), rows(RIM), pl.BlockSpec((KS, KS, LANES), lambda i: (0, 0, i + offset))]


def conv_scratch(lat, lon):
    return [
        pltpu.VMEM((lat + 2 * RIM, lon + 2 * SUB, LANES), F32),
        pltpu.VMEM((KS * KS, SUB, LANES), F32),
    ]


def forward_first(before, mid, after, kernel):
    lat, lon, channels = mid.shape
    tokens, blocks = lat * lon, channels // LANES // 2
    return pl.pallas_call(
        forward_first_body,
        grid=(blocks,),
        in_specs=conv_specs(lat, lon, 0),
        out_specs=pl.BlockSpec((1, tokens, LANES), lambda i: (i, 0, 0)),
        out_shape=jax.ShapeDtypeStruct((blocks, tokens, LANES), F32),
        scratch_shapes=conv_scratch(lat, lon),
        compiler_params=params(4),
        cost_estimate=cost(5),
        name="forward_first",
    )(before, mid, after, kernel)


def forward_last(before, mid, after, kernel, gain, first):
    lat, lon, channels = mid.shape
    tokens, done = lat * lon, first.shape[0]
    blocks = channels // LANES - done
    return pl.pallas_call(
        forward_last_body,
        grid=(blocks,),
        in_specs=conv_specs(lat, lon, done) + [whole((1, channels)), IN_VMEM],
        out_specs=[IN_VMEM] * 3,
        out_shape=[
            jax.ShapeDtypeStruct((tokens, channels), BF16),
            jax.ShapeDtypeStruct((tokens, channels), F32),
            jax.ShapeDtypeStruct((tokens, LANES), F32),
        ],
        scratch_shapes=conv_scratch(lat, lon) + [pltpu.VMEM((blocks, tokens, LANES), F32)],
        compiler_params=params(5),
        cost_estimate=cost(9),
        name="forward_last",
    )(before, mid, after, kernel, gain.reshape(1, channels), first)


def backward_body(before_ref, mid_ref, after_ref, kern_ref, cot_ref, *refs):
    out_ref, pad_ref, weight_ref, sum_ref = refs[-4:]
    lat = mid_ref.shape[0]

    def put(row, start, total):
        sum_ref[row, pl.ds(start, SUB), :] = total

    conv_block(before_ref, mid_ref, after_ref, kern_ref, pad_ref, weight_ref, put, True)
    for row in range(lat):
        out_ref[row] = (cot_ref[row].astype(F32) + sum_ref[row]).astype(BF16)


def backward_conv(before, mid, after, kernel, cot, earlier=None):
    lat, lon, channels = mid.shape
    blocks = channels // LANES // 2
    offset = 0 if earlier is None else blocks
    rows = pl.BlockSpec((lat, lon, LANES), lambda i: (0, 0, i + offset))
    more = () if earlier is None else (earlier,)
    return pl.pallas_call(
        backward_body,
        grid=(blocks,),
        in_specs=conv_specs(lat, lon, offset) + [rows] + [pl.BlockSpec(memory_space=pl.ANY)] * len(more),
        out_specs=rows,
        out_shape=jax.ShapeDtypeStruct((lat, lon, channels), BF16),
        scratch_shapes=conv_scratch(lat, lon) + [pltpu.VMEM((lat, lon, LANES), F32)],
        input_output_aliases={5: 0} if more else {},
        compiler_params=params(4),
        cost_estimate=cost(6),
        name="backward_conv",
    )(before, mid, after, kernel, cot, *more)


def tap_sums_body(scale, before_ref, mid_ref, after_ref, grad_ref, out_ref, pad_ref, wide_ref):
    lat, lon = mid_ref.shape[0], mid_ref.shape[1]
    fill_padded(before_ref, mid_ref, after_ref, pad_ref)
    for row in range(lat):
        wide_ref[row] = grad_ref[row].astype(F32)
    for b in range(KS):

        def tile(t, totals, b=b):
            start = pl.multiple_of(t * SUB, SUB)
            grads = [wide_ref[row, pl.ds(start, SUB), :] for row in range(lat)]
            lines = [
                pad_ref[row, pl.ds(start + (SUB - RIM) + b, SUB), :] for row in range(lat + 2 * RIM)
            ]
            return tuple(
                totals[a] + functools.reduce(jnp.add, [grads[row] * lines[row + a] for row in range(lat)])
                for a in range(KS)
            )

        zero = jnp.zeros((SUB, LANES), F32)
        totals = lax.fori_loop(0, lon // SUB, tile, (zero,) * KS, unroll=8)
        for a in range(KS):
            out_ref[a, b : b + 1, :] = jnp.sum(totals[a], axis=0, keepdims=True) * scale


def tap_sums(before, mid, after, grad, scale):
    lat, lon, channels = mid.shape
    tokens = lat * lon
    rows = lambda n: pl.BlockSpec((n, lon, LANES), lambda i: (0, 0, i))
    return pl.pallas_call(
        functools.partial(tap_sums_body, scale),
        grid=(channels // LANES,),
        in_specs=[rows(RIM), rows(lat), rows(RIM), rows(lat)],
        out_specs=pl.BlockSpec((KS, KS, LANES), lambda i: (0, 0, i)),
        out_shape=jax.ShapeDtypeStruct((KS, KS, channels), F32),
        scratch_shapes=[
            pltpu.VMEM((lat + 2 * RIM, lon + 2 * SUB, LANES), F32),
            pltpu.VMEM((lat, lon, LANES), F32),
        ],
        compiler_params=params(4),
        cost_estimate=cost(10),
        name="tap_sums",
    )(before, mid, after, grad)


HIGH = 256


def tiles(size):
    return [slice(t, t + HIGH) for t in range(0, size, HIGH)]


def hidden_body(n_blocks, chips_ref, n_own, n_sib, c_own, c_sib, *refs):
    shards, last = refs[: n_blocks - 1], refs[n_blocks - 1 : n_blocks + 1]
    hid_ref, grad_ref, win_ref, wout_ref, sems = refs[n_blocks + 1 :]
    size = last[0].shape[0]
    copies = []
    for j in range(n_blocks):
        at = pl.ds(pl.multiple_of(chips_ref[j] * size, size), size)
        for k, target in enumerate((win_ref, wout_ref)):
            source = shards[j].at[k] if j < n_blocks - 1 else last[k]
            copies.append(pltpu.make_async_copy(source, target.at[at, :], sems.at[2 * j + k]))
    for copy in copies:
        copy.start()
    for copy in copies:
        copy.wait()
    for half, (n_ref, c_ref) in enumerate(((n_own, c_own), (n_sib, c_sib))):

        def rows(t, carry, half=half, n_ref=n_ref, c_ref=c_ref):
            at = pl.ds(pl.multiple_of(t * HIGH, HIGH), HIGH)
            for cols in tiles(win_ref.shape[1]):
                pre = jnp.dot(n_ref[at, :], win_ref[:, cols], preferred_element_type=F32)
                back = jnp.dot(c_ref[at, :], wout_ref[:, cols], preferred_element_type=F32)
                area = 0.5 * (1.0 + lax.erf(pre * (1.0 / math.sqrt(2.0))))
                dens = jnp.exp(-0.5 * pre * pre) * (1.0 / math.sqrt(2.0 * math.pi))
                hid_ref[half, at, cols] = (pre * area).astype(BF16)
                grad_ref[half, at, cols] = (back * (area + pre * dens)).astype(BF16)
            return carry

        lax.fori_loop(0, n_ref.shape[0] // HIGH, rows, 0)


def hidden_step(chips, n_own, n_sib, c_own, c_sib, shards):
    tokens, channels = n_own.shape
    width = shards[-1].shape[1]
    return pl.pallas_call(
        functools.partial(hidden_body, len(shards) - 1),
        in_specs=[pl.BlockSpec(memory_space=pltpu.SMEM)]
        + [IN_VMEM] * 4
        + [pl.BlockSpec(memory_space=pltpu.HBM)] * len(shards),
        out_specs=[IN_VMEM] * 4,
        out_shape=[
            jax.ShapeDtypeStruct((2, tokens, width), BF16),
            jax.ShapeDtypeStruct((2, tokens, width), BF16),
            jax.ShapeDtypeStruct((channels, width), BF16),
            jax.ShapeDtypeStruct((channels, width), BF16),
        ],
        scratch_shapes=[pltpu.SemaphoreType.DMA((2 * len(shards),))],
        compiler_params=params(8),
        cost_estimate=cost(17),
        name="hidden_step",
    )(chips, n_own, n_sib, c_own, c_sib, *shards)


def arrange_body(size, chips_ref, *refs):
    count = len(refs) // 2
    for source, target in zip(refs[:count], refs[count:]):
        for j in range(source.shape[1] // size):
            at = pl.ds(pl.multiple_of(chips_ref[j] * size, size), size)
            target[:, j * size : (j + 1) * size] = source[:, at]


def arrange(chips, size, values):
    if size % LANES:
        return [
            jnp.concatenate(
                [
                    lax.dynamic_slice_in_dim(v, chips[j] * size, size, axis=1)
                    for j in range(v.shape[1] // size)
                ],
                axis=1,
            )
            for v in values
        ]
    return pl.pallas_call(
        functools.partial(arrange_body, size),
        in_specs=[pl.BlockSpec(memory_space=pltpu.SMEM)] + [IN_VMEM] * len(values),
        out_specs=[IN_VMEM] * len(values),
        out_shape=[jax.ShapeDtypeStruct(v.shape, v.dtype) for v in values],
        compiler_params=params(4),
        cost_estimate=cost(2),
        name="arrange",
    )(chips, *values)


def weight_grad_body(scale, rows, n_own, n_sib, c_own, c_sib, hid_ref, grad_ref, out_ref):
    contract = (((0,), (0,)), ((), ()))
    for which, (own, sib, rhs) in enumerate(((n_own, n_sib, grad_ref), (c_own, c_sib, hid_ref))):
        for t in range(0, rows[1], LANES):
            size = min(LANES, rows[1] - t)
            at = slice(rows[0] + t, rows[0] + t + size)
            total = lax.dot_general(own[:, at], rhs[0], contract, preferred_element_type=F32)
            total = total + lax.dot_general(sib[:, at], rhs[1], contract, preferred_element_type=F32)
            out_ref[which, t : t + size, :] = (total * scale).astype(BF16)


def weight_grads(n_own, n_sib, c_own, c_sib, hid, grad, scale, rows):
    width = hid.shape[2]
    return pl.pallas_call(
        functools.partial(weight_grad_body, scale, rows),
        in_specs=[IN_VMEM] * 6,
        out_specs=IN_VMEM,
        out_shape=jax.ShapeDtypeStruct((2, rows[1], width), BF16),
        compiler_params=params(12),
        cost_estimate=cost(13 * rows[1] / n_own.shape[1]),
        name="weight_grads",
    )(n_own, n_sib, c_own, c_sib, hid, grad)


def spread_body(lhs_ref, w_ref, own_ref, sib_ref):
    contract = (((1,), (1,)), ((), ()))
    for half, out_ref in enumerate((own_ref, sib_ref)):
        for at in tiles(lhs_ref.shape[1]):
            total = lax.dot_general(lhs_ref[half, at, :], w_ref[...], contract, preferred_element_type=F32)
            out_ref[at, :] = total.astype(out_ref.dtype)


def spread(lhs, weight):
    _, tokens, width = lhs.shape
    channels = weight.shape[0]
    return pl.pallas_call(
        spread_body,
        in_specs=[IN_VMEM] * 2,
        out_specs=[IN_VMEM] * 2,
        out_shape=[
            jax.ShapeDtypeStruct((tokens, channels), F32),
            jax.ShapeDtypeStruct((tokens, channels), BF16),
        ],
        compiler_params=params(8),
        cost_estimate=cost(4.7),
        name="spread",
    )(lhs, weight)


def norm_back_body(scale, own_ref, sib_ref, white_ref, inv_ref, gain_ref, out_ref, gsum_ref):
    channels = own_ref.shape[1]
    blocks = channels // LANES
    high = 16

    def tile(t, sums):
        at = pl.ds(pl.multiple_of(t * high, high), high)
        inv = inv_ref[at, :]
        terms, whites, new = [], [], []
        for j in range(blocks):
            cols = slice(j * LANES, (j + 1) * LANES)
            grad = own_ref[at, cols] + sib_ref[at, cols].astype(F32)
            white = white_ref[at, cols]
            new.append(sums[j] + jnp.sum((grad * white).reshape(high // SUB, SUB, LANES), axis=0))
            terms.append(grad * gain_ref[:, cols])
            whites.append(white)
        mean = jnp.sum(functools.reduce(jnp.add, terms), axis=-1, keepdims=True) * (1.0 / channels)
        cross = functools.reduce(jnp.add, [g * w for g, w in zip(terms, whites)])
        cross = jnp.sum(cross, axis=-1, keepdims=True) * (1.0 / channels)
        for j in range(blocks):
            cols = slice(j * LANES, (j + 1) * LANES)
            out_ref[at, cols] = (inv * (terms[j] - mean - whites[j] * cross)).astype(BF16)
        return tuple(new)

    zero = jnp.zeros((SUB, LANES), F32)
    sums = lax.fori_loop(0, own_ref.shape[0] // high, tile, (zero,) * blocks)
    for j in range(blocks):
        gsum_ref[:, j * LANES : (j + 1) * LANES] = jnp.sum(sums[j], axis=0, keepdims=True) * scale


def norm_back(own, sib, white, inv, gain, scale):
    tokens, channels = own.shape
    return pl.pallas_call(
        functools.partial(norm_back_body, scale),
        in_specs=[pl.BlockSpec(memory_space=pltpu.VMEM)] * 5,
        out_specs=[pl.BlockSpec(memory_space=pltpu.VMEM)] * 2,
        out_shape=[
            jax.ShapeDtypeStruct((tokens, channels), BF16),
            jax.ShapeDtypeStruct((1, channels), F32),
        ],
        compiler_params=params(4),
        cost_estimate=cost(3.5),
        name="norm_back",
    )(own, sib, white, inv, gain.reshape(1, channels))


def ring_order(stations):
    if stations == 8:
        return [0, 2, 4, 6, 7, 5, 3, 1]
    return list(range(stations))


def added(a, b):
    return (a.astype(F32) + b.astype(F32)).astype(BF16)


def on_device(fields, kernel, norm_gain, proj_in, proj_out, cotangent):
    lat, lon, channels = fields.shape
    row_devs = lax.axis_size("row")
    stations = row_devs // 2
    half = stations // 2
    scale = 1.0 / math.sqrt(lat * row_devs * lon)
    me = lax.axis_index("row")
    core, chip = me % 2, me // 2
    order = ring_order(stations)
    place = [order.index(i) for i in range(stations)]
    slots = [0] + [d for r in range(1, half) for d in (-r, r)] + [half]
    table = [[order[(place[p] + d) % stations] for d in slots] for p in range(stations)]
    chips = lax.dynamic_index_in_dim(jnp.array(table, jnp.int32), chip, 0, keepdims=False)
    leaving = [half] + [d for r in range(half - 1, 0, -1) for d in (r, -r)] + [0]
    table = [[order[(place[p] + d) % stations] for d in leaving] for p in range(stations)]
    leave = lax.dynamic_index_in_dim(jnp.array(table, jnp.int32), chip, 0, keepdims=False)

    swap = [(i, i ^ 1) for i in range(row_devs)]
    up = [(i, i + 1) for i in range(row_devs - 1)]
    down = [(i + 1, i) for i in range(row_devs - 1)]
    send = lambda value, pairs: lax.ppermute(value, "row", pairs)

    def rims_sent(value):
        last, first = value[lat - RIM :], value[:RIM]
        if stations != 8:
            return send(last, up), send(first, down)
        above = send(last, [p for p in up if p != (11, 12)])
        below = send(first, [p for p in down if p != (4, 3)])
        return above, below, send(jnp.where(core == 0, first, last), [(11, 9), (4, 6)])

    def rims_passed(rims):
        return (*rims[:2], *(send(r, [(9, 12), (6, 3)]) for r in rims[2:]))

    def rims_got(rims):
        if stations != 8:
            return rims
        above, below, far = rims
        return jnp.where(me == 12, far, above), jnp.where(me == 3, far, below)

    def ring(step):
        return [
            (order[i] * 2 + c, order[(i + step) % stations] * 2 + c)
            for i in range(stations)
            for c in range(2)
        ]

    onward, backward = ring(1), ring(-1)

    hid = proj_in.shape[1]
    mine = hid // 2
    size = channels // stations

    weights = jnp.stack([proj_in, proj_out.T])
    kept = lax.dynamic_slice_in_dim(weights, core * mine, mine, axis=2)
    given = lax.dynamic_slice_in_dim(weights, (1 - core) * mine, mine, axis=2)
    got = send(given, swap)
    shard = jnp.where(
        core == 0, jnp.concatenate([kept, got], axis=1), jnp.concatenate([got, kept], axis=1)
    )

    fence = lax.optimization_barrier

    class Gather:
        def __init__(self, part):
            self.found, self.left = [part], half
            self.pair = part, part

        def step(self):
            self.left -= 1
            on, back = self.pair
            if not self.left:
                on, back = on[0], back[1]
            self.pair = send(on, onward), send(back, backward)
            return self.pair

        def arrived(self, pair):
            self.pair = pair
            self.found += pair

    class Scatter:
        def __init__(self):
            self.d = half
            self.blocks = {}
            self.pair = None

        def step(self):
            d = self.d
            self.d = d - 1
            if d == half:
                on, back = self.blocks[d][0], self.blocks[d][1]
            else:
                on, back = self.blocks[d], self.blocks[-d]
                if d == half - 1:
                    on = jnp.stack([added(on[0], self.pair[0]), on[1]])
                    back, come, on = fence((back, self.pair[1], on))
                    back = jnp.stack([back[0], added(back[1], come)])
                else:
                    on = added(on, self.pair[0])
                    back, come, on = fence((back, self.pair[1], on))
                    back = added(back, come)
            self.pair = send(on, onward), send(back, backward)
            return self.pair

        def arrived(self, pair):
            self.pair = pair

        def total(self):
            total = self.blocks[0].astype(F32) + self.pair[0].astype(F32) + self.pair[1].astype(F32)
            return total.astype(BF16)

    def joined(value, bit):
        low = value.astype(BF16)
        return low, send(low, [(i, i ^ bit) for i in range(row_devs)])

    def summed(pair):
        return pair[0].astype(F32) + pair[1].astype(F32)

    c_own = cotangent.reshape(-1, channels)
    load, sums = Gather(shard), Scatter()
    pairs = load.step()
    rims = rims_sent(fields)
    c_sib = send(c_own, swap)
    pairs = fence(pairs)
    load.arrived(pairs)
    pairs = load.step()
    pairs, rims, c_sib = fence((pairs, rims_passed(rims), c_sib))
    load.arrived(pairs)
    for _ in range(half - 4):
        load.arrived(fence(load.step()))
    pairs = load.step()
    before, after = rims_got(rims)
    conv = forward_first(before, fields, after, kernel)
    n_own, white, inv = forward_last(before, fields, after, kernel, norm_gain, conv)
    pairs, n_own = fence((pairs, n_own))
    load.arrived(pairs)
    pairs = load.step()
    n_sib = send(n_own, swap)
    order_in = arrange(leave, size, (n_own, n_sib, c_own, c_sib))
    pairs, order_in, n_sib = fence((pairs, order_in, n_sib))
    load.arrived(pairs)
    hidden, pre_grad, w_in, w_out = hidden_step(
        chips, n_own, n_sib, c_own, c_sib, load.found
    )
    early = 3 * size

    def keep(part, names):
        for k, d in enumerate(names):
            sums.blocks[d] = part[:, k * size : (k + 1) * size]

    parts = weight_grads(*order_in, hidden, pre_grad, scale, (0, early))
    parts, hidden, pre_grad, order_in = fence((parts, hidden, pre_grad, order_in))
    keep(parts, leaving[:3])
    pairs = sums.step()
    parts = weight_grads(*order_in, hidden, pre_grad, scale, (early, channels - early))
    pre_grad, parts = fence((pre_grad, parts))
    ngrad = spread(pre_grad, w_in)
    pairs, parts, hidden, ngrad = fence((pairs, parts, hidden, ngrad))
    keep(parts, leaving[3:])
    sums.arrived(pairs)
    pairs = sums.step()
    ng_sib = send(ngrad[1], swap)
    branch = spread(hidden, w_out)
    ng_sib, branch = fence((ng_sib, branch))
    conv_grad, gain_local = norm_back(ngrad[0], ng_sib, white, inv, norm_gain, scale)
    conv_grad = fence(conv_grad).reshape(lat, lon, channels)
    rims = send(conv_grad[lat - RIM :], up), send(conv_grad[:RIM], down)
    taps_local = tap_sums(before, fields, after, conv_grad, scale)
    pairs, rims, taps_local, branch = fence((pairs, rims, taps_local, branch))
    sums.arrived(pairs)
    for _ in range(half - 4):
        sums.arrived(fence(sums.step()))
    pairs = sums.step()
    small = joined(jnp.concatenate([taps_local.reshape(KS * KS, channels), gain_local], axis=0), 4)
    rims, small = fence((rims, small))
    g_before, g_after = rims
    small = joined(summed(small), 8)
    fields_grad = backward_conv(g_before, conv_grad, g_after, kernel, cotangent)
    fields_grad = backward_conv(g_before, conv_grad, g_after, kernel, cotangent, fields_grad)
    br_sib = send(branch[1], swap)
    pairs, fields_grad, br_sib, small = fence((pairs, fields_grad, br_sib, small))
    sums.arrived(pairs)
    pairs = sums.step()
    small = joined(summed(small), 2)
    result = (
        fields.astype(F32) + (branch[0] + br_sib.astype(F32)).reshape(fields.shape)
    ).astype(BF16)
    small, pairs, result = fence((small, pairs, result))
    sums.arrived(pairs)
    for bit in [1 << k for k in range(4, row_devs.bit_length() - 1)] + [1]:
        small = joined(summed(small), bit)
    small = summed(small)
    kernel_grad = small[: KS * KS].reshape(KS, KS, channels)
    gain_grad = small[KS * KS]

    share = sums.total()
    rows = size // 2
    stay = lax.dynamic_slice_in_dim(share, core * rows, rows, axis=1)
    give = lax.dynamic_slice_in_dim(share, (1 - core) * rows, rows, axis=1)
    got = send(give, swap)
    final = jnp.where(
        core == 0, jnp.concatenate([stay, got], axis=2), jnp.concatenate([got, stay], axis=2)
    )
    return (result, fields_grad, final[0], final[1].T, kernel_grad, gain_grad)


def solution(mesh):
    in_specs = (
        P(("grp", "row"), None, None),
        P(None, None, "grp"),
        P("grp"),
        P(("grp", "row"), None),
        P("grp", "row"),
        P(("grp", "row"), None, None),
    )
    out_specs = (
        P(("grp", "row"), None, None),
        P(("grp", "row"), None, None),
        P(("grp", "row"), None),
        P("grp", "row"),
        P(None, None, "grp"),
        P("grp"),
    )
    return jax.shard_map(
        on_device, mesh=mesh, in_specs=in_specs, out_specs=out_specs, check_vma=False
    )
```

time: 320 us -> 263 us (0.82)
  Pallas kernels: 93.5 us -> 73.7 us
  starting transfers between devices: 67.8 us -> 51 us
  other arithmetic: 22.8 us -> 17.2 us
  between operations: 6.49 us -> 1.21 us
  waiting for transfers between devices: 108 us -> 103 us
  local copies, waits for them, and re-layouts: 20.1 us -> 16.9 us
    ppermute x46 -> x32, starting transfers between devices: 67.8 us -> 51 us  [on_device(): send = lambda value, pairs: lax.ppermute(value, 'row', pairs)]
    pallas_call x10, Pallas kernels: 75.9 us -> 60.7 us  [the longest x1 16.2 us: hidden_step(): pl.pallas_call(functools.partial(hidden_body, len(shards) - 1), in_specs=...]
    ppermute x46 -> x32, waiting for transfers between devices: 108 us -> 103 us  [on_device(): send = lambda value, pairs: lax.ppermute(value, 'row', pairs)]
    another operation x8 -> x6, other arithmetic: 5.45 us -> 0.47 us  [the longest x2 0.23 us: step(): back = jnp.stack([back[0], added(back[1], come)])]
    pallas_call x1, Pallas kernels: 14.1 us -> 9.44 us  [tap_sums(): pl.pallas_call(functools.partial(tap_sums_body, scale), grid=(channels //...]
    unnamed x66 -> x62, local copies, waits for them, and re-layouts: 13.1 us -> 9.24 us
    convert_element_type x6 -> x4, other arithmetic: 9.95 us -> 6.69 us  [added(): return (a.astype(F32) + b.astype(F32)).astype(BF16)]
  transfers between devices with their start and end apart: 46 -> 32, of which waited for: 19 -> 12; matrix products, arithmetic and copies ran while one was open for 8% -> 6% of each run, Pallas kernels for 24% -> 21%
where the time goes in v2:
time: 263 us
  waiting for transfers between devices  103 us (39%)
  Pallas kernels  73.7 us (28%)
  starting transfers between devices  51 us (19%)
  other arithmetic  17.2 us (7%)
  local copies, waits for them, and re-layouts  16.9 us (6%)
    ppermute x32, waiting for transfers between devices, on_device(): send = lambda value, pairs: lax.ppermute(value, 'row', pairs)  103 us
    ppermute x32, starting transfers between devices, on_device(): send = lambda value, pairs: lax.ppermute(value, 'row', pairs)  51 us
    pallas_call x1, Pallas kernels, hidden_step(): pl.pallas_call(functools.partial(hidden_body, len(shards) - 1), in_specs=...  16.2 us
    pallas_call x2, Pallas kernels, backward_conv(): pl.pallas_call(backward_body, grid=(blocks,), in_specs=conv_specs(lat, lo...  10.4 us
    pallas_call x1, Pallas kernels, tap_sums(): pl.pallas_call(functools.partial(tap_sums_body, scale), grid=(channels //...  9.44 us
    unnamed x62, local copies, waits for them, and re-layouts  9.24 us
    pallas_call x2, Pallas kernels, weight_grads(): pl.pallas_call(functools.partial(weight_grad_body, scale, rows), in_specs...  9.09 us
    pallas_call x2, Pallas kernels, spread(): pl.pallas_call(spread_body, in_specs=[IN_VMEM] * 2, out_specs=[IN_VMEM] *...  9.04 us
  transfers between devices with their start and end apart: 32, of which 12 were waited for; matrix products, arithmetic and copies ran while one was open for 6% of the time, Pallas kernels for 21%

profile of v2, /device:TPU:0, one launch (start us, length us, event | category | flops | bytes accessed | tf_op | source)
XLA Modules:
  0.0 262.6 jit_solution(712569789873876005)
XLA Ops:
  4.3 2.9 %collective-permute-start.2 = (bf16[2,128,2048]{2,1,0:T(8,128)(2,1)S(1)}, bf16[2,128,2048]{2,1,0:T(8,128)(2,1)}, u32[]{:S(2)}, u32[]{:S(2)}) collective-permute-start(bf16[2,128,2048]{2,1,0:T(8,128)(2,1)S(1)} %maximum_select_fusion.refs_0_), channel_id=1, source_target_pairs={{0,2},{1,3},{4,0},{5,1},{8,4},{9,5},{12,8},{13,9},{14,12},{15,13},... | collective-permute-start | bytes 3145736 | tf_op jit(solution)/shard_map/ppermute | solution.py:470
  12.6 18.3 %collective-permute-done.2.refs_2_ = bf16[2,128,2048]{2,1,0:T(8,128)(2,1)} collective-permute-done((bf16[2,128,2048]{2,1,0:T(8,128)(2,1)S(1)}, bf16[2,128,2048]{2,1,0:T(8,128)(2,1)}, u32[]{:S(2)}, u32[]{:S(2)}) %collective-permute-start.2) | collective-permute-done | bytes 1048608 | tf_op jit(solution)/shard_map/ppermute | solution.py:470
  34.3 2.3 collective-permute-start.5
  38.3 24.9 %collective-permute-done.3.refs_3_ = bf16[2,128,2048]{2,1,0:T(8,128)(2,1)} collective-permute-done((bf16[2,128,2048]{2,1,0:T(8,128)(2,1)}, bf16[2,128,2048]{2,1,0:T(8,128)(2,1)}, u32[]{:S(2)}, u32[]{:S(2)}) %collective-permute-start.3) | collective-permute-done | bytes 1048608 | tf_op jit(solution)/shard_map/ppermute | solution.py:470
  63.2 4.7 %collective-permute-start.10 = (bf16[2,128,2048]{2,1,0:T(8,128)(2,1)}, bf16[2,128,2048]{2,1,0:T(8,128)(2,1)S(1)}, u32[]{:S(2)}, u32[]{:S(2)}) collective-permute-start(bf16[2,128,2048]{2,1,0:T(8,128)(2,1)} %collective-permute-done.3.refs_3_), channel_id=1, source_target_pairs={{0,4},{1,5},{4,8},{5,9},{8,12},{9,13},{12,14},{13,15},{14,10},{15,... | collective-permute-start | bytes 3145736 | tf_op jit(solution)/shard_map/ppermute | solution.py:470
  69.7 4.4 %forward_first.1.first_ref = f32[4,512,128]{2,1,0:T(8,128)S(1)} custom-call(bf16[3,128,1024]{2,1,0:T(8,128)(2,1)S(1)} %get-tuple-element.191.before_ref, bf16[4,128,1024]{2,1,0:T(8,128)(2,1)S(1)} %copy-done, bf16[3,128,1024]{2,1,0:T(8,128)(2,1)S(1)} %get-tuple-element.190.after_ref, bf16[7,7,1024]{2,1,0:T(8,128)(2,1)S(1)} %copy-done.20), custom_call_target="tpu_custom_call" | custom-call | flops 5750000128 | tf_op jit(solution)/shard_map/forward_first/pallas_call | solution.py:145
  74.1 8.5 %forward_last.1 = (bf16[512,1024]{1,0:T(8,128)(2,1)}, f32[512,1024]{1,0:T(8,128)S(1)}, f32[512,128]{1,0:T(8,128)S(1)}) custom-call(bf16[3,128,1024]{2,1,0:T(8,128)(2,1)S(1)} %get-tuple-element.191.before_ref, bf16[4,128,1024]{2,1,0:T(8,128)(2,1)S(1)} %copy-done, bf16[3,128,1024]{2,1,0:T(8,128)(2,1)S(1)} %get-tuple-element.190.after_ref, ...), custom_call_target="tpu_custom_call" | custom-call | flops 10350000128 | tf_op jit(solution)/shard_map/forward_last/pallas_call | solution.py:162
  84.6 5.7 %collective-permute-done.10.refs_5_ = bf16[2,128,2048]{2,1,0:T(8,128)(2,1)S(1)} collective-permute-done((bf16[2,128,2048]{2,1,0:T(8,128)(2,1)}, bf16[2,128,2048]{2,1,0:T(8,128)(2,1)S(1)}, u32[]{:S(2)}, u32[]{:S(2)}) %collective-permute-start.10) | collective-permute-done | bytes 1048608 | tf_op jit(solution)/shard_map/ppermute | solution.py:470
  93.3 1.8 collective-permute-start.13
  98.1 3.0 %arrange.1 = (bf16[512,1024]{1,0:T(8,128)(2,1)S(1)}, bf16[512,1024]{1,0:T(8,128)(2,1)S(1)}, bf16[512,1024]{1,0:T(8,128)(2,1)S(1)}, bf16[512,1024]{1,0:T(8,128)(2,1)S(1)}) custom-call(s32[8]{0:T(128)S(1)} %fusion.6.chips_ref, bf16[512,1024]{1,0:T(8,128)(2,1)} %get-tuple-element.100.refs_0_.n_own, bf16[512,1024]{1,0:T(8,128)(2,1)} %collective-permute-done.14.refs_1_.n_sib, ...), custom_call_target="tpu_custom_call" | custom-call | flops 2300000000 | tf_op jit(solution)/shard_map/arrange/pallas_call | solution.py:334
  101.1 6.4 %collective-permute-done.13.refs_8_ = bf16[128,2048]{1,0:T(8,128)(2,1)S(1)} collective-permute-done((bf16[128,2048]{1,0:T(8,128)(2,1)}, bf16[128,2048]{1,0:T(8,128)(2,1)S(1)}, u32[]{:S(2)}, u32[]{:S(2)}) %collective-permute-start.13) | collective-permute-done | bytes 524320 | tf_op jit(solution)/shard_map/ppermute | solution.py:470
  109.2 16.2 %hidden_step.1 = (bf16[2,512,2048]{2,1,0:T(8,128)(2,1)S(1)}, bf16[2,512,2048]{2,1,0:T(8,128)(2,1)S(1)}, bf16[1024,2048]{1,0:T(8,128)(2,1)S(1)}, bf16[1024,2048]{1,0:T(8,128)(2,1)S(1)}) custom-call(s32[8]{0:T(128)S(1)} %fusion.7.chips_ref, bf16[512,1024]{1,0:T(8,128)(2,1)} %get-tuple-element.100.refs_0_.n_own, ...), custom_call_target="tpu_custom_call" | custom-call | flops 19549999104 | tf_op jit(solution)/shard_map/hidden_step/pallas_call | solution.py:295
  125.4 3.5 %weight_grads.2 = bf16[2,384,2048]{2,1,0:T(8,128)(2,1)S(1)} custom-call(bf16[512,1024]{1,0:T(8,128)(2,1)S(1)} %get-tuple-element.117.n_own, bf16[512,1024]{1,0:T(8,128)(2,1)S(1)} %get-tuple-element.118.n_sib, bf16[512,1024]{1,0:T(8,128)(2,1)S(1)} %get-tuple-element.119.c_own, bf16[512,1024]{1,0:T(8,128)(2,1)S(1)} %get-tuple-element.120.c_sib, ...), custom_call_target="tpu_custom_call" | custom-call | flops 5606249984 | tf_op jit(solution)/shard_map/weight_grads/pallas_call | solution.py:358
  129.0 1.7 collective-permute-start.16
  131.1 5.6 %weight_grads.3 = bf16[2,640,2048]{2,1,0:T(8,128)(2,1)S(1)} custom-call(bf16[512,1024]{1,0:T(8,128)(2,1)S(1)} %get-tuple-element.117.n_own, bf16[512,1024]{1,0:T(8,128)(2,1)S(1)} %get-tuple-element.118.n_sib, bf16[512,1024]{1,0:T(8,128)(2,1)S(1)} %get-tuple-element.119.c_own, bf16[512,1024]{1,0:T(8,128)(2,1)S(1)} %get-tuple-element.120.c_sib, ...), custom_call_target="tpu_custom_call" | custom-call | flops 9343750144 | tf_op jit(solution)/shard_map/weight_grads/pallas_call | solution.py:358
  136.8 4.5 %spread.2 = (f32[512,1024]{1,0:T(8,128)S(1)}, bf16[512,1024]{1,0:T(8,128)(2,1)S(1)}) custom-call(bf16[2,512,2048]{2,1,0:T(8,128)(2,1)S(1)} %get-tuple-element.123.grad_ref.lhs_ref, bf16[1024,2048]{1,0:T(8,128)(2,1)S(1)} %get-tuple-element.124.w_ref), custom_call_target="tpu_custom_call" | custom-call | flops 5405000192 | tf_op jit(solution)/shard_map/spread/pallas_call | solution.py:380
  146.0 4.5 %spread.3 = (f32[512,1024]{1,0:T(8,128)S(1)}, bf16[512,1024]{1,0:T(8,128)(2,1)S(1)}) custom-call(bf16[2,512,2048]{2,1,0:T(8,128)(2,1)S(1)} %get-tuple-element.135.hid_ref.lhs_ref, bf16[1024,2048]{1,0:T(8,128)(2,1)S(1)} %get-tuple-element.136.w_ref), custom_call_target="tpu_custom_call" | custom-call | flops 5405000192 | tf_op jit(solution)/shard_map/spread/pallas_call | solution.py:380
  154.7 3.5 %norm_back.1 = (bf16[512,1024]{1,0:T(8,128)(2,1)S(1)}, f32[1,1024]{1,0:T(1,128)S(1)}) custom-call(f32[512,1024]{1,0:T(8,128)S(1)} %get-tuple-element.133.own_ref, bf16[512,1024]{1,0:T(8,128)(2,1)S(1)} %collective-permute-done.19.sib_ref, f32[512,1024]{1,0:T(8,128)S(1)} %copy-done.23, f32[512,128]{1,0:T(8,128)S(1)} %copy-done.25, f32[1,1024]{1,0:T(1,128)S(1)} %bitcast.47), custom_call_target="tpu_custom_call" | custom-call | flops 4024999936 | tf_op jit(solution)/shard_map/norm_back/pallas_call | solution.py:426
  158.4 2.0 collective-permute-start.20
  161.7 9.4 %tap_sums.1 = f32[7,7,1024]{2,1,0:T(8,128)S(1)} custom-call(bf16[3,128,1024]{2,1,0:T(8,128)(2,1)S(1)} %copy-done.5, bf16[4,128,1024]{2,1,0:T(8,128)(2,1)S(1)} %copy-done, bf16[3,128,1024]{2,1,0:T(8,128)(2,1)S(1)} %get-tuple-element.190.after_ref, bf16[4,128,1024]{2,1,0:T(8,128)(2,1)S(1)} %bitcast.40), custom_call_target="tpu_custom_call" | custom-call | flops 11500000256 | tf_op jit(solution)/shard_map/tap_sums/pallas_call | solution.py:239
  173.5 7.6 %collective-permute-start.24 = (bf16[50,1024]{1,0:T(8,128)(2,1)S(1)}, bf16[50,1024]{1,0:T(8,128)(2,1)S(1)}, u32[]{:S(2)}, u32[]{:S(2)}) collective-permute-start(bf16[50,1024]{1,0:T(8,128)(2,1)S(1)} %pad_maximum_fusion.2), channel_id=1, source_target_pairs={{0,4},{1,5},{2,6},{3,7},{4,0},{5,1},{6,2},{7,3},{8,12},{9,13},{10,... | collective-permute-start | bytes 307208 | tf_op jit(solution)/shard_map/ppermute | solution.py:470
  181.0 1.9 add_convert_fusion.5
  183.0 6.1 %collective-permute-start.25 = (bf16[512,1024]{1,0:T(8,128)(2,1)S(1)}, bf16[512,1024]{1,0:T(8,128)(2,1)S(1)}, u32[]{:S(2)}, u32[]{:S(2)}) collective-permute-start(bf16[512,1024]{1,0:T(8,128)(2,1)S(1)} %copy-done.15), channel_id=1, source_target_pairs={{0,1},{1,0},{2,3},{3,2},{4,5},{5,4},{6,7},{7,6},{8,9},{9,8},{10,11... | collective-permute-start | bytes 3145736 | tf_op jit(solution)/shard_map/ppermute | solution.py:470
  189.5 2.4 collective-permute-start.23
  193.1 5.2 %backward_conv.2.refs_0_ = bf16[4,128,1024]{2,1,0:T(8,128)(2,1)} custom-call(bf16[3,128,1024]{2,1,0:T(8,128)(2,1)S(1)} %copy-done.17, bf16[4,128,1024]{2,1,0:T(8,128)(2,1)S(1)} %bitcast.41, bf16[3,128,1024]{2,1,0:T(8,128)(2,1)S(1)} %copy-done.19, bf16[7,7,1024]{2,1,0:T(8,128)(2,1)S(1)} %copy-done.20, bf16[4,128,1024]{2,1,0:T(8,128)(2,1)S(1)} %copy-done.13), custom_call_target="tpu_custom_call" | custom-call | flops 6899999744 | tf_op jit(solution)/shard_map/backward_conv/pallas_call | solution.py:197
  198.3 5.2 %backward_conv.3 = bf16[4,128,1024]{2,1,0:T(8,128)(2,1)} custom-call(bf16[3,128,1024]{2,1,0:T(8,128)(2,1)S(1)} %copy-done.17, bf16[4,128,1024]{2,1,0:T(8,128)(2,1)S(1)} %bitcast.42, bf16[3,128,1024]{2,1,0:T(8,128)(2,1)S(1)} %copy-done.19, bf16[7,7,1024]{2,1,0:T(8,128)(2,1)S(1)} %copy-done.20, ...), custom_call_target="tpu_custom_call", output_to_operand_aliasing={{}: (5, {})} | custom-call | flops 6899999744 | tf_op jit(solution)/shard_map/backward_conv/pallas_call | solution.py:197
  203.5 17.1 %collective-permute-done.26 = bf16[50,1024]{1,0:T(8,128)(2,1)S(1)} collective-permute-done((bf16[50,1024]{1,0:T(8,128)(2,1)S(1)}, bf16[50,1024]{1,0:T(8,128)(2,1)S(1)}, u32[]{:S(2)}, u32[]{:S(2)}) %collective-permute-start.26) | collective-permute-done | bytes 102432 | tf_op jit(solution)/shard_map/ppermute | solution.py:470
  220.6 3.0 %add_convert_fusion.3 = bf16[2,128,2048]{2,1,0:T(8,128)(2,1)} fusion(bf16[2,128,2048]{2,1,0:T(8,128)(2,1)S(1)} %collective-permute-done.22, bf16[2,640,2048]{2,1,0:T(8,128)(2,1)} %copy-done.1), kind=kLoop, calls=%fused_computation.4 | loop fusion | flops 2097152 | bytes 3145728 | tf_op jit(solution)/shard_map/convert_element_type | solution.py:447
  225.0 3.2 %collective-permute-start.29 = (bf16[2,128,2048]{2,1,0:T(8,128)(2,1)}, bf16[2,128,2048]{2,1,0:T(8,128)(2,1)}, u32[]{:S(2)}, u32[]{:S(2)}) collective-permute-start(bf16[2,128,2048]{2,1,0:T(8,128)(2,1)} %add_convert_fusion.2), channel_id=1, source_target_pairs={{0,2},{1,3},{4,0},{5,1},{8,4},{9,5},{12,8},{13,9},{14,12},{15,13},... | collective-permute-start | bytes 3145736 | tf_op jit(solution)/shard_map/ppermute | solution.py:470
  228.3 2.1 collective-permute-start.27
  233.2 22.1 %collective-permute-done.27 = bf16[50,1024]{1,0:T(8,128)(2,1)S(1)} collective-permute-done((bf16[50,1024]{1,0:T(8,128)(2,1)S(1)}, bf16[50,1024]{1,0:T(8,128)(2,1)S(1)}, u32[]{:S(2)}, u32[]{:S(2)}) %collective-permute-start.27) | collective-permute-done | bytes 102432 | tf_op jit(solution)/shard_map/ppermute | solution.py:470
  255.4 2.4 add_convert_fusion
  (143 shorter events, 49.0 us)
Async XLA Ops:
  2.0 2.1 collective-permute-start
  4.3 26.6 %collective-permute-start.2 = (bf16[2,128,2048]{2,1,0:T(8,128)(2,1)S(1)}, bf16[2,128,2048]{2,1,0:T(8,128)(2,1)}, u32[]{:S(2)}, u32[]{:S(2)}) collective-permute-start(bf16[2,128,2048]{2,1,0:T(8,128)(2,1)S(1)} %maximum_select_fusion.refs_0_), channel_id=1, source_target_pairs={{0,2},{1,3},{4,0},{5,1},{8,4},{9,5},{12,8},{13,9},{14,12},{15,13},... | collective-permute-start | bytes 3145736 | tf_op jit(solution)/shard_map/ppermute | solution.py:470
  7.3 25.0 %collective-permute-start.1 = (bf16[2,128,2048]{2,1,0:T(8,128)(2,1)S(1)}, bf16[2,128,2048]{2,1,0:T(8,128)(2,1)}, u32[]{:S(2)}, u32[]{:S(2)}) collective-permute-start(bf16[2,128,2048]{2,1,0:T(8,128)(2,1)S(1)} %maximum_select_fusion.refs_0_), channel_id=1, source_target_pairs={{0,4},{1,5},{4,8},{5,9},{8,12},{9,13},{12,14},{13,15},{14,10},{15,... | collective-permute-start | bytes 3145736 | tf_op jit(solution)/shard_map/ppermute | solution.py:470
  8.4 25.9 %collective-permute-start.7 = (bf16[3,128,1024]{2,1,0:T(8,128)(2,1)S(1)}, bf16[3,128,1024]{2,1,0:T(8,128)(2,1)}, u32[]{:S(2)}, u32[]{:S(2)}) collective-permute-start(bf16[3,128,1024]{2,1,0:T(8,128)(2,1)S(1)} %get-tuple-element.185), channel_id=1, source_target_pairs={{11,9},{4,6},{27,25},{20,22}} | collective-permute-start | bytes 2359304 | tf_op jit(solution)/shard_map/ppermute | solution.py:470
  10.1 26.5 %collective-permute-start.6 = (bf16[3,128,1024]{2,1,0:T(8,128)(2,1)S(1)}, bf16[3,128,1024]{2,1,0:T(8,128)(2,1)}, u32[]{:S(2)}, u32[]{:S(2)}) collective-permute-start(bf16[3,128,1024]{2,1,0:T(8,128)(2,1)S(1)} %get-tuple-element.186), channel_id=1, source_target_pairs={{1,0},{2,1},{3,2},{5,4},{6,5},{7,6},{8,7},{9,8},{10,9},{11,10},{12... | collective-permute-start | bytes 2359304 | tf_op jit(solution)/shard_map/ppermute | solution.py:470
  11.4 26.8 %collective-permute-start.9 = (bf16[512,1024]{1,0:T(8,128)(2,1)S(1)}, bf16[512,1024]{1,0:T(8,128)(2,1)}, u32[]{:S(2)}, u32[]{:S(2)}) collective-permute-start(bf16[512,1024]{1,0:T(8,128)(2,1)S(1)} %bitcast.43), channel_id=1, source_target_pairs={{0,1},{1,0},{2,3},{3,2},{4,5},{5,4},{6,7},{7,6},{8,9},{9,8},{10,11... | collective-permute-start | bytes 3145736 | tf_op jit(solution)/shard_map/ppermute | solution.py:470
  32.3 30.9 %collective-permute-start.3 = (bf16[2,128,2048]{2,1,0:T(8,128)(2,1)}, bf16[2,128,2048]{2,1,0:T(8,128)(2,1)}, u32[]{:S(2)}, u32[]{:S(2)}) collective-permute-start(bf16[2,128,2048]{2,1,0:T(8,128)(2,1)} %collective-permute-done.1.refs_1_), channel_id=1, source_target_pairs={{0,4},{1,5},{4,8},{5,9},{8,12},{9,13},{12,14},{13,15},{14,10},{15,... | collective-permute-start | bytes 3145736 | tf_op jit(solution)/shard_map/ppermute | solution.py:470
  32.7 30.5 %collective-permute-start.4 = (bf16[2,128,2048]{2,1,0:T(8,128)(2,1)}, bf16[2,128,2048]{2,1,0:T(8,128)(2,1)}, u32[]{:S(2)}, u32[]{:S(2)}) collective-permute-start(bf16[2,128,2048]{2,1,0:T(8,128)(2,1)} %collective-permute-done.2.refs_2_), channel_id=1, source_target_pairs={{0,2},{1,3},{4,0},{5,1},{8,4},{9,5},{12,8},{13,9},{14,12},{15,13},... | collective-permute-start | bytes 3145736 | tf_op jit(solution)/shard_map/ppermute | solution.py:470
  34.3 3.9 %collective-permute-start.5 = (bf16[3,128,1024]{2,1,0:T(8,128)(2,1)}, bf16[3,128,1024]{2,1,0:T(8,128)(2,1)}, u32[]{:S(2)}, u32[]{:S(2)}) collective-permute-start(bf16[3,128,1024]{2,1,0:T(8,128)(2,1)} %get-tuple-element.187), channel_id=1, source_target_pairs={{0,1},{1,2},{2,3},{3,4},{4,5},{5,6},{6,7},{7,8},{8,9},{9,10},{10,1... | collective-permute-start | bytes 2359304 | tf_op jit(solution)/shard_map/ppermute | solution.py:470
  36.6 1.7 collective-permute-start.8
  63.2 27.1 %collective-permute-start.10 = (bf16[2,128,2048]{2,1,0:T(8,128)(2,1)}, bf16[2,128,2048]{2,1,0:T(8,128)(2,1)S(1)}, u32[]{:S(2)}, u32[]{:S(2)}) collective-permute-start(bf16[2,128,2048]{2,1,0:T(8,128)(2,1)} %collective-permute-done.3.refs_3_), channel_id=1, source_target_pairs={{0,4},{1,5},{4,8},{5,9},{8,12},{9,13},{12,14},{13,15},{14,10},{15,... | collective-permute-start | bytes 3145736 | tf_op jit(solution)/shard_map/ppermute | solution.py:470
  67.9 22.4 %collective-permute-start.11 = (bf16[2,128,2048]{2,1,0:T(8,128)(2,1)}, bf16[2,128,2048]{2,1,0:T(8,128)(2,1)S(1)}, u32[]{:S(2)}, u32[]{:S(2)}) collective-permute-start(bf16[2,128,2048]{2,1,0:T(8,128)(2,1)} %collective-permute-done.4.refs_4_), channel_id=1, source_target_pairs={{0,2},{1,3},{4,0},{5,1},{8,4},{9,5},{12,8},{13,9},{14,12},{15,13},... | collective-permute-start | bytes 3145736 | tf_op jit(solution)/shard_map/ppermute | solution.py:470
  90.3 6.4 %collective-permute-start.14 = (bf16[512,1024]{1,0:T(8,128)(2,1)}, bf16[512,1024]{1,0:T(8,128)(2,1)}, u32[]{:S(2)}, u32[]{:S(2)}) collective-permute-start(bf16[512,1024]{1,0:T(8,128)(2,1)} %get-tuple-element.100.refs_0_.n_own), channel_id=1, source_target_pairs={{0,1},{1,0},{2,3},{3,2},{4,5},{5,4},{6,7},{7,6},{8,9},{9,8},{10,11... | collective-permute-start | bytes 3145736 | tf_op jit(solution)/shard_map/ppermute | solution.py:470
  93.3 14.2 %collective-permute-start.13 = (bf16[128,2048]{1,0:T(8,128)(2,1)}, bf16[128,2048]{1,0:T(8,128)(2,1)S(1)}, u32[]{:S(2)}, u32[]{:S(2)}) collective-permute-start(bf16[128,2048]{1,0:T(8,128)(2,1)} %slice_bitcast_fusion.4), channel_id=1, source_target_pairs={{0,2},{1,3},{4,0},{5,1},{8,4},{9,5},{12,8},{13,9},{14,12},{15,13},... | collective-permute-start | bytes 1572872 | tf_op jit(solution)/shard_map/ppermute | solution.py:470
  95.1 14.0 %collective-permute-start.12 = (bf16[128,2048]{1,0:T(8,128)(2,1)}, bf16[128,2048]{1,0:T(8,128)(2,1)}, u32[]{:S(2)}, u32[]{:S(2)}) collective-permute-start(bf16[128,2048]{1,0:T(8,128)(2,1)} %slice_bitcast_fusion.5), channel_id=1, source_target_pairs={{0,4},{1,5},{4,8},{5,9},{8,12},{9,13},{12,14},{13,15},{14,10},{15,... | collective-permute-start | bytes 1572872 | tf_op jit(solution)/shard_map/ppermute | solution.py:470
  129.0 12.9 %collective-permute-start.16 = (bf16[128,2048]{1,0:T(8,128)(2,1)S(1)}, bf16[128,2048]{1,0:T(8,128)(2,1)S(1)}, u32[]{:S(2)}, u32[]{:S(2)}) collective-permute-start(bf16[128,2048]{1,0:T(8,128)(2,1)S(1)} %get-tuple-element.177), channel_id=1, source_target_pairs={{0,2},{1,3},{4,0},{5,1},{8,4},{9,5},{12,8},{13,9},{14,12},{15,13},... | collective-permute-start | bytes 1572872 | tf_op jit(solution)/shard_map/ppermute | solution.py:470
  130.8 12.6 %collective-permute-start.15 = (bf16[128,2048]{1,0:T(8,128)(2,1)S(1)}, bf16[128,2048]{1,0:T(8,128)(2,1)S(1)}, u32[]{:S(2)}, u32[]{:S(2)}) collective-permute-start(bf16[128,2048]{1,0:T(8,128)(2,1)S(1)} %get-tuple-element.178), channel_id=1, source_target_pairs={{0,4},{1,5},{4,8},{5,9},{8,12},{9,13},{12,14},{13,15},{14,10},{15,... | collective-permute-start | bytes 1572872 | tf_op jit(solution)/shard_map/ppermute | solution.py:470
  143.8 9.8 %collective-permute-start.19 = (bf16[512,1024]{1,0:T(8,128)(2,1)S(1)}, bf16[512,1024]{1,0:T(8,128)(2,1)S(1)}, u32[]{:S(2)}, u32[]{:S(2)}) collective-permute-start(bf16[512,1024]{1,0:T(8,128)(2,1)S(1)} %get-tuple-element.134), channel_id=1, source_target_pairs={{0,1},{1,0},{2,3},{3,2},{4,5},{5,4},{6,7},{7,6},{8,9},{9,8},{10,11... | collective-permute-start | bytes 3145736 | tf_op jit(solution)/shard_map/ppermute | solution.py:470
  143.9 27.3 %collective-permute-start.18 = (bf16[2,128,2048]{2,1,0:T(8,128)(2,1)S(1)}, bf16[2,128,2048]{2,1,0:T(8,128)(2,1)S(1)}, u32[]{:S(2)}, u32[]{:S(2)}) collective-permute-start(bf16[2,128,2048]{2,1,0:T(8,128)(2,1)S(1)} %pad_maximum_fusion.1), channel_id=1, source_target_pairs={{0,2},{1,3},{4,0},{5,1},{8,4},{9,5},{12,8},{13,9},{14,12},{15,13},... | collective-permute-start | bytes 3145736 | tf_op jit(solution)/shard_map/ppermute | solution.py:470
  144.9 26.3 %collective-permute-start.17 = (bf16[2,128,2048]{2,1,0:T(8,128)(2,1)S(1)}, bf16[2,128,2048]{2,1,0:T(8,128)(2,1)}, u32[]{:S(2)}, u32[]{:S(2)}) collective-permute-start(bf16[2,128,2048]{2,1,0:T(8,128)(2,1)S(1)} %pad_maximum_fusion), channel_id=1, source_target_pairs={{0,4},{1,5},{4,8},{5,9},{8,12},{9,13},{12,14},{13,15},{14,10},{15,... | collective-permute-start | bytes 3145736 | tf_op jit(solution)/shard_map/ppermute | solution.py:470
  158.4 12.8 %collective-permute-start.20 = (bf16[3,128,1024]{2,1,0:T(8,128)(2,1)S(1)}, bf16[3,128,1024]{2,1,0:T(8,128)(2,1)S(1)}, u32[]{:S(2)}, u32[]{:S(2)}) collective-permute-start(bf16[3,128,1024]{2,1,0:T(8,128)(2,1)S(1)} %bitcast.51), channel_id=1, source_target_pairs={{0,1},{1,2},{2,3},{3,4},{4,5},{5,6},{6,7},{7,8},{8,9},{9,10},{10,1... | collective-permute-start | bytes 2359304 | tf_op jit(solution)/shard_map/ppermute | solution.py:470
  160.4 11.7 %collective-permute-start.21 = (bf16[3,128,1024]{2,1,0:T(8,128)(2,1)S(1)}, bf16[3,128,1024]{2,1,0:T(8,128)(2,1)S(1)}, u32[]{:S(2)}, u32[]{:S(2)}) collective-permute-start(bf16[3,128,1024]{2,1,0:T(8,128)(2,1)S(1)} %bitcast.50), channel_id=1, source_target_pairs={{1,0},{2,1},{3,2},{4,3},{5,4},{6,5},{7,6},{8,7},{9,8},{10,9},{11,1... | collective-permute-start | bytes 2359304 | tf_op jit(solution)/shard_map/ppermute | solution.py:470
  173.5 18.5 %collective-permute-start.24 = (bf16[50,1024]{1,0:T(8,128)(2,1)S(1)}, bf16[50,1024]{1,0:T(8,128)(2,1)S(1)}, u32[]{:S(2)}, u32[]{:S(2)}) collective-permute-start(bf16[50,1024]{1,0:T(8,128)(2,1)S(1)} %pad_maximum_fusion.2), channel_id=1, source_target_pairs={{0,4},{1,5},{2,6},{3,7},{4,0},{5,1},{6,2},{7,3},{8,12},{9,13},{10,... | collective-permute-start | bytes 307208 | tf_op jit(solution)/shard_map/ppermute | solution.py:470
  183.0 37.6 %collective-permute-start.25 = (bf16[512,1024]{1,0:T(8,128)(2,1)S(1)}, bf16[512,1024]{1,0:T(8,128)(2,1)S(1)}, u32[]{:S(2)}, u32[]{:S(2)}) collective-permute-start(bf16[512,1024]{1,0:T(8,128)(2,1)S(1)} %copy-done.15), channel_id=1, source_target_pairs={{0,1},{1,0},{2,3},{3,2},{4,5},{5,4},{6,7},{7,6},{8,9},{9,8},{10,11... | collective-permute-start | bytes 3145736 | tf_op jit(solution)/shard_map/ppermute | solution.py:470
  189.5 31.1 %collective-permute-start.23 = (bf16[2,128,2048]{2,1,0:T(8,128)(2,1)S(1)}, bf16[2,128,2048]{2,1,0:T(8,128)(2,1)S(1)}, u32[]{:S(2)}, u32[]{:S(2)}) collective-permute-start(bf16[2,128,2048]{2,1,0:T(8,128)(2,1)S(1)} %add_convert_fusion.4), channel_id=1, source_target_pairs={{0,2},{1,3},{4,0},{5,1},{8,4},{9,5},{12,8},{13,9},{14,12},{15,13},... | collective-permute-start | bytes 3145736 | tf_op jit(solution)/shard_map/ppermute | solution.py:470
  192.0 28.7 %collective-permute-start.22 = (bf16[2,128,2048]{2,1,0:T(8,128)(2,1)S(1)}, bf16[2,128,2048]{2,1,0:T(8,128)(2,1)S(1)}, u32[]{:S(2)}, u32[]{:S(2)}) collective-permute-start(bf16[2,128,2048]{2,1,0:T(8,128)(2,1)S(1)} %add_convert_fusion.5), channel_id=1, source_target_pairs={{0,4},{1,5},{4,8},{5,9},{8,12},{9,13},{12,14},{13,15},{14,10},{15,... | collective-permute-start | bytes 3145736 | tf_op jit(solution)/shard_map/ppermute | solution.py:470
  192.0 28.6 %collective-permute-start.26 = (bf16[50,1024]{1,0:T(8,128)(2,1)S(1)}, bf16[50,1024]{1,0:T(8,128)(2,1)S(1)}, u32[]{:S(2)}, u32[]{:S(2)}) collective-permute-start(bf16[50,1024]{1,0:T(8,128)(2,1)S(1)} %add_convert_fusion.8), channel_id=1, source_target_pairs={{0,8},{1,9},{2,10},{3,11},{4,12},{5,13},{6,14},{7,15},{8,0},{9,1},... | collective-permute-start | bytes 307208 | tf_op jit(solution)/shard_map/ppermute | solution.py:470
  225.0 30.3 %collective-permute-start.29 = (bf16[2,128,2048]{2,1,0:T(8,128)(2,1)}, bf16[2,128,2048]{2,1,0:T(8,128)(2,1)}, u32[]{:S(2)}, u32[]{:S(2)}) collective-permute-start(bf16[2,128,2048]{2,1,0:T(8,128)(2,1)} %add_convert_fusion.2), channel_id=1, source_target_pairs={{0,2},{1,3},{4,0},{5,1},{8,4},{9,5},{12,8},{13,9},{14,12},{15,13},... | collective-permute-start | bytes 3145736 | tf_op jit(solution)/shard_map/ppermute | solution.py:470
  228.2 27.2 %collective-permute-start.28 = (bf16[2,128,2048]{2,1,0:T(8,128)(2,1)}, bf16[2,128,2048]{2,1,0:T(8,128)(2,1)}, u32[]{:S(2)}, u32[]{:S(2)}) collective-permute-start(bf16[2,128,2048]{2,1,0:T(8,128)(2,1)} %add_convert_fusion.3), channel_id=1, source_target_pairs={{0,4},{1,5},{4,8},{5,9},{8,12},{9,13},{12,14},{13,15},{14,10},{15,... | collective-permute-start | bytes 3145736 | tf_op jit(solution)/shard_map/ppermute | solution.py:470
  228.3 27.1 %collective-permute-start.27 = (bf16[50,1024]{1,0:T(8,128)(2,1)S(1)}, bf16[50,1024]{1,0:T(8,128)(2,1)S(1)}, u32[]{:S(2)}, u32[]{:S(2)}) collective-permute-start(bf16[50,1024]{1,0:T(8,128)(2,1)S(1)} %add_convert_fusion.7), channel_id=1, source_target_pairs={{0,2},{1,3},{2,0},{3,1},{4,6},{5,7},{6,4},{7,5},{8,10},{9,11},{10,... | collective-permute-start | bytes 307208 | tf_op jit(solution)/shard_map/ppermute | solution.py:470
  257.8 3.5 %collective-permute-start.30 = (bf16[2,64,2048]{2,1,0:T(8,128)(2,1)S(1)}, bf16[2,64,2048]{2,1,0:T(8,128)(2,1)S(1)}, u32[]{:S(2)}, u32[]{:S(2)}) collective-permute-start(bf16[2,64,2048]{2,1,0:T(8,128)(2,1)S(1)} %get-tuple-element.182), channel_id=1, source_target_pairs={{0,1},{1,0},{2,3},{3,2},{4,5},{5,4},{6,7},{7,6},{8,9},{9,8},{10,11... | collective-permute-start | bytes 1572872 | tf_op jit(solution)/shard_map/ppermute | solution.py:470
  258.0 2.0 collective-permute-start.31
  (31 other events, 258.9 us)

commit v3 on v2

--- a/solution.py
+++ b/solution.py
@@ -342,26 +342,26 @@
     )(chips, *values)
 
 
-def weight_grad_body(scale, rows, n_own, n_sib, c_own, c_sib, hid_ref, grad_ref, out_ref):
+def weight_grad_body(scale, size, first, n_own, n_sib, c_own, c_sib, hid_ref, grad_ref, *outs):
     contract = (((0,), (0,)), ((), ()))
-    for which, (own, sib, rhs) in enumerate(((n_own, n_sib, grad_ref), (c_own, c_sib, hid_ref))):
-        for t in range(0, rows[1], LANES):
-            size = min(LANES, rows[1] - t)
-            at = slice(rows[0] + t, rows[0] + t + size)
+    for k, out_ref in enumerate(outs):
+        at = slice((first + k) * size, (first + k + 1) * size)
+        for which, (own, sib, rhs) in enumerate(((n_own, n_sib, grad_ref), (c_own, c_sib, hid_ref))):
             total = lax.dot_general(own[:, at], rhs[0], contract, preferred_element_type=F32)
             total = total + lax.dot_general(sib[:, at], rhs[1], contract, preferred_element_type=F32)
-            out_ref[which, t : t + size, :] = (total * scale).astype(BF16)
-
-
-def weight_grads(n_own, n_sib, c_own, c_sib, hid, grad, scale, rows):
+            out_ref[which] = (total * scale).astype(BF16)
+
+
+def weight_grads(n_own, n_sib, c_own, c_sib, hid, grad, scale, size, first, count):
     width = hid.shape[2]
-    return pl.pallas_call(
-        functools.partial(weight_grad_body, scale, rows),
+    shape = jax.ShapeDtypeStruct((2, size, width), BF16)
+    return pl.pallas_call(
+        functools.partial(weight_grad_body, scale, size, first),
         in_specs=[IN_VMEM] * 6,
-        out_specs=IN_VMEM,
-        out_shape=jax.ShapeDtypeStruct((2, rows[1], width), BF16),
+        out_specs=[IN_VMEM] * count,
+        out_shape=[shape] * count,
         compiler_params=params(12),
-        cost_estimate=cost(13 * rows[1] / n_own.shape[1]),
+        cost_estimate=cost(9 * size * count / n_own.shape[1]),
         name="weight_grads",
     )(n_own, n_sib, c_own, c_sib, hid, grad)
 
@@ -590,21 +590,20 @@
     hidden, pre_grad, w_in, w_out = hidden_step(
         chips, n_own, n_sib, c_own, c_sib, load.found
     )
-    early = 3 * size
-
-    def keep(part, names):
-        for k, d in enumerate(names):
-            sums.blocks[d] = part[:, k * size : (k + 1) * size]
-
-    parts = weight_grads(*order_in, hidden, pre_grad, scale, (0, early))
-    parts, hidden, pre_grad, order_in = fence((parts, hidden, pre_grad, order_in))
-    keep(parts, leaving[:3])
+    early = 3
+
+    def keep(blocks, names):
+        sums.blocks.update(zip(names, blocks))
+
+    blocks = weight_grads(*order_in, hidden, pre_grad, scale, size, 0, early)
+    blocks, hidden, pre_grad, order_in = fence((blocks, hidden, pre_grad, order_in))
+    keep(blocks, leaving[:early])
     pairs = sums.step()
-    parts = weight_grads(*order_in, hidden, pre_grad, scale, (early, channels - early))
-    pre_grad, parts = fence((pre_grad, parts))
+    blocks = weight_grads(*order_in, hidden, pre_grad, scale, size, early, stations - early)
+    pre_grad, blocks = fence((pre_grad, blocks))
     ngrad = spread(pre_grad, w_in)
-    pairs, parts, hidden, ngrad = fence((pairs, parts, hidden, ngrad))
-    keep(parts, leaving[3:])
+    pairs, blocks, hidden, ngrad = fence((pairs, blocks, hidden, ngrad))
+    keep(blocks, leaving[early:])
     sums.arrived(pairs)
     pairs = sums.step()
     ng_sib = send(ngrad[1], swap)

time: 263 us -> 255 us (0.970)
  local copies, waits for them, and re-layouts: 16.9 us -> 10.6 us
    unnamed x62 -> x66, local copies, waits for them, and re-layouts: 9.24 us -> 4.65 us
  transfers between devices with their start and end apart: 32 -> 32, of which waited for: 12 -> 14; matrix products, arithmetic and copies ran while one was open for 6% -> 5% of each run, Pallas kernels for 21% -> 21%
where the time goes in v3:
time: 255 us; the launch traced here: 254 us
  waiting for transfers between devices  101 us (40%)
  Pallas kernels  74.3 us (29%)
  starting transfers between devices  50.5 us (20%)
  other arithmetic  16.4 us (6%)
  local copies, waits for them, and re-layouts  10.6 us (4%)
    ppermute x32, waiting for transfers between devices, on_device(): send = lambda value, pairs: lax.ppermute(value, 'row', pairs)  101 us
    ppermute x32, starting transfers between devices, on_device(): send = lambda value, pairs: lax.ppermute(value, 'row', pairs)  50.5 us
    pallas_call x1, Pallas kernels, hidden_step(): pl.pallas_call(functools.partial(hidden_body, len(shards) - 1), in_specs=...  16.8 us
    pallas_call x2, Pallas kernels, backward_conv(): pl.pallas_call(backward_body, grid=(blocks,), in_specs=conv_specs(lat, lo...  10.4 us
    pallas_call x1, Pallas kernels, tap_sums(): pl.pallas_call(functools.partial(tap_sums_body, scale), grid=(channels //...  9.44 us
    pallas_call x2, Pallas kernels, weight_grads(): pl.pallas_call(functools.partial(weight_grad_body, scale, size, first), i...  9.15 us
    pallas_call x2, Pallas kernels, spread(): pl.pallas_call(spread_body, in_specs=[IN_VMEM] * 2, out_specs=[IN_VMEM] *...  9.08 us
    pallas_call x1, Pallas kernels, forward_last(): pl.pallas_call(forward_last_body, grid=(blocks,), in_specs=conv_specs(lat...  8.48 us
  transfers between devices with their start and end apart: 32, of which 14 were waited for; matrix products, arithmetic and copies ran while one was open for 5% of the time, Pallas kernels for 21%

profile of v3, /device:TPU:0, one launch (start us, length us, event | category | flops | bytes accessed | tf_op | source)
XLA Modules:
  0.0 254.3 jit_solution(12118614652003195007)
XLA Ops:
  4.3 2.9 %collective-permute-start.2 = (bf16[2,128,2048]{2,1,0:T(8,128)(2,1)S(1)}, bf16[2,128,2048]{2,1,0:T(8,128)(2,1)}, u32[]{:S(2)}, u32[]{:S(2)}) collective-permute-start(bf16[2,128,2048]{2,1,0:T(8,128)(2,1)S(1)} %maximum_select_fusion.refs_0_), channel_id=1, source_target_pairs={{0,2},{1,3},{4,0},{5,1},{8,4},{9,5},{12,8},{13,9},{14,12},{15,13},... | collective-permute-start | bytes 3145736 | tf_op jit(solution)/shard_map/ppermute | solution.py:470
  8.4 1.7 collective-permute-start.7
  12.6 18.3 %collective-permute-done.2.refs_2_ = bf16[2,128,2048]{2,1,0:T(8,128)(2,1)} collective-permute-done((bf16[2,128,2048]{2,1,0:T(8,128)(2,1)S(1)}, bf16[2,128,2048]{2,1,0:T(8,128)(2,1)}, u32[]{:S(2)}, u32[]{:S(2)}) %collective-permute-start.2) | collective-permute-done | bytes 1048608 | tf_op jit(solution)/shard_map/ppermute | solution.py:470
  34.3 2.2 collective-permute-start.5
  36.5 1.6 collective-permute-start.8
  38.2 25.0 %collective-permute-done.3.refs_3_ = bf16[2,128,2048]{2,1,0:T(8,128)(2,1)} collective-permute-done((bf16[2,128,2048]{2,1,0:T(8,128)(2,1)}, bf16[2,128,2048]{2,1,0:T(8,128)(2,1)}, u32[]{:S(2)}, u32[]{:S(2)}) %collective-permute-start.3) | collective-permute-done | bytes 1048608 | tf_op jit(solution)/shard_map/ppermute | solution.py:470
  63.2 4.7 %collective-permute-start.10 = (bf16[2,128,2048]{2,1,0:T(8,128)(2,1)}, bf16[2,128,2048]{2,1,0:T(8,128)(2,1)S(1)}, u32[]{:S(2)}, u32[]{:S(2)}) collective-permute-start(bf16[2,128,2048]{2,1,0:T(8,128)(2,1)} %collective-permute-done.3.refs_3_), channel_id=1, source_target_pairs={{0,4},{1,5},{4,8},{5,9},{8,12},{9,13},{12,14},{13,15},{14,10},{15,... | collective-permute-start | bytes 3145736 | tf_op jit(solution)/shard_map/ppermute | solution.py:470
  67.9 1.7 broadcast_select_fusion
  69.7 4.4 %forward_first.1.first_ref = f32[4,512,128]{2,1,0:T(8,128)S(1)} custom-call(bf16[3,128,1024]{2,1,0:T(8,128)(2,1)S(1)} %get-tuple-element.224.before_ref, bf16[4,128,1024]{2,1,0:T(8,128)(2,1)S(1)} %copy-done, bf16[3,128,1024]{2,1,0:T(8,128)(2,1)S(1)} %get-tuple-element.223.after_ref, bf16[7,7,1024]{2,1,0:T(8,128)(2,1)S(1)} %copy-done.24), custom_call_target="tpu_custom_call" | custom-call | flops 5750000128 | tf_op jit(solution)/shard_map/forward_first/pallas_call | solution.py:145
  74.1 8.5 %forward_last.1 = (bf16[512,1024]{1,0:T(8,128)(2,1)}, f32[512,1024]{1,0:T(8,128)S(1)}, f32[512,128]{1,0:T(8,128)S(1)}) custom-call(bf16[3,128,1024]{2,1,0:T(8,128)(2,1)S(1)} %get-tuple-element.224.before_ref, bf16[4,128,1024]{2,1,0:T(8,128)(2,1)S(1)} %copy-done, bf16[3,128,1024]{2,1,0:T(8,128)(2,1)S(1)} %get-tuple-element.223.after_ref, ...), custom_call_target="tpu_custom_call" | custom-call | flops 10350000128 | tf_op jit(solution)/shard_map/forward_last/pallas_call | solution.py:162
  84.0 6.3 %collective-permute-done.10.refs_5_ = bf16[2,128,2048]{2,1,0:T(8,128)(2,1)S(1)} collective-permute-done((bf16[2,128,2048]{2,1,0:T(8,128)(2,1)}, bf16[2,128,2048]{2,1,0:T(8,128)(2,1)S(1)}, u32[]{:S(2)}, u32[]{:S(2)}) %collective-permute-start.10) | collective-permute-done | bytes 1048608 | tf_op jit(solution)/shard_map/ppermute | solution.py:470
  92.3 1.8 collective-permute-start.13
  97.0 3.0 %arrange.1 = (bf16[512,1024]{1,0:T(8,128)(2,1)S(1)}, bf16[512,1024]{1,0:T(8,128)(2,1)S(1)}, bf16[512,1024]{1,0:T(8,128)(2,1)S(1)}, bf16[512,1024]{1,0:T(8,128)(2,1)S(1)}) custom-call(s32[8]{0:T(128)S(1)} %fusion.6.chips_ref, bf16[512,1024]{1,0:T(8,128)(2,1)} %get-tuple-element.118.refs_0_.n_own, bf16[512,1024]{1,0:T(8,128)(2,1)} %collective-permute-done.14.refs_1_.n_sib, ...), custom_call_target="tpu_custom_call" | custom-call | flops 2300000000 | tf_op jit(solution)/shard_map/arrange/pallas_call | solution.py:334
  100.1 6.6 %collective-permute-done.13.refs_8_ = bf16[128,2048]{1,0:T(8,128)(2,1)} collective-permute-done((bf16[128,2048]{1,0:T(8,128)(2,1)}, bf16[128,2048]{1,0:T(8,128)(2,1)}, u32[]{:S(2)}, u32[]{:S(2)}) %collective-permute-start.13) | collective-permute-done | bytes 524320 | tf_op jit(solution)/shard_map/ppermute | solution.py:470
  108.2 16.8 %hidden_step.1 = (bf16[2,512,2048]{2,1,0:T(8,128)(2,1)S(1)}, bf16[2,512,2048]{2,1,0:T(8,128)(2,1)S(1)}, bf16[1024,2048]{1,0:T(8,128)(2,1)S(1)}, bf16[1024,2048]{1,0:T(8,128)(2,1)S(1)}) custom-call(s32[8]{0:T(128)S(1)} %fusion.7.chips_ref, bf16[512,1024]{1,0:T(8,128)(2,1)} %get-tuple-element.118.refs_0_.n_own, ...), custom_call_target="tpu_custom_call" | custom-call | flops 19549999104 | tf_op jit(solution)/shard_map/hidden_step/pallas_call | solution.py:295
  125.0 3.5 %weight_grads.2 = (bf16[2,128,2048]{2,1,0:T(8,128)(2,1)S(1)}, bf16[2,128,2048]{2,1,0:T(8,128)(2,1)S(1)}, bf16[2,128,2048]{2,1,0:T(8,128)(2,1)S(1)}) custom-call(bf16[512,1024]{1,0:T(8,128)(2,1)S(1)} %get-tuple-element.138.n_own, bf16[512,1024]{1,0:T(8,128)(2,1)S(1)} %get-tuple-element.139.n_sib, bf16[512,1024]{1,0:T(8,128)(2,1)S(1)} %get-tuple-element.140.c_own, ...), custom_call_target="tpu_custom_call" | custom-call | flops 3881250048 | tf_op jit(solution)/shard_map/weight_grads/pallas_call | solution.py:358
  128.6 1.7 collective-permute-start.16
  130.7 5.7 %weight_grads.3 = (bf16[2,128,2048]{2,1,0:T(8,128)(2,1)S(1)}, bf16[2,128,2048]{2,1,0:T(8,128)(2,1)S(1)}, bf16[2,128,2048]{2,1,0:T(8,128)(2,1)S(1)}, bf16[2,128,2...) custom-call(bf16[512,1024]{1,0:T(8,128)(2,1)S(1)} %get-tuple-element.138.n_own, ...), custom_call_target="tpu_custom_call" | custom-call | flops 6468749824 | tf_op jit(solution)/shard_map/weight_grads/pallas_call | solution.py:358
  136.4 4.5 %spread.2 = (f32[512,1024]{1,0:T(8,128)S(1)}, bf16[512,1024]{1,0:T(8,128)(2,1)S(1)}) custom-call(bf16[2,512,2048]{2,1,0:T(8,128)(2,1)S(1)} %get-tuple-element.153.grad_ref.lhs_ref, bf16[1024,2048]{1,0:T(8,128)(2,1)S(1)} %get-tuple-element.154.w_ref), custom_call_target="tpu_custom_call" | custom-call | flops 5405000192 | tf_op jit(solution)/shard_map/spread/pallas_call | solution.py:380
  145.6 4.5 %spread.3 = (f32[512,1024]{1,0:T(8,128)S(1)}, bf16[512,1024]{1,0:T(8,128)(2,1)S(1)}) custom-call(bf16[2,512,2048]{2,1,0:T(8,128)(2,1)S(1)} %get-tuple-element.167.hid_ref.lhs_ref, bf16[1024,2048]{1,0:T(8,128)(2,1)S(1)} %get-tuple-element.168.w_ref), custom_call_target="tpu_custom_call" | custom-call | flops 5405000192 | tf_op jit(solution)/shard_map/spread/pallas_call | solution.py:380
  151.2 3.5 %norm_back.1 = (bf16[512,1024]{1,0:T(8,128)(2,1)S(1)}, f32[1,1024]{1,0:T(1,128)S(1)}) custom-call(f32[512,1024]{1,0:T(8,128)S(1)} %get-tuple-element.165.own_ref, bf16[512,1024]{1,0:T(8,128)(2,1)S(1)} %collective-permute-done.19.sib_ref, f32[512,1024]{1,0:T(8,128)S(1)} %copy-done.27, f32[512,128]{1,0:T(8,128)S(1)} %get-tuple-element.173.inv_ref, ...), custom_call_target="tpu_custom_call" | custom-call | flops 4024999936 | tf_op jit(solution)/shard_map/norm_back/pallas_call | solution.py:426
  154.9 2.0 collective-permute-start.20
  158.2 9.4 %tap_sums.1 = f32[7,7,1024]{2,1,0:T(8,128)S(1)} custom-call(bf16[3,128,1024]{2,1,0:T(8,128)(2,1)S(1)} %copy-done.11, bf16[4,128,1024]{2,1,0:T(8,128)(2,1)S(1)} %copy-done, bf16[3,128,1024]{2,1,0:T(8,128)(2,1)S(1)} %copy-done.9, bf16[4,128,1024]{2,1,0:T(8,128)(2,1)S(1)} %bitcast.40), custom_call_target="tpu_custom_call" | custom-call | flops 11500000256 | tf_op jit(solution)/shard_map/tap_sums/pallas_call | solution.py:239
  171.4 9.0 %collective-permute-start.24 = (bf16[50,1024]{1,0:T(8,128)(2,1)S(1)}, bf16[50,1024]{1,0:T(8,128)(2,1)S(1)}, u32[]{:S(2)}, u32[]{:S(2)}) collective-permute-start(bf16[50,1024]{1,0:T(8,128)(2,1)S(1)} %pad_maximum_fusion.2), channel_id=1, source_target_pairs={{0,4},{1,5},{2,6},{3,7},{4,0},{5,1},{6,2},{7,3},{8,12},{9,13},{10,... | collective-permute-start | bytes 307208 | tf_op jit(solution)/shard_map/ppermute | solution.py:470
  180.5 1.9 add_convert_fusion.4
  182.4 8.5 %collective-permute-start.23 = (bf16[2,128,2048]{2,1,0:T(8,128)(2,1)S(1)}, bf16[2,128,2048]{2,1,0:T(8,128)(2,1)S(1)}, u32[]{:S(2)}, u32[]{:S(2)}) collective-permute-start(bf16[2,128,2048]{2,1,0:T(8,128)(2,1)S(1)} %add_convert_fusion.4), channel_id=1, source_target_pairs={{0,2},{1,3},{4,0},{5,1},{8,4},{9,5},{12,8},{13,9},{14,12},{15,13},... | collective-permute-start | bytes 3145736 | tf_op jit(solution)/shard_map/ppermute | solution.py:470
  192.1 5.2 %backward_conv.2.refs_0_ = bf16[4,128,1024]{2,1,0:T(8,128)(2,1)} custom-call(bf16[3,128,1024]{2,1,0:T(8,128)(2,1)S(1)} %copy-done.21, bf16[4,128,1024]{2,1,0:T(8,128)(2,1)S(1)} %bitcast.41, bf16[3,128,1024]{2,1,0:T(8,128)(2,1)S(1)} %copy-done.23, bf16[7,7,1024]{2,1,0:T(8,128)(2,1)S(1)} %copy-done.24, bf16[4,128,1024]{2,1,0:T(8,128)(2,1)S(1)} %copy-done.17), custom_call_target="tpu_custom_call" | custom-call | flops 6899999744 | tf_op jit(solution)/shard_map/backward_conv/pallas_call | solution.py:197
  197.4 5.2 %backward_conv.3 = bf16[4,128,1024]{2,1,0:T(8,128)(2,1)} custom-call(bf16[3,128,1024]{2,1,0:T(8,128)(2,1)S(1)} %copy-done.21, bf16[4,128,1024]{2,1,0:T(8,128)(2,1)S(1)} %bitcast.42, bf16[3,128,1024]{2,1,0:T(8,128)(2,1)S(1)} %copy-done.23, bf16[7,7,1024]{2,1,0:T(8,128)(2,1)S(1)} %copy-done.24, ...), custom_call_target="tpu_custom_call", output_to_operand_aliasing={{}: (5, {})} | custom-call | flops 6899999744 | tf_op jit(solution)/shard_map/backward_conv/pallas_call | solution.py:197
  202.6 12.9 %collective-permute-done.26 = bf16[50,1024]{1,0:T(8,128)(2,1)S(1)} collective-permute-done((bf16[50,1024]{1,0:T(8,128)(2,1)S(1)}, bf16[50,1024]{1,0:T(8,128)(2,1)S(1)}, u32[]{:S(2)}, u32[]{:S(2)}) %collective-permute-start.26) | collective-permute-done | bytes 102432 | tf_op jit(solution)/shard_map/ppermute | solution.py:470
  219.0 2.0 collective-permute-start.28
  225.2 22.1 %collective-permute-done.27 = bf16[50,1024]{1,0:T(8,128)(2,1)S(1)} collective-permute-done((bf16[50,1024]{1,0:T(8,128)(2,1)S(1)}, bf16[50,1024]{1,0:T(8,128)(2,1)S(1)}, u32[]{:S(2)}, u32[]{:S(2)}) %collective-permute-start.27) | collective-permute-done | bytes 102432 | tf_op jit(solution)/shard_map/ppermute | solution.py:470
  247.4 2.1 add_convert_fusion
  (146 shorter events, 43.5 us)
Async XLA Ops:
  2.0 2.1 collective-permute-start
  4.3 26.6 %collective-permute-start.2 = (bf16[2,128,2048]{2,1,0:T(8,128)(2,1)S(1)}, bf16[2,128,2048]{2,1,0:T(8,128)(2,1)}, u32[]{:S(2)}, u32[]{:S(2)}) collective-permute-start(bf16[2,128,2048]{2,1,0:T(8,128)(2,1)S(1)} %maximum_select_fusion.refs_0_), channel_id=1, source_target_pairs={{0,2},{1,3},{4,0},{5,1},{8,4},{9,5},{12,8},{13,9},{14,12},{15,13},... | collective-permute-start | bytes 3145736 | tf_op jit(solution)/shard_map/ppermute | solution.py:470
  7.3 25.0 %collective-permute-start.1 = (bf16[2,128,2048]{2,1,0:T(8,128)(2,1)S(1)}, bf16[2,128,2048]{2,1,0:T(8,128)(2,1)}, u32[]{:S(2)}, u32[]{:S(2)}) collective-permute-start(bf16[2,128,2048]{2,1,0:T(8,128)(2,1)S(1)} %maximum_select_fusion.refs_0_), channel_id=1, source_target_pairs={{0,4},{1,5},{4,8},{5,9},{8,12},{9,13},{12,14},{13,15},{14,10},{15,... | collective-permute-start | bytes 3145736 | tf_op jit(solution)/shard_map/ppermute | solution.py:470
  8.4 25.9 %collective-permute-start.7 = (bf16[3,128,1024]{2,1,0:T(8,128)(2,1)S(1)}, bf16[3,128,1024]{2,1,0:T(8,128)(2,1)}, u32[]{:S(2)}, u32[]{:S(2)}) collective-permute-start(bf16[3,128,1024]{2,1,0:T(8,128)(2,1)S(1)} %get-tuple-element.218), channel_id=1, source_target_pairs={{11,9},{4,6},{27,25},{20,22}} | collective-permute-start | bytes 2359304 | tf_op jit(solution)/shard_map/ppermute | solution.py:470
  10.1 26.4 %collective-permute-start.6 = (bf16[3,128,1024]{2,1,0:T(8,128)(2,1)S(1)}, bf16[3,128,1024]{2,1,0:T(8,128)(2,1)}, u32[]{:S(2)}, u32[]{:S(2)}) collective-permute-start(bf16[3,128,1024]{2,1,0:T(8,128)(2,1)S(1)} %get-tuple-element.219), channel_id=1, source_target_pairs={{1,0},{2,1},{3,2},{5,4},{6,5},{7,6},{8,7},{9,8},{10,9},{11,10},{12... | collective-permute-start | bytes 2359304 | tf_op jit(solution)/shard_map/ppermute | solution.py:470
  11.4 26.7 %collective-permute-start.9 = (bf16[512,1024]{1,0:T(8,128)(2,1)S(1)}, bf16[512,1024]{1,0:T(8,128)(2,1)}, u32[]{:S(2)}, u32[]{:S(2)}) collective-permute-start(bf16[512,1024]{1,0:T(8,128)(2,1)S(1)} %bitcast.43), channel_id=1, source_target_pairs={{0,1},{1,0},{2,3},{3,2},{4,5},{5,4},{6,7},{7,6},{8,9},{9,8},{10,11... | collective-permute-start | bytes 3145736 | tf_op jit(solution)/shard_map/ppermute | solution.py:470
  32.3 30.9 %collective-permute-start.3 = (bf16[2,128,2048]{2,1,0:T(8,128)(2,1)}, bf16[2,128,2048]{2,1,0:T(8,128)(2,1)}, u32[]{:S(2)}, u32[]{:S(2)}) collective-permute-start(bf16[2,128,2048]{2,1,0:T(8,128)(2,1)} %collective-permute-done.1.refs_1_), channel_id=1, source_target_pairs={{0,4},{1,5},{4,8},{5,9},{8,12},{9,13},{12,14},{13,15},{14,10},{15,... | collective-permute-start | bytes 3145736 | tf_op jit(solution)/shard_map/ppermute | solution.py:470
  32.7 30.5 %collective-permute-start.4 = (bf16[2,128,2048]{2,1,0:T(8,128)(2,1)}, bf16[2,128,2048]{2,1,0:T(8,128)(2,1)}, u32[]{:S(2)}, u32[]{:S(2)}) collective-permute-start(bf16[2,128,2048]{2,1,0:T(8,128)(2,1)} %collective-permute-done.2.refs_2_), channel_id=1, source_target_pairs={{0,2},{1,3},{4,0},{5,1},{8,4},{9,5},{12,8},{13,9},{14,12},{15,13},... | collective-permute-start | bytes 3145736 | tf_op jit(solution)/shard_map/ppermute | solution.py:470
  34.3 3.8 %collective-permute-start.5 = (bf16[3,128,1024]{2,1,0:T(8,128)(2,1)}, bf16[3,128,1024]{2,1,0:T(8,128)(2,1)}, u32[]{:S(2)}, u32[]{:S(2)}) collective-permute-start(bf16[3,128,1024]{2,1,0:T(8,128)(2,1)} %get-tuple-element.220), channel_id=1, source_target_pairs={{0,1},{1,2},{2,3},{3,4},{4,5},{5,6},{6,7},{7,8},{8,9},{9,10},{10,1... | collective-permute-start | bytes 2359304 | tf_op jit(solution)/shard_map/ppermute | solution.py:470
  36.5 1.6 collective-permute-start.8
  63.2 27.1 %collective-permute-start.10 = (bf16[2,128,2048]{2,1,0:T(8,128)(2,1)}, bf16[2,128,2048]{2,1,0:T(8,128)(2,1)S(1)}, u32[]{:S(2)}, u32[]{:S(2)}) collective-permute-start(bf16[2,128,2048]{2,1,0:T(8,128)(2,1)} %collective-permute-done.3.refs_3_), channel_id=1, source_target_pairs={{0,4},{1,5},{4,8},{5,9},{8,12},{9,13},{12,14},{13,15},{14,10},{15,... | collective-permute-start | bytes 3145736 | tf_op jit(solution)/shard_map/ppermute | solution.py:470
  67.9 22.4 %collective-permute-start.11 = (bf16[2,128,2048]{2,1,0:T(8,128)(2,1)}, bf16[2,128,2048]{2,1,0:T(8,128)(2,1)S(1)}, u32[]{:S(2)}, u32[]{:S(2)}) collective-permute-start(bf16[2,128,2048]{2,1,0:T(8,128)(2,1)} %collective-permute-done.4.refs_4_), channel_id=1, source_target_pairs={{0,2},{1,3},{4,0},{5,1},{8,4},{9,5},{12,8},{13,9},{14,12},{15,13},... | collective-permute-start | bytes 3145736 | tf_op jit(solution)/shard_map/ppermute | solution.py:470
  90.3 5.4 %collective-permute-start.14 = (bf16[512,1024]{1,0:T(8,128)(2,1)}, bf16[512,1024]{1,0:T(8,128)(2,1)}, u32[]{:S(2)}, u32[]{:S(2)}) collective-permute-start(bf16[512,1024]{1,0:T(8,128)(2,1)} %get-tuple-element.118.refs_0_.n_own), channel_id=1, source_target_pairs={{0,1},{1,0},{2,3},{3,2},{4,5},{5,4},{6,7},{7,6},{8,9},{9,8},{10,11... | collective-permute-start | bytes 3145736 | tf_op jit(solution)/shard_map/ppermute | solution.py:470
  92.3 14.3 %collective-permute-start.13 = (bf16[128,2048]{1,0:T(8,128)(2,1)}, bf16[128,2048]{1,0:T(8,128)(2,1)}, u32[]{:S(2)}, u32[]{:S(2)}) collective-permute-start(bf16[128,2048]{1,0:T(8,128)(2,1)} %slice_bitcast_fusion.4), channel_id=1, source_target_pairs={{0,2},{1,3},{4,0},{5,1},{8,4},{9,5},{12,8},{13,9},{14,12},{15,13},... | collective-permute-start | bytes 1572872 | tf_op jit(solution)/shard_map/ppermute | solution.py:470
  94.1 14.1 %collective-permute-start.12 = (bf16[128,2048]{1,0:T(8,128)(2,1)}, bf16[128,2048]{1,0:T(8,128)(2,1)}, u32[]{:S(2)}, u32[]{:S(2)}) collective-permute-start(bf16[128,2048]{1,0:T(8,128)(2,1)} %slice_bitcast_fusion.5), channel_id=1, source_target_pairs={{0,4},{1,5},{4,8},{5,9},{8,12},{9,13},{12,14},{13,15},{14,10},{15,... | collective-permute-start | bytes 1572872 | tf_op jit(solution)/shard_map/ppermute | solution.py:470
  128.6 12.9 %collective-permute-start.16 = (bf16[128,2048]{1,0:T(8,128)(2,1)S(1)}, bf16[128,2048]{1,0:T(8,128)(2,1)S(1)}, u32[]{:S(2)}, u32[]{:S(2)}) collective-permute-start(bf16[128,2048]{1,0:T(8,128)(2,1)S(1)} %get-tuple-element.216), channel_id=1, source_target_pairs={{0,2},{1,3},{4,0},{5,1},{8,4},{9,5},{12,8},{13,9},{14,12},{15,13},... | collective-permute-start | bytes 1572872 | tf_op jit(solution)/shard_map/ppermute | solution.py:470
  130.3 12.6 %collective-permute-start.15 = (bf16[128,2048]{1,0:T(8,128)(2,1)S(1)}, bf16[128,2048]{1,0:T(8,128)(2,1)S(1)}, u32[]{:S(2)}, u32[]{:S(2)}) collective-permute-start(bf16[128,2048]{1,0:T(8,128)(2,1)S(1)} %get-tuple-element.217), channel_id=1, source_target_pairs={{0,4},{1,5},{4,8},{5,9},{8,12},{9,13},{12,14},{13,15},{14,10},{15,... | collective-permute-start | bytes 1572872 | tf_op jit(solution)/shard_map/ppermute | solution.py:470
  143.2 7.9 %collective-permute-start.19 = (bf16[512,1024]{1,0:T(8,128)(2,1)S(1)}, bf16[512,1024]{1,0:T(8,128)(2,1)S(1)}, u32[]{:S(2)}, u32[]{:S(2)}) collective-permute-start(bf16[512,1024]{1,0:T(8,128)(2,1)S(1)} %get-tuple-element.166), channel_id=1, source_target_pairs={{0,1},{1,0},{2,3},{3,2},{4,5},{5,4},{6,7},{7,6},{8,9},{9,8},{10,11... | collective-permute-start | bytes 3145736 | tf_op jit(solution)/shard_map/ppermute | solution.py:470
  143.6 25.6 %collective-permute-start.18 = (bf16[2,128,2048]{2,1,0:T(8,128)(2,1)S(1)}, bf16[2,128,2048]{2,1,0:T(8,128)(2,1)S(1)}, u32[]{:S(2)}, u32[]{:S(2)}) collective-permute-start(bf16[2,128,2048]{2,1,0:T(8,128)(2,1)S(1)} %pad_maximum_fusion.1), channel_id=1, source_target_pairs={{0,2},{1,3},{4,0},{5,1},{8,4},{9,5},{12,8},{13,9},{14,12},{15,13},... | collective-permute-start | bytes 3145736 | tf_op jit(solution)/shard_map/ppermute | solution.py:470
  144.5 25.3 %collective-permute-start.17 = (bf16[2,128,2048]{2,1,0:T(8,128)(2,1)S(1)}, bf16[2,128,2048]{2,1,0:T(8,128)(2,1)S(1)}, u32[]{:S(2)}, u32[]{:S(2)}) collective-permute-start(bf16[2,128,2048]{2,1,0:T(8,128)(2,1)S(1)} %pad_maximum_fusion), channel_id=1, source_target_pairs={{0,4},{1,5},{4,8},{5,9},{8,12},{9,13},{12,14},{13,15},{14,10},{15,... | collective-permute-start | bytes 3145736 | tf_op jit(solution)/shard_map/ppermute | solution.py:470
  154.9 14.9 %collective-permute-start.20 = (bf16[3,128,1024]{2,1,0:T(8,128)(2,1)S(1)}, bf16[3,128,1024]{2,1,0:T(8,128)(2,1)S(1)}, u32[]{:S(2)}, u32[]{:S(2)}) collective-permute-start(bf16[3,128,1024]{2,1,0:T(8,128)(2,1)S(1)} %bitcast.51), channel_id=1, source_target_pairs={{0,1},{1,2},{2,3},{3,4},{4,5},{5,6},{6,7},{7,8},{8,9},{9,10},{10,1... | collective-permute-start | bytes 2359304 | tf_op jit(solution)/shard_map/ppermute | solution.py:470
  156.9 12.9 %collective-permute-start.21 = (bf16[3,128,1024]{2,1,0:T(8,128)(2,1)S(1)}, bf16[3,128,1024]{2,1,0:T(8,128)(2,1)S(1)}, u32[]{:S(2)}, u32[]{:S(2)}) collective-permute-start(bf16[3,128,1024]{2,1,0:T(8,128)(2,1)S(1)} %bitcast.50), channel_id=1, source_target_pairs={{1,0},{2,1},{3,2},{4,3},{5,4},{6,5},{7,6},{8,7},{9,8},{10,9},{11,1... | collective-permute-start | bytes 2359304 | tf_op jit(solution)/shard_map/ppermute | solution.py:470
  171.4 19.4 %collective-permute-start.24 = (bf16[50,1024]{1,0:T(8,128)(2,1)S(1)}, bf16[50,1024]{1,0:T(8,128)(2,1)S(1)}, u32[]{:S(2)}, u32[]{:S(2)}) collective-permute-start(bf16[50,1024]{1,0:T(8,128)(2,1)S(1)} %pad_maximum_fusion.2), channel_id=1, source_target_pairs={{0,4},{1,5},{2,6},{3,7},{4,0},{5,1},{6,2},{7,3},{8,12},{9,13},{10,... | collective-permute-start | bytes 307208 | tf_op jit(solution)/shard_map/ppermute | solution.py:470
  182.4 33.1 %collective-permute-start.23 = (bf16[2,128,2048]{2,1,0:T(8,128)(2,1)S(1)}, bf16[2,128,2048]{2,1,0:T(8,128)(2,1)S(1)}, u32[]{:S(2)}, u32[]{:S(2)}) collective-permute-start(bf16[2,128,2048]{2,1,0:T(8,128)(2,1)S(1)} %add_convert_fusion.4), channel_id=1, source_target_pairs={{0,2},{1,3},{4,0},{5,1},{8,4},{9,5},{12,8},{13,9},{14,12},{15,13},... | collective-permute-start | bytes 3145736 | tf_op jit(solution)/shard_map/ppermute | solution.py:470
  190.9 24.6 %collective-permute-start.22 = (bf16[2,128,2048]{2,1,0:T(8,128)(2,1)}, bf16[2,128,2048]{2,1,0:T(8,128)(2,1)S(1)}, u32[]{:S(2)}, u32[]{:S(2)}) collective-permute-start(bf16[2,128,2048]{2,1,0:T(8,128)(2,1)} %add_convert_fusion.5), channel_id=1, source_target_pairs={{0,4},{1,5},{4,8},{5,9},{8,12},{9,13},{12,14},{13,15},{14,10},{15,... | collective-permute-start | bytes 3145736 | tf_op jit(solution)/shard_map/ppermute | solution.py:470
  190.9 25.3 %collective-permute-start.25 = (bf16[512,1024]{1,0:T(8,128)(2,1)S(1)}, bf16[512,1024]{1,0:T(8,128)(2,1)}, u32[]{:S(2)}, u32[]{:S(2)}) collective-permute-start(bf16[512,1024]{1,0:T(8,128)(2,1)S(1)} %copy-done.19), channel_id=1, source_target_pairs={{0,1},{1,0},{2,3},{3,2},{4,5},{5,4},{6,7},{7,6},{8,9},{9,8},{10,11... | collective-permute-start | bytes 3145736 | tf_op jit(solution)/shard_map/ppermute | solution.py:470
  191.0 24.6 %collective-permute-start.26 = (bf16[50,1024]{1,0:T(8,128)(2,1)S(1)}, bf16[50,1024]{1,0:T(8,128)(2,1)S(1)}, u32[]{:S(2)}, u32[]{:S(2)}) collective-permute-start(bf16[50,1024]{1,0:T(8,128)(2,1)S(1)} %add_convert_fusion.8), channel_id=1, source_target_pairs={{0,8},{1,9},{2,10},{3,11},{4,12},{5,13},{6,14},{7,15},{8,0},{9,1},... | collective-permute-start | bytes 307208 | tf_op jit(solution)/shard_map/ppermute | solution.py:470
  219.0 28.4 %collective-permute-start.29 = (bf16[2,128,2048]{2,1,0:T(8,128)(2,1)}, bf16[2,128,2048]{2,1,0:T(8,128)(2,1)}, u32[]{:S(2)}, u32[]{:S(2)}) collective-permute-start(bf16[2,128,2048]{2,1,0:T(8,128)(2,1)} %add_convert_fusion.2), channel_id=1, source_target_pairs={{0,2},{1,3},{4,0},{5,1},{8,4},{9,5},{12,8},{13,9},{14,12},{15,13},... | collective-permute-start | bytes 3145736 | tf_op jit(solution)/shard_map/ppermute | solution.py:470
  219.0 28.4 %collective-permute-start.28 = (bf16[2,128,2048]{2,1,0:T(8,128)(2,1)}, bf16[2,128,2048]{2,1,0:T(8,128)(2,1)}, u32[]{:S(2)}, u32[]{:S(2)}) collective-permute-start(bf16[2,128,2048]{2,1,0:T(8,128)(2,1)} %add_convert_fusion.3), channel_id=1, source_target_pairs={{0,4},{1,5},{4,8},{5,9},{8,12},{9,13},{12,14},{13,15},{14,10},{15,... | collective-permute-start | bytes 3145736 | tf_op jit(solution)/shard_map/ppermute | solution.py:470
  221.1 26.3 %collective-permute-start.27 = (bf16[50,1024]{1,0:T(8,128)(2,1)S(1)}, bf16[50,1024]{1,0:T(8,128)(2,1)S(1)}, u32[]{:S(2)}, u32[]{:S(2)}) collective-permute-start(bf16[50,1024]{1,0:T(8,128)(2,1)S(1)} %add_convert_fusion.7), channel_id=1, source_target_pairs={{0,2},{1,3},{2,0},{3,1},{4,6},{5,7},{6,4},{7,5},{8,10},{9,11},{10,... | collective-permute-start | bytes 307208 | tf_op jit(solution)/shard_map/ppermute | solution.py:470
  249.6 3.5 %collective-permute-start.30 = (bf16[2,64,2048]{2,1,0:T(8,128)(2,1)S(1)}, bf16[2,64,2048]{2,1,0:T(8,128)(2,1)S(1)}, u32[]{:S(2)}, u32[]{:S(2)}) collective-permute-start(bf16[2,64,2048]{2,1,0:T(8,128)(2,1)S(1)} %get-tuple-element.213), channel_id=1, source_target_pairs={{0,1},{1,0},{2,3},{3,2},{4,5},{5,4},{6,7},{7,6},{8,9},{9,8},{10,11... | collective-permute-start | bytes 1572872 | tf_op jit(solution)/shard_map/ppermute | solution.py:470
  249.7 2.0 collective-permute-start.31
  (33 other events, 290.9 us)

commit v4 on v3

--- a/solution.py
+++ b/solution.py
@@ -277,7 +277,7 @@
 
         def rows(t, carry, half=half, n_ref=n_ref, c_ref=c_ref):
             at = pl.ds(pl.multiple_of(t * HIGH, HIGH), HIGH)
-            for cols in tiles(win_ref.shape[1]):
+            for cols in (slice(0, win_ref.shape[1]),):
                 pre = jnp.dot(n_ref[at, :], win_ref[:, cols], preferred_element_type=F32)
                 back = jnp.dot(c_ref[at, :], wout_ref[:, cols], preferred_element_type=F32)
                 area = 0.5 * (1.0 + lax.erf(pre * (1.0 / math.sqrt(2.0))))
@@ -305,7 +305,7 @@
             jax.ShapeDtypeStruct((channels, width), BF16),
         ],
         scratch_shapes=[pltpu.SemaphoreType.DMA((2 * len(shards),))],
-        compiler_params=params(8),
+        compiler_params=params(12),
         cost_estimate=cost(17),
         name="hidden_step",
     )(chips, n_own, n_sib, c_own, c_sib, *shards)

time: 255 us -> 253 us (level)
  no operation moved by 1% of the time
where the time goes in v4:
time: 253 us; the launch traced here: 252 us
  waiting for transfers between devices  101 us (40%)
  Pallas kernels  72 us (28%)
  starting transfers between devices  50.5 us (20%)
  other arithmetic  16.4 us (6%)
  local copies, waits for them, and re-layouts  10.6 us (4%)
    ppermute x32, waiting for transfers between devices, on_device(): send = lambda value, pairs: lax.ppermute(value, 'row', pairs)  101 us
    ppermute x32, starting transfers between devices, on_device(): send = lambda value, pairs: lax.ppermute(value, 'row', pairs)  50.5 us
    pallas_call x1, Pallas kernels, hidden_step(): pl.pallas_call(functools.partial(hidden_body, len(shards) - 1), in_specs=...  14.5 us
    pallas_call x2, Pallas kernels, backward_conv(): pl.pallas_call(backward_body, grid=(blocks,), in_specs=conv_specs(lat, lo...  10.4 us
    pallas_call x1, Pallas kernels, tap_sums(): pl.pallas_call(functools.partial(tap_sums_body, scale), grid=(channels //...  9.44 us
    pallas_call x2, Pallas kernels, weight_grads(): pl.pallas_call(functools.partial(weight_grad_body, scale, size, first), i...  9.15 us
    pallas_call x2, Pallas kernels, spread(): pl.pallas_call(spread_body, in_specs=[IN_VMEM] * 2, out_specs=[IN_VMEM] *...  9.08 us
    pallas_call x1, Pallas kernels, forward_last(): pl.pallas_call(forward_last_body, grid=(blocks,), in_specs=conv_specs(lat...  8.48 us
  transfers between devices with their start and end apart: 32, of which 14 were waited for; matrix products, arithmetic and copies ran while one was open for 5% of the time, Pallas kernels for 21%

profile of v4, /device:TPU:0, one launch (start us, length us, event | category | flops | bytes accessed | tf_op | source)
XLA Modules:
  0.0 252.0 jit_solution(2802824415416631544)
XLA Ops:
  4.3 2.9 %collective-permute-start.2 = (bf16[2,128,2048]{2,1,0:T(8,128)(2,1)S(1)}, bf16[2,128,2048]{2,1,0:T(8,128)(2,1)}, u32[]{:S(2)}, u32[]{:S(2)}) collective-permute-start(bf16[2,128,2048]{2,1,0:T(8,128)(2,1)S(1)} %maximum_select_fusion.refs_0_), channel_id=1, source_target_pairs={{0,2},{1,3},{4,0},{5,1},{8,4},{9,5},{12,8},{13,9},{14,12},{15,13},... | collective-permute-start | bytes 3145736 | tf_op jit(solution)/shard_map/ppermute | solution.py:470
  8.4 1.7 collective-permute-start.7
  12.6 18.3 %collective-permute-done.2.refs_2_ = bf16[2,128,2048]{2,1,0:T(8,128)(2,1)} collective-permute-done((bf16[2,128,2048]{2,1,0:T(8,128)(2,1)S(1)}, bf16[2,128,2048]{2,1,0:T(8,128)(2,1)}, u32[]{:S(2)}, u32[]{:S(2)}) %collective-permute-start.2) | collective-permute-done | bytes 1048608 | tf_op jit(solution)/shard_map/ppermute | solution.py:470
  34.3 2.2 collective-permute-start.5
  36.5 1.6 collective-permute-start.8
  38.2 25.0 %collective-permute-done.3.refs_3_ = bf16[2,128,2048]{2,1,0:T(8,128)(2,1)} collective-permute-done((bf16[2,128,2048]{2,1,0:T(8,128)(2,1)}, bf16[2,128,2048]{2,1,0:T(8,128)(2,1)}, u32[]{:S(2)}, u32[]{:S(2)}) %collective-permute-start.3) | collective-permute-done | bytes 1048608 | tf_op jit(solution)/shard_map/ppermute | solution.py:470
  63.2 4.7 %collective-permute-start.10 = (bf16[2,128,2048]{2,1,0:T(8,128)(2,1)}, bf16[2,128,2048]{2,1,0:T(8,128)(2,1)S(1)}, u32[]{:S(2)}, u32[]{:S(2)}) collective-permute-start(bf16[2,128,2048]{2,1,0:T(8,128)(2,1)} %collective-permute-done.3.refs_3_), channel_id=1, source_target_pairs={{0,4},{1,5},{4,8},{5,9},{8,12},{9,13},{12,14},{13,15},{14,10},{15,... | collective-permute-start | bytes 3145736 | tf_op jit(solution)/shard_map/ppermute | solution.py:470
  67.9 1.7 broadcast_select_fusion
  69.7 4.4 %forward_first.1.first_ref = f32[4,512,128]{2,1,0:T(8,128)S(1)} custom-call(bf16[3,128,1024]{2,1,0:T(8,128)(2,1)S(1)} %get-tuple-element.224.before_ref, bf16[4,128,1024]{2,1,0:T(8,128)(2,1)S(1)} %copy-done, bf16[3,128,1024]{2,1,0:T(8,128)(2,1)S(1)} %get-tuple-element.223.after_ref, bf16[7,7,1024]{2,1,0:T(8,128)(2,1)S(1)} %copy-done.24), custom_call_target="tpu_custom_call" | custom-call | flops 5750000128 | tf_op jit(solution)/shard_map/forward_first/pallas_call | solution.py:145
  74.1 8.5 %forward_last.1 = (bf16[512,1024]{1,0:T(8,128)(2,1)}, f32[512,1024]{1,0:T(8,128)S(1)}, f32[512,128]{1,0:T(8,128)S(1)}) custom-call(bf16[3,128,1024]{2,1,0:T(8,128)(2,1)S(1)} %get-tuple-element.224.before_ref, bf16[4,128,1024]{2,1,0:T(8,128)(2,1)S(1)} %copy-done, bf16[3,128,1024]{2,1,0:T(8,128)(2,1)S(1)} %get-tuple-element.223.after_ref, ...), custom_call_target="tpu_custom_call" | custom-call | flops 10350000128 | tf_op jit(solution)/shard_map/forward_last/pallas_call | solution.py:162
  84.0 6.3 %collective-permute-done.10.refs_5_ = bf16[2,128,2048]{2,1,0:T(8,128)(2,1)S(1)} collective-permute-done((bf16[2,128,2048]{2,1,0:T(8,128)(2,1)}, bf16[2,128,2048]{2,1,0:T(8,128)(2,1)S(1)}, u32[]{:S(2)}, u32[]{:S(2)}) %collective-permute-start.10) | collective-permute-done | bytes 1048608 | tf_op jit(solution)/shard_map/ppermute | solution.py:470
  92.3 1.8 collective-permute-start.13
  97.0 3.0 %arrange.1 = (bf16[512,1024]{1,0:T(8,128)(2,1)S(1)}, bf16[512,1024]{1,0:T(8,128)(2,1)S(1)}, bf16[512,1024]{1,0:T(8,128)(2,1)S(1)}, bf16[512,1024]{1,0:T(8,128)(2,1)S(1)}) custom-call(s32[8]{0:T(128)S(1)} %fusion.6.chips_ref, bf16[512,1024]{1,0:T(8,128)(2,1)} %get-tuple-element.118.refs_0_.n_own, bf16[512,1024]{1,0:T(8,128)(2,1)} %collective-permute-done.14.refs_1_.n_sib, ...), custom_call_target="tpu_custom_call" | custom-call | flops 2300000000 | tf_op jit(solution)/shard_map/arrange/pallas_call | solution.py:334
  100.1 6.6 %collective-permute-done.13.refs_8_ = bf16[128,2048]{1,0:T(8,128)(2,1)} collective-permute-done((bf16[128,2048]{1,0:T(8,128)(2,1)}, bf16[128,2048]{1,0:T(8,128)(2,1)}, u32[]{:S(2)}, u32[]{:S(2)}) %collective-permute-start.13) | collective-permute-done | bytes 524320 | tf_op jit(solution)/shard_map/ppermute | solution.py:470
  108.2 14.5 %hidden_step.1 = (bf16[2,512,2048]{2,1,0:T(8,128)(2,1)S(1)}, bf16[2,512,2048]{2,1,0:T(8,128)(2,1)S(1)}, bf16[1024,2048]{1,0:T(8,128)(2,1)S(1)}, bf16[1024,2048]{1,0:T(8,128)(2,1)S(1)}) custom-call(s32[8]{0:T(128)S(1)} %fusion.7.chips_ref, bf16[512,1024]{1,0:T(8,128)(2,1)} %get-tuple-element.118.refs_0_.n_own, ...), custom_call_target="tpu_custom_call" | custom-call | flops 19549999104 | tf_op jit(solution)/shard_map/hidden_step/pallas_call | solution.py:295
  122.7 3.5 %weight_grads.2 = (bf16[2,128,2048]{2,1,0:T(8,128)(2,1)S(1)}, bf16[2,128,2048]{2,1,0:T(8,128)(2,1)S(1)}, bf16[2,128,2048]{2,1,0:T(8,128)(2,1)S(1)}) custom-call(bf16[512,1024]{1,0:T(8,128)(2,1)S(1)} %get-tuple-element.138.n_own, bf16[512,1024]{1,0:T(8,128)(2,1)S(1)} %get-tuple-element.139.n_sib, bf16[512,1024]{1,0:T(8,128)(2,1)S(1)} %get-tuple-element.140.c_own, ...), custom_call_target="tpu_custom_call" | custom-call | flops 3881250048 | tf_op jit(solution)/shard_map/weight_grads/pallas_call | solution.py:358
  126.3 1.7 collective-permute-start.16
  128.4 5.7 %weight_grads.3 = (bf16[2,128,2048]{2,1,0:T(8,128)(2,1)S(1)}, bf16[2,128,2048]{2,1,0:T(8,128)(2,1)S(1)}, bf16[2,128,2048]{2,1,0:T(8,128)(2,1)S(1)}, bf16[2,128,2...) custom-call(bf16[512,1024]{1,0:T(8,128)(2,1)S(1)} %get-tuple-element.138.n_own, ...), custom_call_target="tpu_custom_call" | custom-call | flops 6468749824 | tf_op jit(solution)/shard_map/weight_grads/pallas_call | solution.py:358
  134.1 4.5 %spread.2 = (f32[512,1024]{1,0:T(8,128)S(1)}, bf16[512,1024]{1,0:T(8,128)(2,1)S(1)}) custom-call(bf16[2,512,2048]{2,1,0:T(8,128)(2,1)S(1)} %get-tuple-element.153.grad_ref.lhs_ref, bf16[1024,2048]{1,0:T(8,128)(2,1)S(1)} %get-tuple-element.154.w_ref), custom_call_target="tpu_custom_call" | custom-call | flops 5405000192 | tf_op jit(solution)/shard_map/spread/pallas_call | solution.py:380
  143.3 4.5 %spread.3 = (f32[512,1024]{1,0:T(8,128)S(1)}, bf16[512,1024]{1,0:T(8,128)(2,1)S(1)}) custom-call(bf16[2,512,2048]{2,1,0:T(8,128)(2,1)S(1)} %get-tuple-element.167.hid_ref.lhs_ref, bf16[1024,2048]{1,0:T(8,128)(2,1)S(1)} %get-tuple-element.168.w_ref), custom_call_target="tpu_custom_call" | custom-call | flops 5405000192 | tf_op jit(solution)/shard_map/spread/pallas_call | solution.py:380
  148.9 3.5 %norm_back.1 = (bf16[512,1024]{1,0:T(8,128)(2,1)S(1)}, f32[1,1024]{1,0:T(1,128)S(1)}) custom-call(f32[512,1024]{1,0:T(8,128)S(1)} %get-tuple-element.165.own_ref, bf16[512,1024]{1,0:T(8,128)(2,1)S(1)} %collective-permute-done.19.sib_ref, f32[512,1024]{1,0:T(8,128)S(1)} %copy-done.27, f32[512,128]{1,0:T(8,128)S(1)} %get-tuple-element.173.inv_ref, ...), custom_call_target="tpu_custom_call" | custom-call | flops 4024999936 | tf_op jit(solution)/shard_map/norm_back/pallas_call | solution.py:426
  152.6 2.0 collective-permute-start.20
  155.9 9.4 %tap_sums.1 = f32[7,7,1024]{2,1,0:T(8,128)S(1)} custom-call(bf16[3,128,1024]{2,1,0:T(8,128)(2,1)S(1)} %copy-done.11, bf16[4,128,1024]{2,1,0:T(8,128)(2,1)S(1)} %copy-done, bf16[3,128,1024]{2,1,0:T(8,128)(2,1)S(1)} %copy-done.9, bf16[4,128,1024]{2,1,0:T(8,128)(2,1)S(1)} %bitcast.40), custom_call_target="tpu_custom_call" | custom-call | flops 11500000256 | tf_op jit(solution)/shard_map/tap_sums/pallas_call | solution.py:239
  169.2 9.0 %collective-permute-start.24 = (bf16[50,1024]{1,0:T(8,128)(2,1)S(1)}, bf16[50,1024]{1,0:T(8,128)(2,1)S(1)}, u32[]{:S(2)}, u32[]{:S(2)}) collective-permute-start(bf16[50,1024]{1,0:T(8,128)(2,1)S(1)} %pad_maximum_fusion.2), channel_id=1, source_target_pairs={{0,4},{1,5},{2,6},{3,7},{4,0},{5,1},{6,2},{7,3},{8,12},{9,13},{10,... | collective-permute-start | bytes 307208 | tf_op jit(solution)/shard_map/ppermute | solution.py:470
  178.2 1.9 add_convert_fusion.4
  180.1 8.5 %collective-permute-start.23 = (bf16[2,128,2048]{2,1,0:T(8,128)(2,1)S(1)}, bf16[2,128,2048]{2,1,0:T(8,128)(2,1)S(1)}, u32[]{:S(2)}, u32[]{:S(2)}) collective-permute-start(bf16[2,128,2048]{2,1,0:T(8,128)(2,1)S(1)} %add_convert_fusion.4), channel_id=1, source_target_pairs={{0,2},{1,3},{4,0},{5,1},{8,4},{9,5},{12,8},{13,9},{14,12},{15,13},... | collective-permute-start | bytes 3145736 | tf_op jit(solution)/shard_map/ppermute | solution.py:470
  189.8 5.2 %backward_conv.2.refs_0_ = bf16[4,128,1024]{2,1,0:T(8,128)(2,1)} custom-call(bf16[3,128,1024]{2,1,0:T(8,128)(2,1)S(1)} %copy-done.21, bf16[4,128,1024]{2,1,0:T(8,128)(2,1)S(1)} %bitcast.41, bf16[3,128,1024]{2,1,0:T(8,128)(2,1)S(1)} %copy-done.23, bf16[7,7,1024]{2,1,0:T(8,128)(2,1)S(1)} %copy-done.24, bf16[4,128,1024]{2,1,0:T(8,128)(2,1)S(1)} %copy-done.17), custom_call_target="tpu_custom_call" | custom-call | flops 6899999744 | tf_op jit(solution)/shard_map/backward_conv/pallas_call | solution.py:197
  195.1 5.2 %backward_conv.3 = bf16[4,128,1024]{2,1,0:T(8,128)(2,1)} custom-call(bf16[3,128,1024]{2,1,0:T(8,128)(2,1)S(1)} %copy-done.21, bf16[4,128,1024]{2,1,0:T(8,128)(2,1)S(1)} %bitcast.42, bf16[3,128,1024]{2,1,0:T(8,128)(2,1)S(1)} %copy-done.23, bf16[7,7,1024]{2,1,0:T(8,128)(2,1)S(1)} %copy-done.24, ...), custom_call_target="tpu_custom_call", output_to_operand_aliasing={{}: (5, {})} | custom-call | flops 6899999744 | tf_op jit(solution)/shard_map/backward_conv/pallas_call | solution.py:197
  200.3 12.9 %collective-permute-done.26 = bf16[50,1024]{1,0:T(8,128)(2,1)S(1)} collective-permute-done((bf16[50,1024]{1,0:T(8,128)(2,1)S(1)}, bf16[50,1024]{1,0:T(8,128)(2,1)S(1)}, u32[]{:S(2)}, u32[]{:S(2)}) %collective-permute-start.26) | collective-permute-done | bytes 102432 | tf_op jit(solution)/shard_map/ppermute | solution.py:470
  216.7 2.0 collective-permute-start.28
  222.9 22.1 %collective-permute-done.27 = bf16[50,1024]{1,0:T(8,128)(2,1)S(1)} collective-permute-done((bf16[50,1024]{1,0:T(8,128)(2,1)S(1)}, bf16[50,1024]{1,0:T(8,128)(2,1)S(1)}, u32[]{:S(2)}, u32[]{:S(2)}) %collective-permute-start.27) | collective-permute-done | bytes 102432 | tf_op jit(solution)/shard_map/ppermute | solution.py:470
  245.1 2.1 add_convert_fusion
  (146 shorter events, 43.5 us)
Async XLA Ops:
  2.0 2.1 collective-permute-start
  4.3 26.6 %collective-permute-start.2 = (bf16[2,128,2048]{2,1,0:T(8,128)(2,1)S(1)}, bf16[2,128,2048]{2,1,0:T(8,128)(2,1)}, u32[]{:S(2)}, u32[]{:S(2)}) collective-permute-start(bf16[2,128,2048]{2,1,0:T(8,128)(2,1)S(1)} %maximum_select_fusion.refs_0_), channel_id=1, source_target_pairs={{0,2},{1,3},{4,0},{5,1},{8,4},{9,5},{12,8},{13,9},{14,12},{15,13},... | collective-permute-start | bytes 3145736 | tf_op jit(solution)/shard_map/ppermute | solution.py:470
  7.3 25.0 %collective-permute-start.1 = (bf16[2,128,2048]{2,1,0:T(8,128)(2,1)S(1)}, bf16[2,128,2048]{2,1,0:T(8,128)(2,1)}, u32[]{:S(2)}, u32[]{:S(2)}) collective-permute-start(bf16[2,128,2048]{2,1,0:T(8,128)(2,1)S(1)} %maximum_select_fusion.refs_0_), channel_id=1, source_target_pairs={{0,4},{1,5},{4,8},{5,9},{8,12},{9,13},{12,14},{13,15},{14,10},{15,... | collective-permute-start | bytes 3145736 | tf_op jit(solution)/shard_map/ppermute | solution.py:470
  8.4 25.9 %collective-permute-start.7 = (bf16[3,128,1024]{2,1,0:T(8,128)(2,1)S(1)}, bf16[3,128,1024]{2,1,0:T(8,128)(2,1)}, u32[]{:S(2)}, u32[]{:S(2)}) collective-permute-start(bf16[3,128,1024]{2,1,0:T(8,128)(2,1)S(1)} %get-tuple-element.218), channel_id=1, source_target_pairs={{11,9},{4,6},{27,25},{20,22}} | collective-permute-start | bytes 2359304 | tf_op jit(solution)/shard_map/ppermute | solution.py:470
  10.1 26.4 %collective-permute-start.6 = (bf16[3,128,1024]{2,1,0:T(8,128)(2,1)S(1)}, bf16[3,128,1024]{2,1,0:T(8,128)(2,1)}, u32[]{:S(2)}, u32[]{:S(2)}) collective-permute-start(bf16[3,128,1024]{2,1,0:T(8,128)(2,1)S(1)} %get-tuple-element.219), channel_id=1, source_target_pairs={{1,0},{2,1},{3,2},{5,4},{6,5},{7,6},{8,7},{9,8},{10,9},{11,10},{12... | collective-permute-start | bytes 2359304 | tf_op jit(solution)/shard_map/ppermute | solution.py:470
  11.4 26.7 %collective-permute-start.9 = (bf16[512,1024]{1,0:T(8,128)(2,1)S(1)}, bf16[512,1024]{1,0:T(8,128)(2,1)}, u32[]{:S(2)}, u32[]{:S(2)}) collective-permute-start(bf16[512,1024]{1,0:T(8,128)(2,1)S(1)} %bitcast.43), channel_id=1, source_target_pairs={{0,1},{1,0},{2,3},{3,2},{4,5},{5,4},{6,7},{7,6},{8,9},{9,8},{10,11... | collective-permute-start | bytes 3145736 | tf_op jit(solution)/shard_map/ppermute | solution.py:470
  32.3 30.9 %collective-permute-start.3 = (bf16[2,128,2048]{2,1,0:T(8,128)(2,1)}, bf16[2,128,2048]{2,1,0:T(8,128)(2,1)}, u32[]{:S(2)}, u32[]{:S(2)}) collective-permute-start(bf16[2,128,2048]{2,1,0:T(8,128)(2,1)} %collective-permute-done.1.refs_1_), channel_id=1, source_target_pairs={{0,4},{1,5},{4,8},{5,9},{8,12},{9,13},{12,14},{13,15},{14,10},{15,... | collective-permute-start | bytes 3145736 | tf_op jit(solution)/shard_map/ppermute | solution.py:470
  32.7 30.5 %collective-permute-start.4 = (bf16[2,128,2048]{2,1,0:T(8,128)(2,1)}, bf16[2,128,2048]{2,1,0:T(8,128)(2,1)}, u32[]{:S(2)}, u32[]{:S(2)}) collective-permute-start(bf16[2,128,2048]{2,1,0:T(8,128)(2,1)} %collective-permute-done.2.refs_2_), channel_id=1, source_target_pairs={{0,2},{1,3},{4,0},{5,1},{8,4},{9,5},{12,8},{13,9},{14,12},{15,13},... | collective-permute-start | bytes 3145736 | tf_op jit(solution)/shard_map/ppermute | solution.py:470
  34.3 3.8 %collective-permute-start.5 = (bf16[3,128,1024]{2,1,0:T(8,128)(2,1)}, bf16[3,128,1024]{2,1,0:T(8,128)(2,1)}, u32[]{:S(2)}, u32[]{:S(2)}) collective-permute-start(bf16[3,128,1024]{2,1,0:T(8,128)(2,1)} %get-tuple-element.220), channel_id=1, source_target_pairs={{0,1},{1,2},{2,3},{3,4},{4,5},{5,6},{6,7},{7,8},{8,9},{9,10},{10,1... | collective-permute-start | bytes 2359304 | tf_op jit(solution)/shard_map/ppermute | solution.py:470
  36.5 1.6 collective-permute-start.8
  63.2 27.1 %collective-permute-start.10 = (bf16[2,128,2048]{2,1,0:T(8,128)(2,1)}, bf16[2,128,2048]{2,1,0:T(8,128)(2,1)S(1)}, u32[]{:S(2)}, u32[]{:S(2)}) collective-permute-start(bf16[2,128,2048]{2,1,0:T(8,128)(2,1)} %collective-permute-done.3.refs_3_), channel_id=1, source_target_pairs={{0,4},{1,5},{4,8},{5,9},{8,12},{9,13},{12,14},{13,15},{14,10},{15,... | collective-permute-start | bytes 3145736 | tf_op jit(solution)/shard_map/ppermute | solution.py:470
  67.9 22.4 %collective-permute-start.11 = (bf16[2,128,2048]{2,1,0:T(8,128)(2,1)}, bf16[2,128,2048]{2,1,0:T(8,128)(2,1)S(1)}, u32[]{:S(2)}, u32[]{:S(2)}) collective-permute-start(bf16[2,128,2048]{2,1,0:T(8,128)(2,1)} %collective-permute-done.4.refs_4_), channel_id=1, source_target_pairs={{0,2},{1,3},{4,0},{5,1},{8,4},{9,5},{12,8},{13,9},{14,12},{15,13},... | collective-permute-start | bytes 3145736 | tf_op jit(solution)/shard_map/ppermute | solution.py:470
  90.3 5.4 %collective-permute-start.14 = (bf16[512,1024]{1,0:T(8,128)(2,1)}, bf16[512,1024]{1,0:T(8,128)(2,1)}, u32[]{:S(2)}, u32[]{:S(2)}) collective-permute-start(bf16[512,1024]{1,0:T(8,128)(2,1)} %get-tuple-element.118.refs_0_.n_own), channel_id=1, source_target_pairs={{0,1},{1,0},{2,3},{3,2},{4,5},{5,4},{6,7},{7,6},{8,9},{9,8},{10,11... | collective-permute-start | bytes 3145736 | tf_op jit(solution)/shard_map/ppermute | solution.py:470
  92.3 14.3 %collective-permute-start.13 = (bf16[128,2048]{1,0:T(8,128)(2,1)}, bf16[128,2048]{1,0:T(8,128)(2,1)}, u32[]{:S(2)}, u32[]{:S(2)}) collective-permute-start(bf16[128,2048]{1,0:T(8,128)(2,1)} %slice_bitcast_fusion.4), channel_id=1, source_target_pairs={{0,2},{1,3},{4,0},{5,1},{8,4},{9,5},{12,8},{13,9},{14,12},{15,13},... | collective-permute-start | bytes 1572872 | tf_op jit(solution)/shard_map/ppermute | solution.py:470
  94.1 14.1 %collective-permute-start.12 = (bf16[128,2048]{1,0:T(8,128)(2,1)}, bf16[128,2048]{1,0:T(8,128)(2,1)}, u32[]{:S(2)}, u32[]{:S(2)}) collective-permute-start(bf16[128,2048]{1,0:T(8,128)(2,1)} %slice_bitcast_fusion.5), channel_id=1, source_target_pairs={{0,4},{1,5},{4,8},{5,9},{8,12},{9,13},{12,14},{13,15},{14,10},{15,... | collective-permute-start | bytes 1572872 | tf_op jit(solution)/shard_map/ppermute | solution.py:470
  126.3 12.9 %collective-permute-start.16 = (bf16[128,2048]{1,0:T(8,128)(2,1)S(1)}, bf16[128,2048]{1,0:T(8,128)(2,1)S(1)}, u32[]{:S(2)}, u32[]{:S(2)}) collective-permute-start(bf16[128,2048]{1,0:T(8,128)(2,1)S(1)} %get-tuple-element.216), channel_id=1, source_target_pairs={{0,2},{1,3},{4,0},{5,1},{8,4},{9,5},{12,8},{13,9},{14,12},{15,13},... | collective-permute-start | bytes 1572872 | tf_op jit(solution)/shard_map/ppermute | solution.py:470
  128.0 12.6 %collective-permute-start.15 = (bf16[128,2048]{1,0:T(8,128)(2,1)S(1)}, bf16[128,2048]{1,0:T(8,128)(2,1)S(1)}, u32[]{:S(2)}, u32[]{:S(2)}) collective-permute-start(bf16[128,2048]{1,0:T(8,128)(2,1)S(1)} %get-tuple-element.217), channel_id=1, source_target_pairs={{0,4},{1,5},{4,8},{5,9},{8,12},{9,13},{12,14},{13,15},{14,10},{15,... | collective-permute-start | bytes 1572872 | tf_op jit(solution)/shard_map/ppermute | solution.py:470
  140.9 7.9 %collective-permute-start.19 = (bf16[512,1024]{1,0:T(8,128)(2,1)S(1)}, bf16[512,1024]{1,0:T(8,128)(2,1)S(1)}, u32[]{:S(2)}, u32[]{:S(2)}) collective-permute-start(bf16[512,1024]{1,0:T(8,128)(2,1)S(1)} %get-tuple-element.166), channel_id=1, source_target_pairs={{0,1},{1,0},{2,3},{3,2},{4,5},{5,4},{6,7},{7,6},{8,9},{9,8},{10,11... | collective-permute-start | bytes 3145736 | tf_op jit(solution)/shard_map/ppermute | solution.py:470
  141.3 25.6 %collective-permute-start.18 = (bf16[2,128,2048]{2,1,0:T(8,128)(2,1)S(1)}, bf16[2,128,2048]{2,1,0:T(8,128)(2,1)S(1)}, u32[]{:S(2)}, u32[]{:S(2)}) collective-permute-start(bf16[2,128,2048]{2,1,0:T(8,128)(2,1)S(1)} %pad_maximum_fusion.1), channel_id=1, source_target_pairs={{0,2},{1,3},{4,0},{5,1},{8,4},{9,5},{12,8},{13,9},{14,12},{15,13},... | collective-permute-start | bytes 3145736 | tf_op jit(solution)/shard_map/ppermute | solution.py:470
  142.2 25.3 %collective-permute-start.17 = (bf16[2,128,2048]{2,1,0:T(8,128)(2,1)S(1)}, bf16[2,128,2048]{2,1,0:T(8,128)(2,1)S(1)}, u32[]{:S(2)}, u32[]{:S(2)}) collective-permute-start(bf16[2,128,2048]{2,1,0:T(8,128)(2,1)S(1)} %pad_maximum_fusion), channel_id=1, source_target_pairs={{0,4},{1,5},{4,8},{5,9},{8,12},{9,13},{12,14},{13,15},{14,10},{15,... | collective-permute-start | bytes 3145736 | tf_op jit(solution)/shard_map/ppermute | solution.py:470
  152.6 14.9 %collective-permute-start.20 = (bf16[3,128,1024]{2,1,0:T(8,128)(2,1)S(1)}, bf16[3,128,1024]{2,1,0:T(8,128)(2,1)S(1)}, u32[]{:S(2)}, u32[]{:S(2)}) collective-permute-start(bf16[3,128,1024]{2,1,0:T(8,128)(2,1)S(1)} %bitcast.51), channel_id=1, source_target_pairs={{0,1},{1,2},{2,3},{3,4},{4,5},{5,6},{6,7},{7,8},{8,9},{9,10},{10,1... | collective-permute-start | bytes 2359304 | tf_op jit(solution)/shard_map/ppermute | solution.py:470
  154.6 12.9 %collective-permute-start.21 = (bf16[3,128,1024]{2,1,0:T(8,128)(2,1)S(1)}, bf16[3,128,1024]{2,1,0:T(8,128)(2,1)S(1)}, u32[]{:S(2)}, u32[]{:S(2)}) collective-permute-start(bf16[3,128,1024]{2,1,0:T(8,128)(2,1)S(1)} %bitcast.50), channel_id=1, source_target_pairs={{1,0},{2,1},{3,2},{4,3},{5,4},{6,5},{7,6},{8,7},{9,8},{10,9},{11,1... | collective-permute-start | bytes 2359304 | tf_op jit(solution)/shard_map/ppermute | solution.py:470
  169.2 19.4 %collective-permute-start.24 = (bf16[50,1024]{1,0:T(8,128)(2,1)S(1)}, bf16[50,1024]{1,0:T(8,128)(2,1)S(1)}, u32[]{:S(2)}, u32[]{:S(2)}) collective-permute-start(bf16[50,1024]{1,0:T(8,128)(2,1)S(1)} %pad_maximum_fusion.2), channel_id=1, source_target_pairs={{0,4},{1,5},{2,6},{3,7},{4,0},{5,1},{6,2},{7,3},{8,12},{9,13},{10,... | collective-permute-start | bytes 307208 | tf_op jit(solution)/shard_map/ppermute | solution.py:470
  180.1 33.1 %collective-permute-start.23 = (bf16[2,128,2048]{2,1,0:T(8,128)(2,1)S(1)}, bf16[2,128,2048]{2,1,0:T(8,128)(2,1)S(1)}, u32[]{:S(2)}, u32[]{:S(2)}) collective-permute-start(bf16[2,128,2048]{2,1,0:T(8,128)(2,1)S(1)} %add_convert_fusion.4), channel_id=1, source_target_pairs={{0,2},{1,3},{4,0},{5,1},{8,4},{9,5},{12,8},{13,9},{14,12},{15,13},... | collective-permute-start | bytes 3145736 | tf_op jit(solution)/shard_map/ppermute | solution.py:470
  188.6 24.6 %collective-permute-start.22 = (bf16[2,128,2048]{2,1,0:T(8,128)(2,1)}, bf16[2,128,2048]{2,1,0:T(8,128)(2,1)S(1)}, u32[]{:S(2)}, u32[]{:S(2)}) collective-permute-start(bf16[2,128,2048]{2,1,0:T(8,128)(2,1)} %add_convert_fusion.5), channel_id=1, source_target_pairs={{0,4},{1,5},{4,8},{5,9},{8,12},{9,13},{12,14},{13,15},{14,10},{15,... | collective-permute-start | bytes 3145736 | tf_op jit(solution)/shard_map/ppermute | solution.py:470
  188.6 25.3 %collective-permute-start.25 = (bf16[512,1024]{1,0:T(8,128)(2,1)S(1)}, bf16[512,1024]{1,0:T(8,128)(2,1)}, u32[]{:S(2)}, u32[]{:S(2)}) collective-permute-start(bf16[512,1024]{1,0:T(8,128)(2,1)S(1)} %copy-done.19), channel_id=1, source_target_pairs={{0,1},{1,0},{2,3},{3,2},{4,5},{5,4},{6,7},{7,6},{8,9},{9,8},{10,11... | collective-permute-start | bytes 3145736 | tf_op jit(solution)/shard_map/ppermute | solution.py:470
  188.7 24.6 %collective-permute-start.26 = (bf16[50,1024]{1,0:T(8,128)(2,1)S(1)}, bf16[50,1024]{1,0:T(8,128)(2,1)S(1)}, u32[]{:S(2)}, u32[]{:S(2)}) collective-permute-start(bf16[50,1024]{1,0:T(8,128)(2,1)S(1)} %add_convert_fusion.8), channel_id=1, source_target_pairs={{0,8},{1,9},{2,10},{3,11},{4,12},{5,13},{6,14},{7,15},{8,0},{9,1},... | collective-permute-start | bytes 307208 | tf_op jit(solution)/shard_map/ppermute | solution.py:470
  216.7 28.4 %collective-permute-start.29 = (bf16[2,128,2048]{2,1,0:T(8,128)(2,1)}, bf16[2,128,2048]{2,1,0:T(8,128)(2,1)}, u32[]{:S(2)}, u32[]{:S(2)}) collective-permute-start(bf16[2,128,2048]{2,1,0:T(8,128)(2,1)} %add_convert_fusion.2), channel_id=1, source_target_pairs={{0,2},{1,3},{4,0},{5,1},{8,4},{9,5},{12,8},{13,9},{14,12},{15,13},... | collective-permute-start | bytes 3145736 | tf_op jit(solution)/shard_map/ppermute | solution.py:470
  216.7 28.4 %collective-permute-start.28 = (bf16[2,128,2048]{2,1,0:T(8,128)(2,1)}, bf16[2,128,2048]{2,1,0:T(8,128)(2,1)}, u32[]{:S(2)}, u32[]{:S(2)}) collective-permute-start(bf16[2,128,2048]{2,1,0:T(8,128)(2,1)} %add_convert_fusion.3), channel_id=1, source_target_pairs={{0,4},{1,5},{4,8},{5,9},{8,12},{9,13},{12,14},{13,15},{14,10},{15,... | collective-permute-start | bytes 3145736 | tf_op jit(solution)/shard_map/ppermute | solution.py:470
  218.8 26.3 %collective-permute-start.27 = (bf16[50,1024]{1,0:T(8,128)(2,1)S(1)}, bf16[50,1024]{1,0:T(8,128)(2,1)S(1)}, u32[]{:S(2)}, u32[]{:S(2)}) collective-permute-start(bf16[50,1024]{1,0:T(8,128)(2,1)S(1)} %add_convert_fusion.7), channel_id=1, source_target_pairs={{0,2},{1,3},{2,0},{3,1},{4,6},{5,7},{6,4},{7,5},{8,10},{9,11},{10,... | collective-permute-start | bytes 307208 | tf_op jit(solution)/shard_map/ppermute | solution.py:470
  247.3 3.5 %collective-permute-start.30 = (bf16[2,64,2048]{2,1,0:T(8,128)(2,1)S(1)}, bf16[2,64,2048]{2,1,0:T(8,128)(2,1)S(1)}, u32[]{:S(2)}, u32[]{:S(2)}) collective-permute-start(bf16[2,64,2048]{2,1,0:T(8,128)(2,1)S(1)} %get-tuple-element.213), channel_id=1, source_target_pairs={{0,1},{1,0},{2,3},{3,2},{4,5},{5,4},{6,7},{7,6},{8,9},{9,8},{10,11... | collective-permute-start | bytes 1572872 | tf_op jit(solution)/shard_map/ppermute | solution.py:470
  247.4 2.0 collective-permute-start.31
  (33 other events, 290.9 us)
